TPU v7x, 32 devices: a whole 2x2x4 slice. The times are simulated.
32 devices in a mesh: fsdp: 8 (over z, y), rep: 4 (over x, core).
Axes of the slice: x: 2, y: 2, z: 4, core: 2. Of those that a mesh axis runs over, the one named last changes fastest.
Arguments:
- tokens: bfloat16 [32768, 768], P(('fsdp', 'rep')), may hold values from -6 to 6
- seq_ids: int32 [32, 1024], P(('fsdp', 'rep')), may hold values from 0 to 31, never falling along the last dimension, each value on 1 to 256 neighbouring positions
- key_mask: int32 [32, 1024], P(('fsdp', 'rep')), may hold values 0 or 1
- weight_query: bfloat16 [768, 768], P('fsdp'), may hold values from -0.21875 to 0.21875
- bias_query: bfloat16 [768], P('fsdp'), may hold values from -3 to 3
- weight_key: bfloat16 [768, 768], P('fsdp'), may hold values from -0.21875 to 0.21875
- weight_value: bfloat16 [768, 768], P('fsdp'), may hold values from -0.21875 to 0.21875
- bias_value: bfloat16 [768], P('fsdp'), may hold values from -3 to 3
- weight_out: bfloat16 [768, 768], P('fsdp'), may hold values from -0.625 to 0.625
- bias_out: bfloat16 [768], P('fsdp'), may hold values from -3 to 3
- norm1_gain: bfloat16 [768], P('fsdp'), may hold values from 0.5 to 1.5
- norm1_bias: bfloat16 [768], P('fsdp'), may hold values from -2 to 2
- weight_inner: bfloat16 [768, 3072], P('fsdp'), may hold values from -0.21875 to 0.21875
- bias_inner: bfloat16 [3072], P('fsdp'), may hold values from -3 to 3
- weight_outer: bfloat16 [3072, 768], P('fsdp'), may hold values from -0.109375 to 0.109375
- bias_outer: bfloat16 [768], P('fsdp'), may hold values from -2 to 2
- norm2_gain: bfloat16 [768], P('fsdp'), may hold values from 0.5 to 1.5
- norm2_bias: bfloat16 [768], P('fsdp'), may hold values from -2 to 2
- out_grad: bfloat16 [32768, 768], P(('fsdp', 'rep')), may hold values from -6 to 6
Outputs:
- layer_out: bfloat16 [32768, 768], P(('fsdp', 'rep'))
- grad_tokens: bfloat16 [32768, 768], P(('fsdp', 'rep'))
- grad_weight_query: float32 [768, 768], P('fsdp')
- grad_bias_query: float32 [768], P('fsdp')
- grad_weight_key: float32 [768, 768], P('fsdp')
- grad_weight_value: float32 [768, 768], P('fsdp')
- grad_bias_value: float32 [768], P('fsdp')
- grad_weight_out: float32 [768, 768], P('fsdp')
- grad_bias_out: float32 [768], P('fsdp')
- grad_norm1_gain: float32 [768], P('fsdp')
- grad_norm1_bias: float32 [768], P('fsdp')
- grad_weight_inner: float32 [768, 3072], P('fsdp')
- grad_bias_inner: float32 [3072], P('fsdp')
- grad_weight_outer: float32 [3072, 768], P('fsdp')
- grad_bias_outer: float32 [768], P('fsdp')
- grad_norm2_gain: float32 [768], P('fsdp')
- grad_norm2_bias: float32 [768], P('fsdp')
Inputs may be any that keep to these rules, and one draw needn't show every extreme that they name: `seq_ids`: in each row of 1024 tokens the ids never fall, a sequence has at most min(256, 512) tokens, and one has exactly that many.
All inputs are finite; a program needn't handle non-finite values. No bound on the sum of `key_mask` on one device may be relied on, other than what follows from the above.
Results may differ from a plain program's by a relative error of at most 0.017.
Values may be sent and summed in bfloat16 or wider, within the bound.
No kernel may reach another device: no remote copies, remote signals or barrier semaphores. Data moves between devices by JAX's collectives and lax.ppermute only.
A program may use at most 320 MiB of HBM per device.

v0:
```python
import math

import jax
import jax.numpy as jnp
from jax import lax
from jax.sharding import PartitionSpec as P

D = 768
HEADS = 12
DH = 64
QBLOCK = 512


NEGATIVE = -1e30
EPSILON = 1e-12
INV_ROOT_TWO = 0.7071067811865476
INV_ROOT_TWOPI = 0.3989422804014327


def product(left, right):
    return jnp.dot(left, right, preferred_element_type=jnp.float32)


def product_left(left, right):
    return lax.dot_general(
        left, right, (((0,), (0,)), ((), ())), preferred_element_type=jnp.float32
    )


def product_right(left, right):
    return lax.dot_general(
        left, right, (((1,), (1,)), ((), ())), preferred_element_type=jnp.float32
    )


def norm_forward(hidden):
    center = hidden - jnp.mean(hidden, axis=-1, keepdims=True)
    inverse = lax.rsqrt(jnp.mean(center * center, axis=-1, keepdims=True) + EPSILON)
    return (center * inverse, inverse)


def norm_backward(grad_normed, normed, inverse):
    first_mean = jnp.mean(grad_normed, axis=-1, keepdims=True)
    second_mean = jnp.mean(grad_normed * normed, axis=-1, keepdims=True)
    return inverse * (grad_normed - first_mean - normed * second_mean)


def allowed_mask(seq_row, mask_row, offset, height):
    positions = jnp.arange(seq_row.shape[0], dtype=jnp.int32)
    query_pos = positions[offset : offset + height]
    same_seq = seq_row[offset : offset + height][:, None] == seq_row[None, :]
    visible = (mask_row[None, :] == 1) | (query_pos[:, None] == positions[None, :])
    return same_seq & visible


def block_scores(query_part, key_heads, allowed, scale_factor):
    scores = (
        jnp.einsum("qhd,khd->hqk", query_part, key_heads, preferred_element_type=jnp.float32)
        * scale_factor
    )
    return jnp.where(allowed[None], scores, NEGATIVE)


def local(
    tokens,
    seq_ids,
    key_mask,
    weight_query,
    bias_query,
    weight_key,
    weight_value,
    bias_value,
    weight_out,
    bias_out,
    norm1_gain,
    norm1_bias,
    weight_inner,
    bias_inner,
    weight_outer,
    bias_outer,
    norm2_gain,
    norm2_bias,
    out_grad,
):
    tok_rows = tokens.shape[0]
    scale_factor = 1.0 / math.sqrt(DH)
    seq_row = seq_ids[0]
    mask_row = key_mask[0]
    (
        full_query,
        full_key,
        full_value,
        full_out,
        full_bias_query,
        full_bias_value,
        full_bias_out,
        full_gain_one,
        full_shift_one,
    ) = (
        lax.all_gather(weight_query, "fsdp", axis=0, tiled=True),
        lax.all_gather(weight_key, "fsdp", axis=0, tiled=True),
        lax.all_gather(weight_value, "fsdp", axis=0, tiled=True),
        lax.all_gather(weight_out, "fsdp", axis=0, tiled=True),
        lax.all_gather(bias_query, "fsdp", axis=0, tiled=True),
        lax.all_gather(bias_value, "fsdp", axis=0, tiled=True),
        lax.all_gather(bias_out, "fsdp", axis=0, tiled=True),
        lax.all_gather(norm1_gain, "fsdp", axis=0, tiled=True),
        lax.all_gather(norm1_bias, "fsdp", axis=0, tiled=True),
    )
    queries = (product(tokens, full_query) + full_bias_query).astype(jnp.bfloat16)
    keys_all = product(tokens, full_key).astype(jnp.bfloat16)
    values_all = (product(tokens, full_value) + full_bias_value).astype(jnp.bfloat16)
    query_heads = queries.reshape(tok_rows, HEADS, DH)
    key_heads = keys_all.reshape(tok_rows, HEADS, DH)
    value_heads = values_all.reshape(tok_rows, HEADS, DH)
    context_parts = []
    logsum_parts = []
    for offset in range(0, tok_rows, QBLOCK):
        allowed = allowed_mask(seq_row, mask_row, offset, QBLOCK)
        scores = block_scores(
            query_heads[offset : offset + QBLOCK], key_heads, allowed, scale_factor
        )
        peak = jnp.max(scores, axis=-1, keepdims=True)
        expon = jnp.exp(scores - peak)
        denom = jnp.sum(expon, axis=-1, keepdims=True)
        probs = (expon / denom).astype(jnp.bfloat16)
        logsum_parts.append(peak + jnp.log(denom))
        mixed = jnp.einsum("hqk,khd->qhd", probs, value_heads, preferred_element_type=jnp.float32)
        context_parts.append(mixed.reshape(QBLOCK, D))
    context = jnp.concatenate(context_parts, axis=0).astype(jnp.bfloat16)
    attended = product(context, full_out) + full_bias_out
    first_normed, first_inverse = norm_forward(tokens + attended)
    first = first_normed * full_gain_one + full_shift_one
    first_low = first.astype(jnp.bfloat16)
    full_inner, full_outer, full_bias_inner, full_bias_outer, full_gain_two, full_shift_two = (
        lax.all_gather(weight_inner, "fsdp", axis=0, tiled=True),
        lax.all_gather(weight_outer, "fsdp", axis=0, tiled=True),
        lax.all_gather(bias_inner, "fsdp", axis=0, tiled=True),
        lax.all_gather(bias_outer, "fsdp", axis=0, tiled=True),
        lax.all_gather(norm2_gain, "fsdp", axis=0, tiled=True),
        lax.all_gather(norm2_bias, "fsdp", axis=0, tiled=True),
    )
    inner = product(first_low, full_inner) + full_bias_inner
    activated = jax.nn.gelu(inner, approximate=False).astype(jnp.bfloat16)
    outer = product(activated, full_outer) + full_bias_outer
    second_normed, second_inverse = norm_forward(first + outer)
    layer_out = (second_normed * full_gain_two + full_shift_two).astype(jnp.bfloat16)
    grad_output = out_grad.astype(jnp.float32)
    grad_gain_two = jnp.sum(grad_output * second_normed, axis=0)
    grad_shift_two = jnp.sum(grad_output, axis=0)
    grad_second = norm_backward(grad_output * full_gain_two, second_normed, second_inverse)
    back_inner, back_outer = (full_inner, full_outer)
    grad_outer_low = grad_second.astype(jnp.bfloat16)
    grad_bias_outer = jnp.sum(grad_outer_low.astype(jnp.float32), axis=0)
    grad_weight_outer = product_left(activated, grad_outer_low)
    grad_active = product_right(grad_outer_low, back_outer)
    slope = (
        0.5 * (1.0 + lax.erf(inner * INV_ROOT_TWO))
        + inner * jnp.exp(-0.5 * inner * inner) * INV_ROOT_TWOPI
    )
    grad_inner_low = (grad_active * slope).astype(jnp.bfloat16)
    grad_bias_inner = jnp.sum(grad_inner_low.astype(jnp.float32), axis=0)
    grad_weight_inner = product_left(first_low, grad_inner_low)
    grad_first = grad_second + product_right(grad_inner_low, back_inner)
    (
        owned_inner,
        owned_outer,
        owned_bias_inner,
        owned_bias_outer,
        owned_gain_two,
        owned_shift_two,
    ) = (
        lax.psum_scatter(grad_weight_inner, "fsdp", scatter_dimension=0, tiled=True),
        lax.psum_scatter(grad_weight_outer, "fsdp", scatter_dimension=0, tiled=True),
        lax.psum_scatter(grad_bias_inner, "fsdp", scatter_dimension=0, tiled=True),
        lax.psum_scatter(grad_bias_outer, "fsdp", scatter_dimension=0, tiled=True),
        lax.psum_scatter(grad_gain_two, "fsdp", scatter_dimension=0, tiled=True),
        lax.psum_scatter(grad_shift_two, "fsdp", scatter_dimension=0, tiled=True),
    )
    grad_gain_one = jnp.sum(grad_first * first_normed, axis=0)
    grad_shift_one = jnp.sum(grad_first, axis=0)
    grad_hidden = norm_backward(grad_first * full_gain_one, first_normed, first_inverse)
    back_query, back_key, back_value, back_out = (full_query, full_key, full_value, full_out)
    grad_att_low = grad_hidden.astype(jnp.bfloat16)
    grad_bias_out = jnp.sum(grad_att_low.astype(jnp.float32), axis=0)
    grad_weight_out = product_left(context, grad_att_low)
    grad_context = product_right(grad_att_low, back_out).astype(jnp.bfloat16)
    grad_ctx_heads = grad_context.reshape(tok_rows, HEADS, DH)
    grad_keys = jnp.zeros((tok_rows, HEADS, DH), jnp.float32)
    grad_values = jnp.zeros((tok_rows, HEADS, DH), jnp.float32)
    grad_query_parts = []
    for block_number, offset in enumerate(range(0, tok_rows, QBLOCK)):
        allowed = allowed_mask(seq_row, mask_row, offset, QBLOCK)
        query_part = query_heads[offset : offset + QBLOCK]
        scores = block_scores(query_part, key_heads, allowed, scale_factor)
        soft = jnp.exp(scores - logsum_parts[block_number])
        soft_low = soft.astype(jnp.bfloat16)
        grad_part = grad_ctx_heads[offset : offset + QBLOCK]
        grad_values = grad_values + jnp.einsum(
            "hqk,qhd->khd", soft_low, grad_part, preferred_element_type=jnp.float32
        )
        grad_probs = jnp.einsum(
            "qhd,khd->hqk", grad_part, value_heads, preferred_element_type=jnp.float32
        )
        row_dot = jnp.sum(grad_probs * soft, axis=-1, keepdims=True)
        grad_scores = (soft * (grad_probs - row_dot)).astype(jnp.bfloat16)
        grad_query_parts.append(
            jnp.einsum("hqk,khd->qhd", grad_scores, key_heads, preferred_element_type=jnp.float32)
            * scale_factor
        )
        grad_keys = (
            grad_keys
            + jnp.einsum(
                "hqk,qhd->khd", grad_scores, query_part, preferred_element_type=jnp.float32
            )
            * scale_factor
        )
    grad_queries_low = (
        jnp.concatenate(grad_query_parts, axis=0).reshape(tok_rows, D).astype(jnp.bfloat16)
    )
    grad_keys_low = grad_keys.reshape(tok_rows, D).astype(jnp.bfloat16)
    grad_values_low = grad_values.reshape(tok_rows, D).astype(jnp.bfloat16)
    grad_bias_query = jnp.sum(grad_queries_low.astype(jnp.float32), axis=0)
    grad_bias_value = jnp.sum(grad_values_low.astype(jnp.float32), axis=0)
    grad_weight_query = product_left(tokens, grad_queries_low)
    grad_weight_key = product_left(tokens, grad_keys_low)
    grad_weight_value = product_left(tokens, grad_values_low)
    grad_tokens = (
        grad_hidden
        + product_right(grad_queries_low, back_query)
        + product_right(grad_keys_low, back_key)
        + product_right(grad_values_low, back_value)
    ).astype(jnp.bfloat16)
    (
        owned_query,
        owned_key,
        owned_value,
        owned_out,
        owned_bias_query,
        owned_bias_value,
        owned_bias_out,
        owned_gain_one,
        owned_shift_one,
    ) = (
        lax.psum_scatter(grad_weight_query, "fsdp", scatter_dimension=0, tiled=True),
        lax.psum_scatter(grad_weight_key, "fsdp", scatter_dimension=0, tiled=True),
        lax.psum_scatter(grad_weight_value, "fsdp", scatter_dimension=0, tiled=True),
        lax.psum_scatter(grad_weight_out, "fsdp", scatter_dimension=0, tiled=True),
        lax.psum_scatter(grad_bias_query, "fsdp", scatter_dimension=0, tiled=True),
        lax.psum_scatter(grad_bias_value, "fsdp", scatter_dimension=0, tiled=True),
        lax.psum_scatter(grad_bias_out, "fsdp", scatter_dimension=0, tiled=True),
        lax.psum_scatter(grad_gain_one, "fsdp", scatter_dimension=0, tiled=True),
        lax.psum_scatter(grad_shift_one, "fsdp", scatter_dimension=0, tiled=True),
    )
    (
        final_query,
        final_key,
        final_value,
        final_out,
        final_bias_query,
        final_bias_value,
        final_bias_out,
        final_gain_one,
        final_shift_one,
        final_inner,
        final_outer,
        final_bias_inner,
        final_bias_outer,
        final_gain_two,
        final_shift_two,
    ) = (
        lax.psum(owned_query.astype(jnp.bfloat16), "rep").astype(jnp.float32),
        lax.psum(owned_key.astype(jnp.bfloat16), "rep").astype(jnp.float32),
        lax.psum(owned_value.astype(jnp.bfloat16), "rep").astype(jnp.float32),
        lax.psum(owned_out.astype(jnp.bfloat16), "rep").astype(jnp.float32),
        lax.psum(owned_bias_query.astype(jnp.bfloat16), "rep").astype(jnp.float32),
        lax.psum(owned_bias_value.astype(jnp.bfloat16), "rep").astype(jnp.float32),
        lax.psum(owned_bias_out.astype(jnp.bfloat16), "rep").astype(jnp.float32),
        lax.psum(owned_gain_one.astype(jnp.bfloat16), "rep").astype(jnp.float32),
        lax.psum(owned_shift_one.astype(jnp.bfloat16), "rep").astype(jnp.float32),
        lax.psum(owned_inner.astype(jnp.bfloat16), "rep").astype(jnp.float32),
        lax.psum(owned_outer.astype(jnp.bfloat16), "rep").astype(jnp.float32),
        lax.psum(owned_bias_inner.astype(jnp.bfloat16), "rep").astype(jnp.float32),
        lax.psum(owned_bias_outer.astype(jnp.bfloat16), "rep").astype(jnp.float32),
        lax.psum(owned_gain_two.astype(jnp.bfloat16), "rep").astype(jnp.float32),
        lax.psum(owned_shift_two.astype(jnp.bfloat16), "rep").astype(jnp.float32),
    )
    return (
        layer_out,
        grad_tokens,
        final_query,
        final_bias_query,
        final_key,
        final_value,
        final_bias_value,
        final_out,
        final_bias_out,
        final_gain_one,
        final_shift_one,
        final_inner,
        final_bias_inner,
        final_outer,
        final_bias_outer,
        final_gain_two,
        final_shift_two,
    )


def solution(mesh):
    placed = (
        P(("fsdp", "rep"), None),
        P(("fsdp", "rep"), None),
        P(("fsdp", "rep"), None),
        P("fsdp", None),
        P("fsdp"),
        P("fsdp", None),
        P("fsdp", None),
        P("fsdp"),
        P("fsdp", None),
        P("fsdp"),
        P("fsdp"),
        P("fsdp"),
        P("fsdp", None),
        P("fsdp"),
        P("fsdp", None),
        P("fsdp"),
        P("fsdp"),
        P("fsdp"),
        P(("fsdp", "rep"), None),
    )
    return jax.shard_map(
        local,
        mesh=mesh,
        in_specs=placed,
        out_specs=(
            P(("fsdp", "rep"), None),
            P(("fsdp", "rep"), None),
            P("fsdp", None),
            P("fsdp"),
            P("fsdp", None),
            P("fsdp", None),
            P("fsdp"),
            P("fsdp", None),
            P("fsdp"),
            P("fsdp"),
            P("fsdp"),
            P("fsdp", None),
            P("fsdp"),
            P("fsdp", None),
            P("fsdp"),
            P("fsdp"),
            P("fsdp"),
        ),
        check_vma=False,
    )
```

profile of v0, /device:TPU:0, one launch (start us, length us, event | category | flops | bytes accessed | tf_op | source)
XLA Modules:
  0.0 1087.1 jit_solution(14092976459832094819)
XLA Ops:
  21.3 39.0 %all-reduce.18 = (bf16[768]{0:T(1024)(128)(2,1)S(1)}, bf16[768]{0:T(1024)(128)(2,1)S(1)}, bf16[768]{0:T(1024)(128)(2,1)S(1)}, bf16[768]{0:T(1024)(128)(2,1)S(1)}...) all-reduce(bf16[768]{0:T(1024)(128)(2,1)S(1)} %dynamic-update-slice, ...), channel_id=1, replica_groups=mesh['fsdp'=8,'rep'=4] {'fsdp'}, use_global_device_ids=true, to_apply=%add.2 | all-reduce | flops 6144 | bytes 24576
  62.8 26.4 %all-gather = bf16[8,1,384]{2,1,0:T(2,128)(2,1)S(1)} all-gather(bf16[1,1,384]{2,1,0:T(2,128)(2,1)S(1)} %reshape.297), channel_id=1, replica_groups=mesh['fsdp'=8,'rep'=4] {'fsdp'}, dimensions={0}, use_global_device_ids=true | all-gather | bytes 6912 | tf_op jit(solution)/shard_map/all_gather | solution.py:138
  94.8 2.9 add_convert_fusion.3
  98.7 3.5 convolution_convert_fusion.1
  102.2 10.7 fusion.28
  112.9 11.9 %fusion = f32[12,512]{1,0:T(8,128)S(1)} fusion(f32[12,512]{1,0:T(8,128)S(1)} %get-tuple-element.110, f32[12,512,1024]{2,1,0:T(8,128)} %get-tuple-element.111, pred[512,1024]{1,0:T(8,128)(4,1)S(1)} %get-tuple-element.102), kind=kLoop, calls=%fused_computation.12 | loop fusion | flops 25159680 | bytes 25739264 | tf_op jit(solution)/shard_map/reduce_sum | solution.py:125
  125.4 13.1 %all-gather.8.cloned.1.call-done = bf16[768,768]{1,0:T(8,128)(2,1)} async-done(((bf16[96,768]{1,0:T(8,128)(2,1)}), bf16[768,768]{1,0:T(8,128)(2,1)}) %all-gather.8.cloned.1.call-update) | async-done | bytes 1179664 | tf_op jit(solution)/shard_map/all_gather | solution.py:102
  138.6 3.2 add_convert_fusion.4
  141.8 13.3 %fusion.45 = bf16[12,64,512]{2,1,0:T(8,128)(2,1)} fusion(bf16[1024,12,64]{0,2,1:T(8,128)(2,1)S(1)} %bitcast.96, f32[12,512]{1,0:T(8,128)S(1)} %fusion, f32[12,512]{1,0:T(8,128)S(1)} %get-tuple-element.110, f32[12,512,1024]{2,1,0:T(8,128)} %get-tuple-element.111, pred[512,1024]{1,0:T(8,128)(4,1)S(1)} %get-tuple-element.102), kind=kOutput, calls=%fused_computation.100 | convolution fusion | flops 837156864 | bytes 28098560 | tf_op jit(solution)/shard_map/hqk,khd->qhd/dot_general | solution.py:128
  155.0 11.3 %fusion.29 = (f32[12,512]{1,0:T(8,128)S(1)}, f32[12,512,1024]{2,1,0:T(8,128)}) fusion(pred[512,1024]{1,0:T(8,128)(4,1)S(1)} %get-tuple-element.103, bf16[512,12,64]{0,2,1:T(8,128)(2,1)S(1)} %bitcast.92, bf16[1024,12,64]{0,2,1:T(8,128)(2,1)S(1)} %bitcast.89), kind=kOutput, calls=%fused_computation.50 | convolution fusion | flops 824174592 | bytes 28073984 | tf_op jit(solution)/shard_map/qhd,khd->hqk/dot_general | solution.py:58
  166.3 12.3 %fusion.1 = f32[12,512]{1,0:T(8,128)S(1)} fusion(f32[12,512]{1,0:T(8,128)S(1)} %get-tuple-element.108, f32[12,512,1024]{2,1,0:T(8,128)} %get-tuple-element.109, pred[512,1024]{1,0:T(8,128)(4,1)S(1)} %get-tuple-element.103), kind=kLoop, calls=%fused_computation.13 | loop fusion | flops 25159680 | bytes 25739264 | tf_op jit(solution)/shard_map/reduce_sum | solution.py:125
  181.8 8.5 fusion.44
  190.3 3.2 fusion.69
  195.6 65.6 %all-gather.16.cloned.1.call-done = bf16[768,3072]{1,0:T(8,128)(2,1)} async-done(((bf16[96,3072]{1,0:T(8,128)(2,1)}), bf16[768,3072]{1,0:T(8,128)(2,1)}) %all-gather.16.cloned.1.call-update) | async-done | bytes 4718608 | tf_op jit(solution)/shard_map/all_gather | solution.py:136
  261.2 39.1 %fusion.6 = (bf16[1024,3072]{1,0:T(8,128)(2,1)}, f32[1024,3072]{1,0:T(8,128)}) fusion(f32[3072]{0:T(1024)S(1)} %bitcast.111, bf16[768,3072]{1,0:T(8,128)(2,1)} %all-gather.16.cloned.1.call-done, f32[1024,768]{0,1:T(8,128)} %copy-done.6, f32[768]{0:T(1024)S(1)} %convert_element_type.232, f32[768]{0:T(1024)S(1)} %convert_element_type.231, ...), kind=kOutput, calls=%fused_computation.20 | convolution fusion | flops 5043388416 | bytes 26765312 | tf_op jit(solution)/shard_map/dot_general | solution.py:21
  300.3 41.0 %all-gather.18.cloned.1.call-done = bf16[3072,768]{1,0:T(8,128)(2,1)} async-done(((bf16[384,768]{1,0:T(8,128)(2,1)}), bf16[3072,768]{1,0:T(8,128)(2,1)}) %all-gather.18.cloned.1.call-update) | async-done | bytes 4718608 | tf_op jit(solution)/shard_map/all_gather | solution.py:137
  341.3 9.4 fusion.70
  354.2 3.2 convert_reduce_fusion.2
  357.4 14.7 %convert_reduce_fusion = (f32[3072]{0:T(1024)}, bf16[1024,3072]{1,0:T(8,128)(2,1)}) fusion(f32[1024,3072]{1,0:T(8,128)} %get-tuple-element.115, f32[3072]{0:T(1024)S(1)} %bitcast.112, bf16[1024,768]{0,1:T(8,128)(2,1)S(1)} %get-tuple-element.92, bf16[3072,768]{1,0:T(8,128)(2,1)S(1)} %copy-done.46), kind=kOutput, calls=%fused_computation.29 | convolution fusion | flops 4872729600 | bytes 25190400 | tf_op jit(solution)/shard_map/dot_general | solution.py:31
  372.1 9.7 multiply_reduce_fusion.2
  385.2 2.9 fusion.46
  388.1 3.3 convolution_convert_fusion
  392.2 11.6 %fusion.13 = f32[12,64,1024]{2,1,0:T(8,128)S(1)} fusion(bf16[512,12,64]{0,2,1:T(8,128)(2,1)S(1)} %bitcast.102, f32[12,512]{1,0:T(8,128)S(1)} %copy-done.31, f32[12,512,1024]{2,1,0:T(8,128)} %get-tuple-element.109, pred[512,1024]{1,0:T(8,128)(4,1)S(1)} %get-tuple-element.103), kind=kOutput, calls=%fused_computation.27 | convolution fusion | flops 830472192 | bytes 29646848 | tf_op jit(solution)/shard_map/hqk,qhd->khd/dot_general | solution.py:199
  403.8 12.8 %convert_reduce_fusion.4 = (f32[12,64]{1,0:T(8,128)}, bf16[12,64,1024]{2,1,0:T(8,128)(2,1)S(1)}) fusion(f32[12,64,1024]{2,1,0:T(8,128)S(1)} %fusion.13, bf16[512,12,64]{0,2,1:T(8,128)(2,1)S(1)} %bitcast.104, f32[12,512]{1,0:T(8,128)S(1)} %copy-done.30, f32[12,512,1024]{2,1,0:T(8,128)} %get-tuple-element.111, pred[512,1024]{1,0:T(8,128)(4,1)S(1)} %copy-done.5), kind=kOutput, calls=%fused_computation.65 | convolution fusion | flops 833617152 | bytes 31222784 | tf_op jit(solution)/shard_map/hqk,qhd->khd/dot_general | solution.py:199
  417.8 2.8 convolution_bitcast_fusion
  420.5 3.2 copy.69
  423.7 17.7 %multiply_reduce_fusion.1 = (f32[12,512]{1,0:T(8,128)S(1)}, f32[12,512,1024]{2,1,0:T(8,128)}) fusion(f32[12,512]{1,0:T(8,128)S(1)} %copy-done.30, f32[12,512,1024]{2,1,0:T(8,128)} %get-tuple-element.111, pred[512,1024]{1,0:T(8,128)(4,1)S(1)} %copy-done.5, bf16[512,12,64]{0,2,1:T(8,128)(2,1)} %bitcast.105, bf16[1024,12,64]{0,2,1:T(8,128)(2,1)S(1)} %bitcast.98), kind=kOutput, calls=%fused_computation.4 | convolution fusion | flops 836757504 | bytes 53264384 | tf_op jit(solution)/shard_map/qhd,khd->hqk/dot_general | solution.py:202
  441.4 21.8 %multiply_reduce_fusion = (f32[12,512]{1,0:T(8,128)S(1)}, f32[12,512,1024]{2,1,0:T(8,128)}) fusion(f32[12,512]{1,0:T(8,128)S(1)} %copy-done.31, f32[12,512,1024]{2,1,0:T(8,128)} %get-tuple-element.109, pred[512,1024]{1,0:T(8,128)(4,1)S(1)} %get-tuple-element.103, bf16[512,12,64]{0,2,1:T(8,128)(2,1)S(1)} %bitcast.103, bf16[1024,12,64]{0,2,1:T(8,128)(2,1)S(1)} %bitcast.99), kind=kOutput, calls=%fused_computation.1 | convolution fusion | flops 836757504 | bytes 53264384 | tf_op jit(solution)/shard_map/qhd,khd->hqk/dot_general | solution.py:202
  463.3 42.5 %multiply_convert_fusion = (bf16[12,512,1024]{2,1,0:T(8,128)(2,1)}, bf16[12,512,1024]{2,1,0:T(8,128)(2,1)}) fusion(f32[12,512,1024]{2,1,0:T(8,128)} %get-tuple-element.122, f32[12,512]{1,0:T(8,128)S(1)} %get-tuple-element.121, f32[12,512]{1,0:T(8,128)S(1)} %copy-done.31, f32[12,512,1024]{2,1,0:T(8,128)} %get-tuple-element.109, ...), kind=kLoop, calls=%fused_computation | loop fusion | flops 75497472 | bytes 126976000 | tf_op jit(solution)/shard_map/convert_element_type | solution.py:206
  505.8 10.1 multiply_bitcast_fusion
  515.9 6.2 multiply_bitcast_fusion.1
  525.0 2.8 convolution_bitcast_fusion.2
  527.8 3.1 copy.65
  531.5 6.9 fusion.71
  538.4 7.1 multiply_convert_fusion.2
  546.7 2.8 convolution_bitcast_fusion.1
  549.5 3.3 copy.67
  552.9 10.7 fusion.60
  565.0 10.3 fusion.72
  577.0 3.1 fusion.73
  583.5 18.5 %reduce-scatter.19.cloned.1.call-done = f32[96,768]{1,0:T(8,128)} async-done(((f32[768,768]{1,0:T(8,128)}), f32[96,768]{1,0:T(8,128)}) %reduce-scatter.19.cloned.1.call-update) | async-done | bytes 294928
  603.9 69.7 %reduce-scatter.21.cloned.1.call-done = f32[96,768]{1,0:T(8,128)} async-done(((f32[768,768]{1,0:T(8,128)}), f32[96,768]{1,0:T(8,128)}) %reduce-scatter.21.cloned.1.call-update) | async-done | bytes 294928
  675.3 164.2 %reduce-scatter.15.cloned.1.call-done = f32[96,3072]{1,0:T(8,128)} async-done(((f32[768,3072]{1,0:T(8,128)}), f32[96,3072]{1,0:T(8,128)}) %reduce-scatter.15.cloned.1.call-update) | async-done | bytes 1179664 | tf_op jit(solution)/shard_map/reduce_scatter | solution.py:173
  841.7 163.7 %reduce-scatter.17.cloned.1.call-done = f32[384,768]{1,0:T(8,128)} async-done(((f32[3072,768]{1,0:T(8,128)}), f32[384,768]{1,0:T(8,128)}) %reduce-scatter.17.cloned.1.call-update) | async-done | bytes 1179664 | tf_op jit(solution)/shard_map/reduce_scatter | solution.py:174
  1007.6 3.0 fusion.74
  1013.6 35.9 %all-reduce.17 = (bf16[768]{0:T(1024)(128)(2,1)S(1)}, bf16[768]{0:T(1024)(128)(2,1)S(1)}, bf16[768]{0:T(1024)(128)(2,1)S(1)}, bf16[768]{0:T(1024)(128)(2,1)S(1)}...) all-reduce(f32[768]{0:T(1024)S(1)} %reduce_sum.206, ...), channel_id=3, replica_groups=mesh['fsdp'=8,'rep'=4] {'fsdp'}, use_global_device_ids=true, to_apply=%region_17.18.clone | all-reduce | flops 9216 | bytes 55296
  1050.2 6.4 all-reduce.19
  1061.3 6.2 add_convert_fusion
  (228 shorter events, 75.8 us)
Async XLA Ops:
  7.2 84.6 %copy-start.20 = (bf16[1024,768]{1,0:T(8,128)(2,1)S(1)}, bf16[1024,768]{1,0:T(8,128)(2,1)}, u32[]{:S(2)}) copy-start(bf16[1024,768]{1,0:T(8,128)(2,1)} %param.19) | copy-start | bytes 4718596
  7.2 87.6 %all-gather.10.cloned.1.call-start = ((), (), s32[]{:S(2)}) async-start(), calls=%async_computation.7 | async-start | bytes 1327104 | tf_op jit(solution)/shard_map/all_gather | solution.py:100
  7.9 90.7 %all-gather.12.cloned.1.call-start = ((), (), s32[]{:S(2)}) async-start(), calls=%async_computation.8 | async-start | bytes 1327104 | tf_op jit(solution)/shard_map/all_gather | solution.py:101
  8.7 129.9 %all-gather.8.cloned.1.call-start = ((), (), s32[]{:S(2)}) async-start(), calls=%async_computation.6 | async-start | bytes 1327104 | tf_op jit(solution)/shard_map/all_gather | solution.py:102
  9.4 180.9 %all-gather.14.cloned.1.call-start = ((), (), s32[]{:S(2)}) async-start(), calls=%async_computation.9 | async-start | bytes 1327104 | tf_op jit(solution)/shard_map/all_gather | solution.py:103
  10.0 251.2 %all-gather.16.cloned.1.call-start = ((), (), s32[]{:S(2)}) async-start(), calls=%async_computation.10 | async-start | bytes 5308416 | tf_op jit(solution)/shard_map/all_gather | solution.py:136
  10.6 330.7 %all-gather.18.cloned.1.call-start = ((), (), s32[]{:S(2)}) async-start(), calls=%async_computation.11 | async-start | bytes 5308416 | tf_op jit(solution)/shard_map/all_gather | solution.py:137
  11.2 569.0 %reduce-scatter.13.cloned.1.call-start = ((), (), s32[]{:S(2)}) async-start(), calls=%async_computation.12 | async-start | bytes 2654208 | tf_op jit(solution)/shard_map/reduce_scatter | solution.py:248
  60.3 281.0 %copy-start.41 = (f32[768]{0:T(1024)}, f32[768]{0:T(1024)S(1)}, u32[]{:S(2)}) copy-start(f32[768]{0:T(1024)S(1)} %convert_element_type.232) | copy-start | bytes 9220
  89.2 4.2 copy-start.33
  94.8 47.0 %copy-start.4 = (pred[512,1024]{1,0:T(8,128)(4,1)}, pred[512,1024]{1,0:T(8,128)(4,1)S(1)}, u32[]{:S(2)}) copy-start(pred[512,1024]{1,0:T(8,128)(4,1)S(1)} %get-tuple-element.102) | copy-start | bytes 1572868
  98.7 56.4 %copy-start.11 = (bf16[512,768]{0,1:T(8,128)(2,1)}, bf16[512,768]{0,1:T(8,128)(2,1)S(1)}, u32[]{:S(2)}) copy-start(bf16[512,768]{0,1:T(8,128)(2,1)S(1)} %get-tuple-element.101) | copy-start | bytes 2359300
  98.7 3.5 copy-start.13
  102.2 52.9 %copy-start.2 = (bf16[1024,768]{0,1:T(8,128)(2,1)}, bf16[1024,768]{0,1:T(8,128)(2,1)S(1)}, u32[]{:S(2)}) copy-start(bf16[1024,768]{0,1:T(8,128)(2,1)S(1)} %convolution_convert_fusion.1) | copy-start | bytes 4718596
  141.8 37.6 %copy-start.15 = (bf16[1024,768]{0,1:T(8,128)(2,1)}, bf16[1024,768]{0,1:T(8,128)(2,1)S(1)}, u32[]{:S(2)}) copy-start(bf16[1024,768]{0,1:T(8,128)(2,1)S(1)} %add_convert_fusion.4) | copy-start | bytes 4718596
  166.3 15.5 %copy-start = (f32[12,512,1024]{2,1,0:T(8,128)S(1)}, f32[12,512,1024]{2,1,0:T(8,128)}, u32[]{:S(2)}) copy-start(f32[12,512,1024]{2,1,0:T(8,128)} %get-tuple-element.109) | copy-start | bytes 75497472
  181.8 8.5 copy-start.25
  181.8 8.5 copy-start.50
  261.2 80.1 %copy-start.43 = (f32[768]{0:T(1024)S(1)}, f32[768]{0:T(1024)}, u32[]{:S(2)}) copy-start(f32[768]{0:T(1024)} %convert_element_type.236) | copy-start | bytes 9220
  351.2 3.0 copy-start.34
  352.2 5.2 copy-start.46
  354.2 17.9 %slice-start = ((s8[4718592]{0:T(1024)(128)(4,1)}), s8[4194304]{0:T(1024)(128)(4,1)S(1)}, s32[]{:S(2)}) async-start(s8[4718592]{0:T(1024)(128)(4,1)} %bitcast.115), calls=%async_computation.19 | async-start | bytes 8388608
  357.4 14.7 %copy-start.26 = (bf16[1024,768]{0,1:T(8,128)(2,1)}, bf16[1024,768]{0,1:T(8,128)(2,1)S(1)}, u32[]{:S(2)}) copy-start(bf16[1024,768]{0,1:T(8,128)(2,1)S(1)} %get-tuple-element.92) | copy-start | bytes 4718596
  357.4 14.7 %copy-start.7 = (f32[1024,768]{0,1:T(8,128)S(1)}, f32[1024,768]{0,1:T(8,128)}, u32[]{:S(2)}) copy-start(f32[1024,768]{0,1:T(8,128)} %copy-done.6) | copy-start | bytes 9437188
  357.4 14.7 %slice-start.1 = ((s8[4718592]{0:T(1024)(128)(4,1)}), s8[524288]{0:T(1024)(128)(4,1)S(1)}, s32[]{:S(2)}) async-start(s8[4718592]{0:T(1024)(128)(4,1)} %bitcast.115), calls=%async_computation.20 | async-start | bytes 1048576
  381.8 3.4 copy-start.51
  391.5 12.2 %copy-start.19 = (bf16[512,768]{0,1:T(8,128)(2,1)}, bf16[512,768]{0,1:T(8,128)(2,1)S(1)}, u32[]{:S(2)}) copy-start(bf16[512,768]{0,1:T(8,128)(2,1)S(1)} %get-tuple-element.99) | copy-start | bytes 2359300
  391.6 190.2 %reduce-scatter.23.cloned.1.call-start = ((), (), s32[]{:S(2)}) async-start(), calls=%async_computation.17 | async-start | bytes 2654208
  392.2 11.6 %copy-start.5 = (pred[512,1024]{1,0:T(8,128)(4,1)S(1)}, pred[512,1024]{1,0:T(8,128)(4,1)}, u32[]{:S(2)}) copy-start(pred[512,1024]{1,0:T(8,128)(4,1)} %copy-done.4) | copy-start | bytes 1572868
  392.2 11.6 %copy-start.30 = (f32[12,512]{1,0:T(8,128)S(1)}, f32[12,512]{1,0:T(8,128)}, u32[]{:S(2)}) copy-start(f32[12,512]{1,0:T(8,128)} %log_add_fusion.1) | copy-start | bytes 73732
  403.8 14.0 %copy-start.21 = (bf16[1024,768]{1,0:T(8,128)(2,1)S(1)}, bf16[1024,768]{1,0:T(8,128)(2,1)}, u32[]{:S(2)}) copy-start(bf16[1024,768]{1,0:T(8,128)(2,1)} %param.19) | copy-start | bytes 4718596
  420.5 3.2 copy-start.16
  463.2 138.9 %reduce-scatter.19.cloned.1.call-start = ((), (), s32[]{:S(2)}) async-start(), calls=%async_computation.15 | async-start | bytes 2654208
  505.8 10.1 copy-start.1
  522.1 2.9 copy-start.22
  527.8 3.6 copy-start.14
  531.0 7.4 copy-start.12
  531.0 142.5 %reduce-scatter.21.cloned.1.call-start = ((), (), s32[]{:S(2)}) async-start(), calls=%async_computation.16 | async-start | bytes 2654208
  549.5 3.4 copy-start.8
  549.5 3.4 copy-start.42
  552.8 286.7 %reduce-scatter.15.cloned.1.call-start = ((), (), s32[]{:S(2)}) async-start(), calls=%async_computation.13 | async-start | bytes 10616832 | tf_op jit(solution)/shard_map/reduce_scatter | solution.py:173
  563.6 441.8 %reduce-scatter.17.cloned.1.call-start = ((), (), s32[]{:S(2)}) async-start(), calls=%async_computation.14 | async-start | bytes 10616832 | tf_op jit(solution)/shard_map/reduce_scatter | solution.py:174
  575.3 494.8 %all-reduce.23.cloned.1.call-start = ((), (), s32[]{:S(2)}) async-start(), calls=%async_computation.18 | async-start | bytes 3833856 | tf_op jit(solution)/shard_map/psum | solution.py:272
  583.5 424.0 %copy-start.18 = (bf16[12,64,1024]{2,1,0:T(8,128)(2,1)S(1)}, bf16[12,64,1024]{2,1,0:T(8,128)(2,1)}, u32[]{:S(2)}) copy-start(bf16[12,64,1024]{2,1,0:T(8,128)(2,1)} %copy-done.17) | copy-start | bytes 4718596
  583.5 424.1 %copy-start.47 = (bf16[768,768]{1,0:T(8,128)(2,1)S(1)}, bf16[768,768]{1,0:T(8,128)(2,1)}, u32[]{:S(2)}) copy-start(bf16[768,768]{1,0:T(8,128)(2,1)} %all-gather.12.cloned.1.call-done) | copy-start | bytes 3538948
  1007.6 5.8 copy-start.40
  1010.7 50.6 %copy-start.10 = (f32[1024,768]{0,1:T(8,128)S(1)}, f32[1024,768]{0,1:T(8,128)}, u32[]{:S(2)}) copy-start(f32[1024,768]{0,1:T(8,128)} %copy-done.9) | copy-start | bytes 9437188
  1070.1 9.2 copy-start.29
  (19 other events, 38.6 us)
Sparse Core Ops, SparseCore 0:
  10.2 44.1 all-gather.9
  56.6 39.8 all-gather.11
  98.7 39.8 all-gather.7
  140.6 39.8 all-gather.13
  182.5 78.6 all-gather.15
  263.2 78.0 all-gather.17
  391.7 67.0 reduce-scatter.12
  463.3 67.1 reduce-scatter.22
  534.0 68.0 reduce-scatter.18
  605.4 68.0 reduce-scatter.20
  677.2 162.3 reduce-scatter.14
  843.0 162.3 reduce-scatter.16
  1009.4 48.9 all-reduce.22
where the time goes:
time: 1090 us
  waiting for transfers between devices  540 us (50%)
  matrix products  271 us (25%)
  blocking collectives  108 us (10%)
  other arithmetic  97 us (9%)
  local copies, waits for them, and re-layouts  53.8 us (5%)
  between operations  16.8 us (2%)
    reduce_scatter x1, waiting for transfers between devices, local(): lax.psum_scatter(grad_weight_inner, 'fsdp', scatter_dimension=0, tiled=True)  164 us
    reduce_scatter x1, waiting for transfers between devices, local(): lax.psum_scatter(grad_weight_outer, 'fsdp', scatter_dimension=0, tiled=True)  164 us
    unnamed x16, waiting for transfers between devices  92 us
    unnamed x2, blocking collectives  74.8 us
    all_gather x1, waiting for transfers between devices, local(): lax.all_gather(weight_inner, 'fsdp', axis=0, tiled=True)  65.6 us
    dot_general x6, matrix products, product(): return jnp.dot(left, right, preferred_element_type=jnp.float32)  61.2 us
    unnamed x148, local copies, waits for them, and re-layouts  51.8 us
    convert_element_type x1, other arithmetic, local(): grad_scores = (soft * (grad_probs - row_dot)).astype(jnp.bfloat16)  42.5 us
  transfers between devices with their start and end apart: 13, of which 7 were waited for; matrix products, arithmetic and copies ran while one was open for 32% of the time, Pallas kernels for 0%

commit v1 on v0

v1 whole, which is shorter than its diff:
```python
import functools
import math

import jax
import jax.numpy as jnp
from jax import lax
from jax.experimental import pallas as pl
from jax.experimental.pallas import tpu as pltpu
from jax.sharding import PartitionSpec as P

HEADS = 12
DH = 64
BF = jnp.bfloat16
F32 = jnp.float32
NEGATIVE = -1e30
EPSILON = 1e-12
QB = 128
KB = 128
SPAN = 5
ROWS = 256
VMEM = 60 * 1024 * 1024
ANY = pl.BlockSpec(memory_space=pl.ANY)


def dot(left, right):
    return jnp.dot(left, right, preferred_element_type=F32)


def dot_right(left, right):
    return lax.dot_general(left, right, (((1,), (1,)), ((), ())), preferred_element_type=F32)


def params(steps=1):
    return pltpu.CompilerParams(
        dimension_semantics=("arbitrary",) * steps, vmem_limit_bytes=VMEM
    )


def cost(flops, size):
    return pl.CostEstimate(flops=int(flops), bytes_accessed=int(size), transcendentals=0)


def struct(shape, dtype):
    return jax.ShapeDtypeStruct(shape, dtype)


def whole(shape):
    return pl.BlockSpec(shape, lambda i, s: (0,) * len(shape))


def rows_of(width, height=ROWS):
    return pl.BlockSpec((height, width), lambda i, s: (i, 0))


def norm(hidden):
    center = hidden - jnp.mean(hidden, axis=-1, keepdims=True)
    inverse = lax.rsqrt(jnp.mean(center * center, axis=-1, keepdims=True) + EPSILON)
    return center * inverse, inverse


def norm_back(grad, normed, inverse):
    mean = jnp.mean(grad, axis=-1, keepdims=True)
    along = jnp.mean(grad * normed, axis=-1, keepdims=True)
    return inverse * (grad - mean - normed * along)


def gelu_parts(inner):
    size = jnp.abs(inner)
    t = 1.0 / (1.0 + (0.3275911 * 0.7071067811865476) * size)
    decay = jnp.exp(-0.5 * inner * inner)
    poly = t * (
        0.254829592 + t * (-0.284496736 + t * (1.421413741 + t * (-1.453152027 + t * 1.061405429)))
    )
    tail = 0.5 * poly * decay
    phi = jnp.where(inner >= 0, 1.0 - tail, tail)
    return inner * phi, phi + inner * decay * 0.3989422804014327


def column_sum(value):
    return jnp.sum(value, axis=0, keepdims=True)


def windows(seq_row):
    tiles = seq_row.reshape(seq_row.shape[0] // QB, QB)
    below = jnp.sum((seq_row[None] < tiles[:, :1]).astype(jnp.int32), axis=1)
    upto = jnp.sum((seq_row[None] <= tiles[:, -1:]).astype(jnp.int32), axis=1)
    low = below // KB
    return jnp.concatenate([low, (upto + KB - 1) // KB - low])


def first_half(shape):
    return lax.broadcasted_iota(jnp.int32, shape, len(shape) - 1) < DH


def stack_pair(pair):
    low = first_half(pair.shape)
    zero = jnp.zeros_like(pair)
    return jnp.concatenate([jnp.where(low, pair, zero), jnp.where(low, zero, pair)], axis=0)


def fold_pair(both):
    half = both.shape[0] // 2
    return jnp.where(first_half((half, both.shape[1])), both[:half], both[half:])


def attend_kernel(win, seq_ref, mask_ref, q_ref, k_ref, v_ref, ctx_ref, p_ref, bias_ref):
    i = pl.program_id(0)
    low = win[i]
    count = win[pl.num_programs(0) + i]
    pairs = q_ref.shape[1] // (2 * DH)

    def body(n):
        w = n * KB
        base = pl.multiple_of(low * KB, KB)
        start = pl.multiple_of(i * QB, QB)
        own = jnp.broadcast_to(seq_ref[:, pl.ds(start, QB)], (QB, QB)).T
        rows = start + lax.broadcasted_iota(jnp.int32, (QB, KB), 0)
        for b in range(n):
            off = pl.multiple_of(base + b * KB, KB)
            cols = off + lax.broadcasted_iota(jnp.int32, (QB, KB), 1)
            visible = (mask_ref[:, pl.ds(off, KB)] == 1) | (rows == cols)
            allowed = (own == seq_ref[:, pl.ds(off, KB)]) & visible
            bias_ref[:, b * KB : (b + 1) * KB] = jnp.where(allowed, 0.0, NEGATIVE).astype(F32)
        for pair in range(pairs):
            lanes = slice(pair * 2 * DH, (pair + 1) * 2 * DH)
            bias = bias_ref[:, :w]
            scores = dot_right(stack_pair(q_ref[:, lanes]), k_ref[pl.ds(base, w), lanes])
            scores = scores + jnp.concatenate([bias, bias], axis=0)
            expon = jnp.exp(scores - jnp.max(scores, axis=1, keepdims=True))
            soft = expon * (1.0 / jnp.sum(expon, axis=1, keepdims=True))
            probs = soft.astype(BF)
            p_ref[0, pair, :, :w] = probs
            ctx_ref[:, lanes] = fold_pair(dot(probs, v_ref[pl.ds(base, w), lanes])).astype(BF)

    for n in range(1, SPAN + 1):
        pl.when(count == n)(functools.partial(body, n))


def attend(win, seq, mask, q, k, v):
    tok, d = q.shape
    tiles, pairs = tok // QB, d // (2 * DH)
    return pl.pallas_call(
        attend_kernel,
        grid_spec=pltpu.PrefetchScalarGridSpec(
            num_scalar_prefetch=1,
            grid=(tiles,),
            in_specs=[whole(seq.shape), whole(mask.shape), rows_of(d, QB), whole(k.shape), whole(v.shape)],
            out_specs=[
                rows_of(d, QB),
                pl.BlockSpec((1, pairs, 2 * QB, SPAN * KB), lambda i, s: (i, 0, 0, 0)),
            ],
            scratch_shapes=[pltpu.VMEM((QB, SPAN * KB), F32)],
        ),
        out_shape=[struct((tok, d), BF), struct((tiles, pairs, 2 * QB, SPAN * KB), BF)],
        compiler_params=params(),
        cost_estimate=cost(1.4e10, 2e7),
        name="attend",
    )(win, seq, mask, q, k, v)


def attend_back_kernel(
    win, q_ref, k_ref, v_ref, ctx_ref, do_ref, p_ref, dq_ref, dk_ref, dv_ref, bq_ref, bv_ref, dkt, dvt
):
    i = pl.program_id(0)
    low = win[i]
    count = win[pl.num_programs(0) + i]
    pairs = q_ref.shape[1] // (2 * DH)

    @pl.when(i == 0)
    def _():
        dkt[...] = jnp.zeros_like(dkt)
        dvt[...] = jnp.zeros_like(dvt)
        bq_ref[...] = jnp.zeros_like(bq_ref)

    def body(n):
        w = n * KB
        base = pl.multiple_of(low * KB, KB)
        for pair in range(pairs):
            lanes = slice(pair * 2 * DH, (pair + 1) * 2 * DH)
            grad = do_ref[:, lanes]
            do = stack_pair(grad)
            delta = jnp.sum(
                stack_pair(grad.astype(F32) * ctx_ref[:, lanes].astype(F32)), axis=1, keepdims=True
            )
            probs = p_ref[0, pair, :, :w]
            grad_probs = dot_right(do, v_ref[pl.ds(base, w), lanes])
            ds = (probs.astype(F32) * (grad_probs - delta)).astype(BF)
            dq = (fold_pair(dot(ds, k_ref[pl.ds(base, w), lanes])) * (1.0 / math.sqrt(DH))).astype(BF)
            dq_ref[:, lanes] = dq
            bq_ref[0:1, lanes] += column_sum(dq.astype(F32))
            dvt[lanes, pl.ds(base, w)] += dot(do.T, probs)
            dkt[lanes, pl.ds(base, w)] += dot(stack_pair(q_ref[:, lanes]).T, ds)

    for n in range(1, SPAN + 1):
        pl.when(count == n)(functools.partial(body, n))

    @pl.when(i == pl.num_programs(0) - 1)
    def _():
        bv_ref[...] = jnp.zeros_like(bv_ref)
        for o in range(0, k_ref.shape[0], QB):
            dk_ref[o : o + QB, :] = dkt[:, o : o + QB].T.astype(BF)
            dv = dvt[:, o : o + QB].T.astype(BF)
            dv_ref[o : o + QB, :] = dv
            bv_ref[0:1, :] += column_sum(dv.astype(F32))


def attend_back(win, q, k, v, ctx, do, p):
    tok, d = q.shape
    tiles, pairs = tok // QB, d // (2 * DH)
    row = rows_of(d, QB)
    return pl.pallas_call(
        attend_back_kernel,
        grid_spec=pltpu.PrefetchScalarGridSpec(
            num_scalar_prefetch=1,
            grid=(tiles,),
            in_specs=[
                row,
                whole(k.shape),
                whole(v.shape),
                row,
                row,
                pl.BlockSpec((1, pairs, 2 * QB, SPAN * KB), lambda i, s: (i, 0, 0, 0)),
            ],
            out_specs=[row, whole((tok, d)), whole((tok, d)), whole((8, d)), whole((8, d))],
            scratch_shapes=[pltpu.VMEM((d, tok), F32), pltpu.VMEM((d, tok), F32)],
        ),
        out_shape=[struct((tok, d), BF)] * 3 + [struct((8, d), F32)] * 2,
        compiler_params=params(),
        cost_estimate=cost(2e10, 2e7),
        name="attend_back",
    )(win, q, k, v, ctx, do, p)


class Weight:
    def __init__(self, shard, first):
        self.rows, self.width = shard.shape
        self.shard = shard
        self.first = first


class Group:
    def __init__(self, mesh, shards):
        self.fsdp = mesh.shape["fsdp"]
        self.fast = fast_path(mesh, shards)
        self.pieces = []
        self.weights = []
        first = 0
        for shard in shards:
            self.weights.append(Weight(shard, first))
            first += shard.size // (2 * PIECE)

    def full(self, k):
        weight = self.weights[k]
        return (weight.rows * (self.fsdp if self.fast else 1), weight.width)

    def payload(self, core):
        parts = []
        for weight in self.weights:
            half = lax.dynamic_slice_in_dim(weight.shard, core * (weight.rows // 2), weight.rows // 2, 0)
            parts += [half[:, c : c + PIECE] for c in range(0, weight.width, PIECE)]
        return jnp.concatenate(parts, axis=0)

    def operands(self, used):
        if not self.fast:
            return [self.weights[k].shard for k in used]
        return [self.weights[k].shard for k in used] + [array for array, _, _ in self.pieces]

    def load(self, used, table, refs, targets, sems):
        if not self.fast:
            for n, target in enumerate(targets):
                pltpu.make_async_copy(refs[n], target, sems.at[n]).start()
            return
        core = table[self.fsdp]
        for n, k in enumerate(used):
            weight, target, sem = self.weights[k], targets[n], sems.at[n]
            half = weight.rows // 2
            base = pl.multiple_of(table[0] * weight.rows, weight.rows)
            pltpu.make_async_copy(refs[n], target.at[pl.ds(base, weight.rows), :], sem).start()
            for piece, (_, sources, mate) in zip(refs[len(used) :], self.pieces):
                side = (1 - core) if mate else core
                height = piece.shape[0] // len(sources)
                for order, source in enumerate(sources):
                    row = pl.multiple_of(table[source] * weight.rows + side * half, 16)
                    for c in range(weight.width // PIECE):
                        start = order * height + weight.first + c * half
                        pltpu.make_async_copy(
                            piece.at[start : start + half, :],
                            target.at[pl.ds(row, half), c * PIECE : (c + 1) * PIECE],
                            sem,
                        ).start()

    def wait(self, targets, sems):
        for n, target in enumerate(targets):
            pltpu.make_async_copy(target, target, sems.at[n]).wait()

    def scratch(self, used):
        return [pltpu.VMEM(self.full(k), BF) for k in used] + [pltpu.SemaphoreType.DMA((len(used),))]


PIECE = 768


def fast_path(mesh, shards):
    return (
        mesh.shape["fsdp"] == 8
        and mesh.shape["rep"] == 4
        and all(s.shape[0] % 32 == 0 and s.shape[1] % PIECE == 0 for s in shards)
    )


RING = (0, 2, 4, 6, 7, 5, 3, 1)


def ring_table():
    size = len(RING)
    place = {v: p for p, v in enumerate(RING)}
    steps = list(range(0, -(size // 2) - 1, -1)) + list(range(1, size - size // 2))
    return [[RING[(place[f] + s) % size] for s in steps] for f in range(size)]


def ring_step(value, step):
    size = len(RING)
    return lax.ppermute(value, "fsdp", [(RING[p], RING[(p + step) % size]) for p in range(size)])


def rep_step(value, bits):
    return lax.ppermute(value, "rep", [(r, r ^ bits) for r in range(4)])


def pallas(body, name, grid, table, operands, in_specs, out_specs, outs, scratch, flops):
    size = sum(o.size * o.dtype.itemsize for o in list(operands) + list(outs))
    return pl.pallas_call(
        body,
        grid_spec=pltpu.PrefetchScalarGridSpec(
            num_scalar_prefetch=1, grid=grid, in_specs=in_specs, out_specs=out_specs, scratch_shapes=scratch
        ),
        out_shape=outs,
        compiler_params=params(len(grid)),
        cost_estimate=cost(flops, size),
        name=name,
    )(table, *operands)


def project(table, group, tokens, vectors):
    tok, d = tokens.shape
    used = (0, 1, 2)
    extra = group.operands(used)

    def body(s, x_ref, vec_ref, *refs):
        pieces, (q_ref, k_ref, v_ref, *weights, sems) = refs[: len(extra)], refs[len(extra) :]

        @pl.when(pl.program_id(0) == 0)
        def _():
            group.load(used, s, pieces, weights, sems)
            group.wait(weights, sems)

        x = x_ref[...]
        q = (dot(x, weights[0][...]) + vec_ref[0:1, :]).astype(BF)
        q_ref[...] = q * jnp.asarray(1.0 / math.sqrt(DH), BF)
        k_ref[...] = dot(x, weights[1][...]).astype(BF)
        v_ref[...] = (dot(x, weights[2][...]) + vec_ref[1:2, :]).astype(BF)

    return pallas(
        body,
        "project",
        (tok // ROWS,),
        table,
        [tokens, vectors] + extra,
        [rows_of(d), whole(vectors.shape)] + [ANY] * len(extra),
        [rows_of(d)] * 3,
        [struct((tok, d), BF)] * 3,
        group.scratch(used),
        6 * tok * d * d,
    )


def inner_block(table, group, context, tokens, vectors, bias_inner):
    tok, d = tokens.shape
    used = (0, 1)
    ff = group.full(1)[1]
    extra = group.operands(used)

    def body(s, ctx_ref, x_ref, vec_ref, bias_ref, *refs):
        pieces = refs[: len(extra)]
        hid_ref, low_ref, act_ref, slope_ref, w_out, w_in, sems = refs[len(extra) :]

        @pl.when(pl.program_id(0) == 0)
        def _():
            group.load(used, s, pieces, (w_out, w_in), sems)
            group.wait((w_out, w_in), sems)

        hidden = x_ref[...].astype(F32) + dot(ctx_ref[...], w_out[...]) + vec_ref[2:3, :]
        hid_ref[...] = hidden
        normed, _ = norm(hidden)
        low = (normed * vec_ref[3:4, :] + vec_ref[4:5, :]).astype(BF)
        low_ref[...] = low
        for c in range(0, ff, d):
            act, slope = gelu_parts(dot(low, w_in[:, c : c + d]) + bias_ref[0:1, c : c + d])
            act_ref[:, c : c + d] = act.astype(BF)
            slope_ref[:, c : c + d] = slope.astype(BF)

    return pallas(
        body,
        "inner_block",
        (tok // ROWS,),
        table,
        [context, tokens, vectors, bias_inner] + extra,
        [rows_of(d), rows_of(d), whole(vectors.shape), whole(bias_inner.shape)] + [ANY] * len(extra),
        [rows_of(d), rows_of(d), rows_of(ff), rows_of(ff)],
        [struct((tok, d), F32), struct((tok, d), BF), struct((tok, ff), BF), struct((tok, ff), BF)],
        group.scratch(used),
        2 * tok * d * (d + ff),
    )


def outer_block(table, group, activated, hidden, out_grad, vectors):
    tok, d = hidden.shape
    ff = activated.shape[1]
    used = (0,)
    extra = group.operands(used)

    def body(s, act_ref, hid_ref, g_ref, vec_ref, *refs):
        pieces = refs[: len(extra)]
        out_ref, second_ref, low_ref, sum_ref, w_outer, sems = refs[len(extra) :]

        @pl.when(pl.program_id(0) == 0)
        def _():
            group.load(used, s, pieces, (w_outer,), sems)
            sum_ref[...] = jnp.zeros_like(sum_ref)
            group.wait((w_outer,), sems)

        normed, _ = norm(hid_ref[...])
        first = normed * vec_ref[3:4, :] + vec_ref[4:5, :]
        normed, inverse = norm(first + dot(act_ref[...], w_outer[...]) + vec_ref[5:6, :])
        gain = vec_ref[6:7, :]
        out_ref[...] = (normed * gain + vec_ref[7:8, :]).astype(BF)
        grad = g_ref[...].astype(F32)
        second = norm_back(grad * gain, normed, inverse)
        second_ref[...] = second
        low = second.astype(BF)
        low_ref[...] = low
        sum_ref[0:1, :] += column_sum(grad * normed)
        sum_ref[1:2, :] += column_sum(grad)
        sum_ref[2:3, :] += column_sum(low.astype(F32))

    return pallas(
        body,
        "outer_block",
        (tok // ROWS,),
        table,
        [activated, hidden, out_grad, vectors] + extra,
        [rows_of(ff), rows_of(d), rows_of(d), whole(vectors.shape)] + [ANY] * len(extra),
        [rows_of(d), rows_of(d), rows_of(d), whole((8, d))],
        [struct((tok, d), BF), struct((tok, d), F32), struct((tok, d), BF), struct((8, d), F32)],
        group.scratch(used),
        2 * tok * d * ff,
    )


def active_back(table, group, grad_low, slope):
    tok, d = grad_low.shape
    ff = slope.shape[1]
    used = (0,)
    extra = group.operands(used)

    def body(s, g_ref, slope_ref, *refs):
        pieces = refs[: len(extra)]
        out_ref, sum_ref, w_outer, sems = refs[len(extra) :]

        @pl.when(pl.program_id(0) == 0)
        def _():
            group.load(used, s, pieces, (w_outer,), sems)
            sum_ref[...] = jnp.zeros_like(sum_ref)
            group.wait((w_outer,), sems)

        g = g_ref[...]
        for c in range(0, ff, d):
            low = (dot_right(g, w_outer[c : c + d, :]) * slope_ref[:, c : c + d].astype(F32)).astype(BF)
            out_ref[:, c : c + d] = low
            sum_ref[0:1, c : c + d] += column_sum(low.astype(F32))

    return pallas(
        body,
        "active_back",
        (tok // ROWS,),
        table,
        [grad_low, slope] + extra,
        [rows_of(d), rows_of(ff)] + [ANY] * len(extra),
        [rows_of(ff), whole((8, ff))],
        [struct((tok, ff), BF), struct((8, ff), F32)],
        group.scratch(used),
        2 * tok * d * ff,
    )


def inner_back(table, group, grad_inner, grad_second, hidden, vectors):
    tok, d = hidden.shape
    ff = grad_inner.shape[1]
    used = (0, 1)
    extra = group.operands(used)

    def body(s, g_ref, second_ref, hid_ref, vec_ref, *refs):
        pieces = refs[: len(extra)]
        out_ref, low_ref, ctx_ref, sum_ref, w_out, w_in, sems = refs[len(extra) :]

        @pl.when(pl.program_id(0) == 0)
        def _():
            group.load(used, s, pieces, (w_out, w_in), sems)
            sum_ref[...] = jnp.zeros_like(sum_ref)
            group.wait((w_out, w_in), sems)

        grad = second_ref[...] + dot_right(g_ref[...], w_in[...])
        normed, inverse = norm(hid_ref[...])
        hidden_grad = norm_back(grad * vec_ref[3:4, :], normed, inverse)
        out_ref[...] = hidden_grad
        low = hidden_grad.astype(BF)
        low_ref[...] = low
        ctx_ref[...] = dot_right(low, w_out[...]).astype(BF)
        sum_ref[0:1, :] += column_sum(grad * normed)
        sum_ref[1:2, :] += column_sum(grad)
        sum_ref[2:3, :] += column_sum(low.astype(F32))

    return pallas(
        body,
        "inner_back",
        (tok // ROWS,),
        table,
        [grad_inner, grad_second, hidden, vectors] + extra,
        [rows_of(ff), rows_of(d), rows_of(d), whole(vectors.shape)] + [ANY] * len(extra),
        [rows_of(d), rows_of(d), rows_of(d), whole((8, d))],
        [struct((tok, d), F32), struct((tok, d), BF), struct((tok, d), BF), struct((8, d), F32)],
        group.scratch(used),
        2 * tok * d * (d + ff),
    )


def tokens_back(table, group, grad_hidden, grads):
    tok, d = grad_hidden.shape
    used = (0, 1, 2)
    extra = group.operands(used)

    def body(s, hid_ref, q_ref, k_ref, v_ref, *refs):
        pieces, (out_ref, *weights, sems) = refs[: len(extra)], refs[len(extra) :]

        @pl.when(pl.program_id(0) == 0)
        def _():
            group.load(used, s, pieces, weights, sems)
            group.wait(weights, sems)

        total = hid_ref[...]
        for ref, weight in zip((q_ref, k_ref, v_ref), weights):
            total = total + dot_right(ref[...], weight[...])
        out_ref[...] = total.astype(BF)

    return pallas(
        body,
        "tokens_back",
        (tok // ROWS,),
        table,
        [grad_hidden, *grads] + extra,
        [rows_of(d)] * 4 + [ANY] * len(extra),
        [rows_of(d)],
        [struct((tok, d), BF)],
        group.scratch(used),
        6 * tok * d * d,
    )[0]


BLOCK = 384


def weight_grad(choice, side, left, rights, owner_rows, received=None, order=None):
    tok, m = left.shape
    halves = [r.shape[1] // 2 for r in rights]
    n = sum(halves)
    count = len(rights)
    per = BLOCK // owner_rows
    flops = 2 * tok * m * n

    def product(left_ref, right_refs):
        right = jnp.concatenate([r[...] for r in right_refs], axis=1)
        return dot(left_ref[...].T, right)

    in_specs = [pl.BlockSpec((tok, BLOCK), lambda i, s: (0, i))] + [
        pl.BlockSpec((tok, h), lambda i, s: (0, s[0] if side == 0 else 1 - s[0])) for h in halves
    ]
    if received is None:

        def body(s, left_ref, *refs):
            refs[count][...] = product(left_ref, refs[:count]).astype(BF)

        return pallas(
            body,
            "weight_grad",
            (m // BLOCK,),
            choice,
            [left, *rights],
            in_specs,
            [pl.BlockSpec((BLOCK, n), lambda i, s: (i, 0))],
            [struct((m, n), BF)],
            [],
            flops,
        )[0]

    paired = order == "y" and per == 1

    def body(s, left_ref, *refs):
        add_ref, keep_ref, send_ref = refs[count:]
        total = (product(left_ref, refs[:count]) + add_ref[...].astype(F32)).astype(BF)
        if paired:
            mine = (pl.program_id(0) % 2) == s[2]

            @pl.when(mine)
            def _():
                keep_ref[...] = total

            @pl.when(jnp.logical_not(mine))
            def _():
                send_ref[...] = total

            return
        shape = (per, 2, owner_rows // 2, n) if order == "x" else (per // 2, 2, owner_rows, n)
        parts = total.reshape(shape)
        bit = s[1] if order == "x" else s[2]
        low, high = parts[:, 0].reshape(BLOCK // 2, n), parts[:, 1].reshape(BLOCK // 2, n)
        keep_ref[...] = jnp.where(bit == 0, low, high)
        send_ref[...] = jnp.where(bit == 0, high, low)

    if paired:
        out_spec = pl.BlockSpec((BLOCK, n), lambda i, s: (i // 2, 0))
    else:
        out_spec = pl.BlockSpec((BLOCK // 2, n), lambda i, s: (i, 0))
    return pallas(
        body,
        "weight_grad_sum",
        (m // BLOCK,),
        choice,
        [left, *rights, received],
        in_specs + [pl.BlockSpec((BLOCK, n), lambda i, s: (i, 0))],
        [out_spec] * 2,
        [struct((m // 2, n), BF)] * 2,
        [],
        flops,
    )


def axis_step(value, axis):
    if axis == "x":
        return rep_step(value, 2)
    return lax.ppermute(value, "fsdp", [(f, f ^ 1) for f in range(8)])


def added(keep, received):
    return (keep.astype(F32) + received.astype(F32)).astype(BF)


class Reduce:
    def __init__(self, place, left, rights, owner_rows, order):
        self.place, self.left, self.rights = place, left, rights
        self.rows, self.order = owner_rows, order
        self.widths = [r.shape[1] for r in rights]
        self.n = sum(self.widths) // 2

    def core(self):
        other = weight_grad(self.place.choice, 1, self.left, self.rights, self.rows)
        self.received = rep_step(other, 1)

    def first(self):
        keep, send = weight_grad(
            self.place.choice, 0, self.left, self.rights, self.rows, self.received, self.order
        )
        self.keep, self.received = keep, axis_step(send, self.order)

    def second(self):
        total = added(self.keep, self.received)
        if self.order == "x":
            parts, bit, last = total.reshape(4, 2, self.rows // 2, self.n), self.place.y, "y"
        else:
            parts, bit, last = total.reshape(4, 2, self.rows // 2, self.n), self.place.x, "x"
        self.keep = lax.dynamic_index_in_dim(parts, bit, 1, keepdims=False)
        self.received = axis_step(lax.dynamic_index_in_dim(parts, 1 - bit, 1, keepdims=False), last)

    def third(self):
        parts = added(self.keep, self.received)
        z = self.place.z
        chunk = lambda k: lax.dynamic_index_in_dim(parts, (z + k) % 4, 0, keepdims=False)
        moved = [
            lax.ppermute(chunk(k), "fsdp", [(f, (f // 2 + k) % 4 * 2 + f % 2) for f in range(8)])
            for k in (1, 2, 3)
        ]
        total = chunk(0).astype(F32)
        for part in moved:
            total = total + part.astype(F32)
        self.own = total.astype(BF)

    def last(self):
        own = self.own
        others = [rep_step(own, bits) for bits in (1, 2, 3)]
        core, x = self.place.core, self.place.x

        def wide(mine, mate):
            outs, start = [], 0
            for width in self.widths:
                a, b = mine[:, start : start + width // 2], mate[:, start : start + width // 2]
                outs.append(jnp.where(core == 0, jnp.concatenate([a, b], 1), jnp.concatenate([b, a], 1)))
                start += width // 2
            return outs

        here, there = wide(own, others[0]), wide(others[1], others[2])
        return [
            jnp.where(x == 0, jnp.concatenate([a, b], 0), jnp.concatenate([b, a], 0)).astype(F32)
            for a, b in zip(here, there)
        ]


class Place:
    def __init__(self, mesh):
        f, r = lax.axis_index("fsdp"), lax.axis_index("rep")
        self.f, self.core, self.x = f, r % 2, r // 2
        self.y, self.z = f % 2, f // 2
        self.choice = jnp.stack([self.core, self.x, self.y]).astype(jnp.int32)
        if mesh.shape["fsdp"] == len(RING):
            row = lax.dynamic_index_in_dim(jnp.array(ring_table(), jnp.int32), f, 0, keepdims=False)
            self.table = jnp.concatenate([row, self.core[None].astype(jnp.int32)])
        else:
            self.table = jnp.zeros((1,), jnp.int32)


def plain_gather(mesh, shards):
    return Group(mesh, [lax.all_gather(s, "fsdp", axis=0, tiled=True) for s in shards])


def ring_gather(groups, core):
    half = len(RING) // 2
    for group in groups:
        up = down = group.payload(core)
        for step in range(1, half + 1):
            up = ring_step(up, 1)
            group.pieces.append((up, (step,), False))
            group.pieces.append((rep_step(up, 1), (step,), True))
            if step < half:
                down = ring_step(down, -1)
                group.pieces.append((down, (half + step,), False))
                group.pieces.append((rep_step(down, 1), (half + step,), True))


def local(mesh, *args):
    (
        tokens, seq_ids, key_mask, weight_query, bias_query, weight_key, weight_value, bias_value,
        weight_out, bias_out, norm1_gain, norm1_bias, weight_inner, bias_inner, weight_outer, bias_outer,
        norm2_gain, norm2_bias, out_grad,
    ) = args
    place = Place(mesh)
    table = place.table
    fsdp = mesh.shape["fsdp"]
    d = tokens.shape[1]
    win = windows(seq_ids[0])
    shards = [[weight_query, weight_key, weight_value], [weight_out, weight_inner], [weight_outer]]
    fast = all(fast_path(mesh, s) for s in shards)
    if fast:
        groups = [Group(mesh, s) for s in shards]
        ring_gather(groups, place.core)
    else:
        groups = [plain_gather(mesh, s) for s in shards]
    qkv, inner_group, outer_group = groups
    narrow = [bias_query, bias_value, bias_out, norm1_gain, norm1_bias, bias_outer, norm2_gain, norm2_bias]
    small = lax.all_gather(jnp.concatenate(narrow + [bias_inner]), "fsdp", axis=0, tiled=False)
    split = len(narrow) * (d // fsdp)
    vectors = small[:, :split].reshape(fsdp, len(narrow), d // fsdp).transpose(1, 0, 2).reshape(len(narrow), d)
    vectors = vectors.astype(F32)
    full_bias_inner = jnp.broadcast_to(small[:, split:].reshape(1, -1), (8, bias_inner.size * fsdp)).astype(F32)

    q, k, v = project(table, qkv, tokens, vectors)
    context, probs = attend(win, seq_ids, key_mask, q, k, v)
    hidden, first_low, activated, slope = inner_block(table, inner_group, context, tokens, vectors, full_bias_inner)
    layer_out, grad_second, grad_outer, sums2 = outer_block(
        table, outer_group, activated, hidden, out_grad, vectors
    )
    outer_sum = Reduce(place, activated, [grad_outer], weight_outer.shape[0], "x")
    if fast:
        outer_sum.core()
    grad_inner, sums_inner = active_back(table, outer_group, grad_outer, slope)
    inner_sum = Reduce(place, first_low, [grad_inner], weight_inner.shape[0], "y")
    if fast:
        outer_sum.first()
        inner_sum.core()
    grad_hidden, grad_att, grad_context, sums1 = inner_back(
        table, inner_group, grad_inner, grad_second, hidden, vectors
    )
    out_sum = Reduce(place, context, [grad_att], weight_out.shape[0], "y")
    if fast:
        inner_sum.first()
        outer_sum.second()
        out_sum.core()
        out_sum.first()
        inner_sum.second()
    dq, dk, dv, sum_q, sum_v = attend_back(win, q, k, v, context, grad_context, probs)
    query_sum = Reduce(place, tokens, [dq, dk, dv], weight_query.shape[0], "x")
    if fast:
        outer_sum.third()
        inner_sum.third()
        out_sum.second()
        query_sum.core()
    grad_tokens = tokens_back(table, qkv, grad_hidden, (dq, dk, dv))
    sums = jnp.concatenate(
        [sum_q[0], sum_v[0], sums1[2], sums1[0], sums1[1], sums_inner[0], sums2[2], sums2[0], sums2[1]]
    )
    sums = lax.psum(sums, ("fsdp", "rep"))
    if fast:
        query_sum.first()
        out_sum.third()
        query_sum.second()
        query_sum.third()
        (final_outer,), (final_inner,), (final_out,) = outer_sum.last(), inner_sum.last(), out_sum.last()
        final_query, final_key, final_value = query_sum.last()
    else:

        def plain(left, right):
            halves = [
                weight_grad(jnp.zeros((3,), jnp.int32), side, left, [right], left.shape[1] // 8)
                for side in (0, 1)
            ]
            owned = lax.psum_scatter(jnp.concatenate(halves, 1), "fsdp", scatter_dimension=0, tiled=True)
            return lax.psum(owned, "rep").astype(F32)

        final_outer = plain(activated, grad_outer)
        final_inner = plain(first_low, grad_inner)
        final_out = plain(context, grad_att)
        final_query, final_key, final_value = (plain(tokens, g) for g in (dq, dk, dv))

    starts = [0]
    for width in (d, d, d, d, d, bias_inner.size * fsdp, d, d, d):
        starts.append(starts[-1] + width)
    owned = [
        lax.dynamic_slice_in_dim(sums, a + place.f * ((b - a) // fsdp), (b - a) // fsdp, 0)
        for a, b in zip(starts[:-1], starts[1:])
    ]
    return (
        layer_out,
        grad_tokens,
        final_query,
        owned[0],
        final_key,
        final_value,
        owned[1],
        final_out,
        owned[2],
        owned[3],
        owned[4],
        final_inner,
        owned[5],
        final_outer,
        owned[6],
        owned[7],
        owned[8],
    )


def solution(mesh):
    rows, shard, part = P(("fsdp", "rep"), None), P("fsdp", None), P("fsdp")
    return jax.shard_map(
        functools.partial(local, mesh),
        mesh=mesh,
        in_specs=(
            rows, rows, rows, shard, part, shard, shard, part, shard, part, part, part, shard, part, shard,
            part, part, part, rows,
        ),
        out_specs=(
            rows, rows, shard, part, shard, shard, part, shard, part, part, part, shard, part, shard, part,
            part, part,
        ),
        check_vma=False,
    )
```

time: 1090 us -> 482 us (0.44)
  waiting for transfers between devices: 540 us -> 96.2 us
  matrix products: 271 us -> 0 us
  Pallas kernels: 0 us -> 188 us
  other arithmetic: 97 us -> 12.7 us
  starting transfers between devices: 0.92 us -> 62 us
  local copies, waits for them, and re-layouts: 53.8 us -> 29.2 us
  blocking collectives: 108 us -> 83.7 us
  between operations: 16.8 us -> 1.97 us
    reduce_scatter x3 -> x0, waiting for transfers between devices: 328 us -> none  [the longest x1 164 us: local(): lax.psum_scatter(grad_weight_inner, 'fsdp', scatter_dimension=0, tiled=True)]
    dot_general x30 -> x0, matrix products: 271 us -> none  [the longest x6 61.2 us: product(): return jnp.dot(left, right, preferred_element_type=jnp.float32)]
    pallas_call x0 -> x16, Pallas kernels: none -> 188 us  [the longest x14 143 us: pallas(): pl.pallas_call(body, grid_spec=pltpu.PrefetchScalarGridSpec(num_scalar_pr...]
    all_gather x6 -> x0, waiting for transfers between devices: 120 us -> none  [the longest x1 65.6 us: local(): lax.all_gather(weight_inner, 'fsdp', axis=0, tiled=True)]
    ppermute x0 -> x78, waiting for transfers between devices: none -> 96.2 us  [the longest x41 39.1 us: rep_step(): return lax.ppermute(value, 'rep', [(r, r ^ bits) for r in range(4)])]
    unnamed x16 -> x0, waiting for transfers between devices: 92 us -> none
    unnamed x2 -> x0, blocking collectives: 74.8 us -> none
    ppermute x0 -> x78, starting transfers between devices: none -> 62 us  [the longest x21 22.3 us: ring_step(): lax.ppermute(value, 'fsdp', [(RING[p], RING[(p + step) % size]) for p in...]
  transfers between devices with their start and end apart: 13 -> 78, of which waited for: 7 -> 21; matrix products, arithmetic and copies ran while one was open for 32% -> 7% of each run, Pallas kernels for 0% -> 34%
where the time goes in v1:
time: 482 us; the launch traced here: 473 us
  Pallas kernels  188 us (39%)
  waiting for transfers between devices  96.2 us (20%)
  blocking collectives  83.7 us (17%)
  starting transfers between devices  62 us (13%)
  local copies, waits for them, and re-layouts  29.2 us (6%)
  other arithmetic  12.7 us (3%)
    pallas_call x14, Pallas kernels, pallas(): pl.pallas_call(body, grid_spec=pltpu.PrefetchScalarGridSpec(num_scalar_pr...  143 us
    psum x1, blocking collectives, local(): sums = lax.psum(sums, ('fsdp', 'rep'))  47.2 us
    ppermute x41, waiting for transfers between devices, rep_step(): return lax.ppermute(value, 'rep', [(r, r ^ bits) for r in range(4)])  39.1 us
    all_gather x1, blocking collectives, local(): lax.all_gather(jnp.concatenate(narrow + [bias_inner]), 'fsdp', axis=0, ti...  36.5 us
    ppermute x21, waiting for transfers between devices, ring_step(): lax.ppermute(value, 'fsdp', [(RING[p], RING[(p + step) % size]) for p in...  34.8 us
    pallas_call x1, Pallas kernels, attend(): pl.pallas_call(attend_kernel, grid_spec=pltpu.PrefetchScalarGridSpec(num_...  23.1 us
    ppermute x21, starting transfers between devices, ring_step(): lax.ppermute(value, 'fsdp', [(RING[p], RING[(p + step) % size]) for p in...  22.3 us
    pallas_call x1, Pallas kernels, attend_back(): pl.pallas_call(attend_back_kernel, grid_spec=pltpu.PrefetchScalarGridSpec...  21.3 us
  transfers between devices with their start and end apart: 78, of which 21 were waited for; matrix products, arithmetic and copies ran while one was open for 7% of the time, Pallas kernels for 34%

profile of v1, /device:TPU:0, one launch (start us, length us, event | category | flops | bytes accessed | tf_op | source)
XLA Modules:
  0.0 473.5 jit_solution(10080489286143697978)
XLA Ops:
  2.8 3.1 collective-permute-start
  6.8 2.1 collective-permute-start.28
  12.0 2.1 collective-permute-start.30
  15.0 3.4 collective-permute-done.28.refs_1_
  18.4 2.1 collective-permute-start.6
  20.6 36.5 %all-gather.1 = bf16[8,1,1152]{2,1,0:T(2,128)(2,1)S(1)} all-gather(bf16[1,1,1152]{2,1,0:T(2,128)(2,1)S(1)} %reshape.88), channel_id=2, replica_groups=mesh['fsdp'=8,'rep'=4] {'fsdp'}, dimensions={0}, use_global_device_ids=true | all-gather | bytes 20736 | tf_op jit(solution)/shard_map/all_gather | solution.py:767
  58.5 2.0 collective-permute-start.34
  60.7 6.9 %collective-permute-done.32.refs_5_ = bf16[192,768]{1,0:T(8,128)(2,1)S(1)} collective-permute-done((bf16[192,768]{1,0:T(8,128)(2,1)S(1)}, bf16[192,768]{1,0:T(8,128)(2,1)S(1)}, u32[]{:S(2)}, u32[]{:S(2)}) %collective-permute-start.32) | collective-permute-done | bytes 294944 | tf_op jit(solution)/shard_map/ppermute | solution.py:323
  67.7 2.0 collective-permute-start.10
  70.6 8.8 %collective-permute-done.8.refs_11_ = bf16[144,768]{1,0:T(8,128)(2,1)} collective-permute-done((bf16[144,768]{1,0:T(8,128)(2,1)}, bf16[144,768]{1,0:T(8,128)(2,1)}, u32[]{:S(2)}, u32[]{:S(2)}) %collective-permute-start.8) | collective-permute-done | bytes 221216 | tf_op jit(solution)/shard_map/ppermute | solution.py:323
  84.7 11.2 %collective-permute-done.12.refs_15_ = bf16[144,768]{1,0:T(8,128)(2,1)} collective-permute-done((bf16[144,768]{1,0:T(8,128)(2,1)}, bf16[144,768]{1,0:T(8,128)(2,1)}, u32[]{:S(2)}, u32[]{:S(2)}) %collective-permute-start.12) | collective-permute-done | bytes 221216 | tf_op jit(solution)/shard_map/ppermute | solution.py:323
  100.9 1.7 collective-permute-start.38
  102.7 8.9 %project.1 = (bf16[1024,768]{1,0:T(8,128)(2,1)}, bf16[1024,768]{1,0:T(8,128)(2,1)}, bf16[1024,768]{1,0:T(8,128)(2,1)}) custom-call(s32[9]{0:T(128)} %pad_add_fusion.s, bf16[1024,768]{1,0:T(8,128)(2,1)} %left_ref.3, f32[8,768]{1,0:T(8,128)} %reshape.76.vec_ref, bf16[96,768]{1,0:T(8,128)(2,1)} %refs_0_.11, bf16[96,768]{1,0:T(8,128)(2,1)} %refs_1_.7, ...), custom_call_target="tpu_custom_call" | custom-call | flops 3623878656 | bytes 9854976 | tf_op jit(solution)/shard_map/project/pallas_call | solution.py:332
  111.7 3.1 collective-permute-done.36.refs_9_
  116.9 23.1 %attend.1 = (bf16[1024,768]{1,0:T(8,128)(2,1)}, bf16[8,6,256,640]{3,2,1,0:T(8,128)(2,1)}) custom-call(s32[16]{0:T(128)} %pad_add_fusion.1.win, s32[1,1024]{1,0:T(1,128)} %seq_ref.1, s32[1,1024]{1,0:T(1,128)} %mask_ref.1, bf16[1024,768]{1,0:T(8,128)(2,1)} %get-tuple-element.49.q_ref, bf16[1024,768]{1,0:T(8,128)(2,1)} %get-tuple-element.50.k_ref, ...), custom_call_target="tpu_custom_call" | custom-call | flops 14000000000 | bytes 20000000 | tf_op jit(solution)/shard_map/attend/pallas_call | solution.py:142
  142.0 25.3 %inner_block.1 = (f32[1024,768]{1,0:T(8,128)}, bf16[1024,768]{1,0:T(8,128)(2,1)}, bf16[1024,3072]{1,0:T(8,128)(2,1)}, bf16[1024,3072]{1,0:T(8,128)(2,1)}) custom-call(s32[9]{0:T(128)} %pad_add_fusion.s, bf16[1024,768]{1,0:T(8,128)(2,1)} %get-tuple-element.52.ctx_ref.left_ref, bf16[1024,768]{1,0:T(8,128)(2,1)} %left_ref.3, f32[8,768]{1,0:T(8,128)} %reshape.76.vec_ref, ...), custom_call_target="tpu_custom_call" | custom-call | flops 6039797760 | bytes 26468352 | tf_op jit(solution)/shard_map/inner_block/pallas_call | solution.py:332
  168.4 14.7 %outer_block.1 = (bf16[1024,768]{1,0:T(8,128)(2,1)}, f32[1024,768]{1,0:T(8,128)}, bf16[1024,768]{1,0:T(8,128)(2,1)}, f32[8,768]{1,0:T(8,128)}) custom-call(s32[9]{0:T(128)} %pad_add_fusion.s, bf16[1024,3072]{1,0:T(8,128)(2,1)} %get-tuple-element.53.act_ref.left_ref, f32[1024,768]{1,0:T(8,128)} %get-tuple-element.54.hid_ref, bf16[1024,768]{1,0:T(8,128)(2,1)} %g_ref.1, ...), custom_call_target="tpu_custom_call" | custom-call | flops 4831838208 | bytes 22069248 | tf_op jit(solution)/shard_map/outer_block/pallas_call | solution.py:332
  183.1 9.7 %weight_grad.7 = bf16[3072,384]{1,0:T(8,128)(2,1)} custom-call(s32[3]{0:T(128)} %pad_add_fusion.2.s, bf16[1024,3072]{1,0:T(8,128)(2,1)} %get-tuple-element.53.act_ref.left_ref, bf16[1024,768]{1,0:T(8,128)(2,1)} %get-tuple-element.56.g_ref.refs_0_), custom_call_target="tpu_custom_call" | custom-call | flops 2415919104 | bytes 10223616 | tf_op jit(solution)/shard_map/weight_grad/pallas_call | solution.py:332
  193.2 12.8 %active_back.1 = (bf16[1024,3072]{1,0:T(8,128)(2,1)}, f32[8,3072]{1,0:T(8,128)}) custom-call(s32[9]{0:T(128)} %pad_add_fusion.s, bf16[1024,768]{1,0:T(8,128)(2,1)} %get-tuple-element.56.g_ref.refs_0_, bf16[1024,3072]{1,0:T(8,128)(2,1)} %get-tuple-element.57.slope_ref, bf16[384,768]{1,0:T(8,128)(2,1)} %refs_0_.9, bf16[192,768]{1,0:T(8,128)(2,1)} %copy-done.31, ...), custom_call_target="tpu_custom_call" | custom-call | flops 4831838208 | bytes 18972672 | tf_op jit(solution)/shard_map/active_back/pallas_call | solution.py:332
  206.0 17.1 %inner_back.1 = (f32[1024,768]{1,0:T(8,128)}, bf16[1024,768]{1,0:T(8,128)(2,1)}, bf16[1024,768]{1,0:T(8,128)(2,1)}, f32[8,768]{1,0:T(8,128)}) custom-call(s32[9]{0:T(128)} %pad_add_fusion.s, bf16[1024,3072]{1,0:T(8,128)(2,1)} %get-tuple-element.58.g_ref.refs_0_, f32[1024,768]{1,0:T(8,128)} %get-tuple-element.59.second_ref, ...), custom_call_target="tpu_custom_call" | custom-call | flops 6039797760 | bytes 24821760 | tf_op jit(solution)/shard_map/inner_back/pallas_call | solution.py:332
  223.1 4.0 weight_grad.5
  227.2 21.3 %attend_back.1 = (bf16[1024,768]{1,0:T(8,128)(2,1)}, bf16[1024,768]{1,0:T(8,128)(2,1)}, bf16[1024,768]{1,0:T(8,128)(2,1)}, f32[8,768]{1,0:T(8,128)}, f32[8,768]{1,0:T(8,128)}) custom-call(s32[16]{0:T(128)} %pad_add_fusion.1.win, bf16[1024,768]{1,0:T(8,128)(2,1)} %get-tuple-element.49.q_ref, bf16[1024,768]{1,0:T(8,128)(2,1)} %get-tuple-element.50.k_ref, ...), custom_call_target="tpu_custom_call" | custom-call | flops 20000000000 | bytes 20000000 | tf_op jit(solution)/shard_map/attend_back/pallas_call | solution.py:211
  248.6 6.0 %weight_grad.4 = bf16[768,1152]{1,0:T(8,128)(2,1)} custom-call(s32[3]{0:T(128)} %pad_add_fusion.2.s, bf16[1024,768]{1,0:T(8,128)(2,1)} %left_ref.3, bf16[1024,768]{1,0:T(8,128)(2,1)} %get-tuple-element.63.q_ref.refs_0_, bf16[1024,768]{1,0:T(8,128)(2,1)} %get-tuple-element.64.k_ref.refs_1_, bf16[1024,768]{1,0:T(8,128)(2,1)} %get-tuple-element.65.v_ref.refs_2_), custom_call_target="tpu_custom_call" | custom-call | flops 1811939328 | bytes 8060928 | tf_op jit(solution)/shard_map/weight_grad/pallas_call | solution.py:332
  269.1 6.7 %weight_grad.6 = bf16[768,1536]{1,0:T(8,128)(2,1)} custom-call(s32[3]{0:T(128)} %pad_add_fusion.2.s, bf16[1024,768]{1,0:T(8,128)(2,1)} %get-tuple-element.76.left_ref, bf16[1024,3072]{1,0:T(8,128)(2,1)} %get-tuple-element.58.g_ref.refs_0_), custom_call_target="tpu_custom_call" | custom-call | flops 2415919104 | bytes 10223616 | tf_op jit(solution)/shard_map/weight_grad/pallas_call | solution.py:332
  276.6 4.1 weight_grad_sum.5
  281.3 10.5 %tokens_back.1 = bf16[1024,768]{1,0:T(8,128)(2,1)} custom-call(s32[9]{0:T(128)} %pad_add_fusion.s, f32[1024,768]{1,0:T(8,128)} %get-tuple-element.60.hid_ref, bf16[1024,768]{1,0:T(8,128)(2,1)} %get-tuple-element.63.q_ref.refs_0_, bf16[1024,768]{1,0:T(8,128)(2,1)} %get-tuple-element.64.k_ref.refs_1_, bf16[1024,768]{1,0:T(8,128)(2,1)} %get-tuple-element.65.v_ref.refs_2_, ...), custom_call_target="tpu_custom_call" | custom-call | flops 3623878656 | bytes 12976128 | tf_op jit(solution)/shard_map/tokens_back/pallas_call | solution.py:332
  292.7 6.2 %weight_grad_sum.4 = (bf16[384,1152]{1,0:T(8,128)(2,1)}, bf16[384,1152]{1,0:T(8,128)(2,1)}) custom-call(s32[3]{0:T(128)} %pad_add_fusion.2.s, bf16[1024,768]{1,0:T(8,128)(2,1)} %left_ref.3, bf16[1024,768]{1,0:T(8,128)(2,1)} %get-tuple-element.63.q_ref.refs_0_, bf16[1024,768]{1,0:T(8,128)(2,1)} %get-tuple-element.64.k_ref.refs_1_, ...), custom_call_target="tpu_custom_call" | custom-call | flops 1811939328 | bytes 9830400 | tf_op jit(solution)/shard_map/weight_grad_sum/pallas_call | solution.py:332
  301.6 2.3 collective-permute-start.55
  303.8 2.0 collective-permute-start.56
  307.1 47.2 %psum.7 = f32[9216]{0:T(1024)S(1)} all-reduce(f32[9216]{0:T(1024)} %constant_dynamic-update-slice_fusion.1), channel_id=1, replica_groups=mesh['fsdp'=8,'rep'=4] {'fsdp','rep'}, use_global_device_ids=true, to_apply=%region_2.3 | all-reduce | flops 9216 | bytes 73728 | tf_op jit(solution)/shard_map/psum | solution.py:808
  357.1 2.1 collective-permute-start.58
  367.5 10.1 %weight_grad_sum.7 = (bf16[1536,384]{1,0:T(8,128)(2,1)}, bf16[1536,384]{1,0:T(8,128)(2,1)}) custom-call(s32[3]{0:T(128)} %pad_add_fusion.2.s, bf16[1024,3072]{1,0:T(8,128)(2,1)} %get-tuple-element.53.act_ref.left_ref, bf16[1024,768]{1,0:T(8,128)(2,1)} %get-tuple-element.56.g_ref.refs_0_, bf16[3072,384]{1,0:T(8,128)(2,1)} %copy-done), custom_call_target="tpu_custom_call" | custom-call | flops 2415919104 | bytes 12582912 | tf_op jit(solution)/shard_map/weight_grad_sum/pallas_call | solution.py:332
  382.1 2.0 collective-permute-start.47
  384.1 7.1 %weight_grad_sum.6 = (bf16[384,1536]{1,0:T(8,128)(2,1)}, bf16[384,1536]{1,0:T(8,128)(2,1)}) custom-call(s32[3]{0:T(128)} %pad_add_fusion.2.s, bf16[1024,768]{1,0:T(8,128)(2,1)} %get-tuple-element.76.left_ref, bf16[1024,3072]{1,0:T(8,128)(2,1)} %get-tuple-element.58.g_ref.refs_0_, bf16[768,1536]{1,0:T(8,128)(2,1)} %collective-permute-done.60.refs_1_), custom_call_target="tpu_custom_call" | custom-call | flops 2415919104 | bytes 12582912 | tf_op jit(solution)/shard_map/weight_grad_sum/pallas_call | solution.py:332
  391.6 1.8 collective-permute-start.49
  393.6 15.5 %collective-permute-done.49 = bf16[48,1152]{1,0:T(8,128)(2,1)S(1)} collective-permute-done((bf16[48,1152]{1,0:T(8,128)(2,1)S(1)}, bf16[48,1152]{1,0:T(8,128)(2,1)S(1)}, u32[]{:S(2)}, u32[]{:S(2)}) %collective-permute-start.49) | collective-permute-done | bytes 110624 | tf_op jit(solution)/shard_map/ppermute | solution.py:327
  412.1 6.2 %collective-permute-done.61 = bf16[384,1536]{1,0:T(8,128)(2,1)S(1)} collective-permute-done((bf16[384,1536]{1,0:T(8,128)(2,1)}, bf16[384,1536]{1,0:T(8,128)(2,1)S(1)}, u32[]{:S(2)}, u32[]{:S(2)}) %collective-permute-start.61) | collective-permute-done | bytes 1179680 | tf_op jit(solution)/shard_map/ppermute | solution.py:650
  421.1 10.9 %collective-permute-done.62 = bf16[4,48,1536]{2,1,0:T(8,128)(2,1)S(1)} collective-permute-done((bf16[4,48,1536]{2,1,0:T(8,128)(2,1)S(1)}, bf16[4,48,1536]{2,1,0:T(8,128)(2,1)S(1)}, u32[]{:S(2)}, u32[]{:S(2)}) %collective-permute-start.62) | collective-permute-done | bytes 589856 | tf_op jit(solution)/shard_map/ppermute | solution.py:327
  434.2 2.7 collective-permute-start.65
  438.4 2.6 collective-permute-done.63
  441.0 2.0 collective-permute-start.74
  443.0 4.1 collective-permute-done.64
  447.3 2.5 collective-permute-done.72
  449.8 6.8 %collective-permute-done.73 = bf16[192,384]{1,0:T(8,128)(2,1)S(1)} collective-permute-done((bf16[192,384]{1,0:T(8,128)(2,1)S(1)}, bf16[192,384]{1,0:T(8,128)(2,1)S(1)}, u32[]{:S(2)}, u32[]{:S(2)}) %collective-permute-start.73) | collective-permute-done | bytes 147488 | tf_op jit(solution)/shard_map/ppermute | solution.py:688
  460.5 3.0 collective-permute-done.76
  463.4 2.3 collective-permute-done.77
  466.9 2.8 collective-permute-done.67
  469.8 2.3 collective-permute-done.68
  (313 shorter events, 77.9 us)
Async XLA Ops:
  9.0 48.2 %collective-permute-start.14 = (bf16[240,768]{1,0:T(8,128)(2,1)S(1)}, bf16[240,768]{1,0:T(8,128)(2,1)S(1)}, u32[]{:S(2)}, u32[]{:S(2)}) collective-permute-start(bf16[240,768]{1,0:T(8,128)(2,1)S(1)} %dynamic-slice_dynamic-update-slice_fusion), channel_id=1, source_target_pairs={{0,8},{8,16},{16,24},{24,28},{28,20},{20,12},{12,4},{4,0},{1,9},{9... | collective-permute-start | bytes 1105928 | tf_op jit(solution)/shard_map/ppermute | solution.py:323
  10.6 47.0 %collective-permute-start.16 = (bf16[240,768]{1,0:T(8,128)(2,1)S(1)}, bf16[240,768]{1,0:T(8,128)(2,1)S(1)}, u32[]{:S(2)}, u32[]{:S(2)}) collective-permute-start(bf16[240,768]{1,0:T(8,128)(2,1)S(1)} %dynamic-slice_dynamic-update-slice_fusion), channel_id=1, source_target_pairs={{0,4},{8,0},{16,8},{24,16},{28,24},{20,28},{12,20},{4,12},{1,5},{9... | collective-permute-start | bytes 1105928 | tf_op jit(solution)/shard_map/ppermute | solution.py:323
  12.0 45.0 %collective-permute-start.30 = (bf16[192,768]{1,0:T(8,128)(2,1)S(1)}, bf16[192,768]{1,0:T(8,128)(2,1)S(1)}, u32[]{:S(2)}, u32[]{:S(2)}) collective-permute-start(bf16[192,768]{1,0:T(8,128)(2,1)S(1)} %constant_dynamic-slice_fusion), channel_id=1, source_target_pairs={{0,4},{8,0},{16,8},{24,16},{28,24},{20,28},{12,20},{4,12},{1,5},{9... | collective-permute-start | bytes 884744 | tf_op jit(solution)/shard_map/ppermute | solution.py:323
  14.1 43.6 %collective-permute-start.4 = (bf16[144,768]{1,0:T(8,128)(2,1)S(1)}, bf16[144,768]{1,0:T(8,128)(2,1)S(1)}, u32[]{:S(2)}, u32[]{:S(2)}) collective-permute-start(bf16[144,768]{1,0:T(8,128)(2,1)S(1)} %collective-permute-done.refs_3_), channel_id=1, source_target_pairs={{0,8},{8,16},{16,24},{24,28},{28,20},{20,12},{12,4},{4,0},{1,9},{9... | collective-permute-start | bytes 663560 | tf_op jit(solution)/shard_map/ppermute | solution.py:323
  18.4 40.1 %collective-permute-start.6 = (bf16[144,768]{1,0:T(8,128)(2,1)S(1)}, bf16[144,768]{1,0:T(8,128)(2,1)S(1)}, u32[]{:S(2)}, u32[]{:S(2)}) collective-permute-start(bf16[144,768]{1,0:T(8,128)(2,1)S(1)} %collective-permute-done.2.refs_5_), channel_id=1, source_target_pairs={{0,4},{8,0},{16,8},{24,16},{28,24},{20,28},{12,20},{4,12},{1,5},{9... | collective-permute-start | bytes 663560 | tf_op jit(solution)/shard_map/ppermute | solution.py:323
  60.6 19.5 %collective-permute-start.18 = (bf16[240,768]{1,0:T(8,128)(2,1)S(1)}, bf16[240,768]{1,0:T(8,128)(2,1)S(1)}, u32[]{:S(2)}, u32[]{:S(2)}) collective-permute-start(bf16[240,768]{1,0:T(8,128)(2,1)S(1)} %collective-permute-done.14.refs_2_), channel_id=1, source_target_pairs={{0,8},{8,16},{16,24},{24,28},{28,20},{20,12},{12,4},{4,0},{1,9},{9... | collective-permute-start | bytes 1105928 | tf_op jit(solution)/shard_map/ppermute | solution.py:323
  69.9 13.7 %collective-permute-start.20 = (bf16[240,768]{1,0:T(8,128)(2,1)S(1)}, bf16[240,768]{1,0:T(8,128)(2,1)S(1)}, u32[]{:S(2)}, u32[]{:S(2)}) collective-permute-start(bf16[240,768]{1,0:T(8,128)(2,1)S(1)} %collective-permute-done.16.refs_4_), channel_id=1, source_target_pairs={{0,4},{8,0},{16,8},{24,16},{28,24},{20,28},{12,20},{4,12},{1,5},{9... | collective-permute-start | bytes 1105928 | tf_op jit(solution)/shard_map/ppermute | solution.py:323
  79.5 17.0 %collective-permute-start.17 = (bf16[240,768]{1,0:T(8,128)(2,1)S(1)}, bf16[240,768]{1,0:T(8,128)(2,1)S(1)}, u32[]{:S(2)}, u32[]{:S(2)}) collective-permute-start(bf16[240,768]{1,0:T(8,128)(2,1)S(1)} %collective-permute-done.16.refs_4_), channel_id=1, source_target_pairs={{0,1},{1,0},{2,3},{3,2},{4,5},{5,4},{6,7},{7,6},{8,9},{9,8},{10,11... | collective-permute-start | bytes 1105928 | tf_op jit(solution)/shard_map/ppermute | solution.py:327
  80.1 17.1 %collective-permute-start.22 = (bf16[240,768]{1,0:T(8,128)(2,1)S(1)}, bf16[240,768]{1,0:T(8,128)(2,1)S(1)}, u32[]{:S(2)}, u32[]{:S(2)}) collective-permute-start(bf16[240,768]{1,0:T(8,128)(2,1)S(1)} %collective-permute-done.18.refs_6_), channel_id=1, source_target_pairs={{0,8},{8,16},{16,24},{24,28},{28,20},{20,12},{12,4},{4,0},{1,9},{9... | collective-permute-start | bytes 1105928 | tf_op jit(solution)/shard_map/ppermute | solution.py:323
  82.1 13.8 %collective-permute-start.12 = (bf16[144,768]{1,0:T(8,128)(2,1)}, bf16[144,768]{1,0:T(8,128)(2,1)}, u32[]{:S(2)}, u32[]{:S(2)}) collective-permute-start(bf16[144,768]{1,0:T(8,128)(2,1)} %collective-permute-done.8.refs_11_), channel_id=1, source_target_pairs={{0,8},{8,16},{16,24},{24,28},{28,20},{20,12},{12,4},{4,0},{1,9},{9... | collective-permute-start | bytes 663560 | tf_op jit(solution)/shard_map/ppermute | solution.py:323
  83.6 13.5 %collective-permute-start.11 = (bf16[144,768]{1,0:T(8,128)(2,1)}, bf16[144,768]{1,0:T(8,128)(2,1)S(1)}, u32[]{:S(2)}, u32[]{:S(2)}) collective-permute-start(bf16[144,768]{1,0:T(8,128)(2,1)} %collective-permute-done.10.refs_13_), channel_id=1, source_target_pairs={{0,1},{1,0},{2,3},{3,2},{4,5},{5,4},{6,7},{7,6},{8,9},{9,8},{10,11... | collective-permute-start | bytes 663560 | tf_op jit(solution)/shard_map/ppermute | solution.py:327
  84.2 16.4 %collective-permute-start.9 = (bf16[144,768]{1,0:T(8,128)(2,1)}, bf16[144,768]{1,0:T(8,128)(2,1)}, u32[]{:S(2)}, u32[]{:S(2)}) collective-permute-start(bf16[144,768]{1,0:T(8,128)(2,1)} %collective-permute-done.8.refs_11_), channel_id=1, source_target_pairs={{0,1},{1,0},{2,3},{3,2},{4,5},{5,4},{6,7},{7,6},{8,9},{9,8},{10,11... | collective-permute-start | bytes 663560 | tf_op jit(solution)/shard_map/ppermute | solution.py:327
  96.5 19.9 %collective-permute-start.19 = (bf16[240,768]{1,0:T(8,128)(2,1)S(1)}, bf16[240,768]{1,0:T(8,128)(2,1)S(1)}, u32[]{:S(2)}, u32[]{:S(2)}) collective-permute-start(bf16[240,768]{1,0:T(8,128)(2,1)S(1)} %collective-permute-done.18.refs_6_), channel_id=1, source_target_pairs={{0,1},{1,0},{2,3},{3,2},{4,5},{5,4},{6,7},{7,6},{8,9},{9,8},{10,11... | collective-permute-start | bytes 1105928 | tf_op jit(solution)/shard_map/ppermute | solution.py:327
  97.1 19.1 %collective-permute-start.24 = (bf16[240,768]{1,0:T(8,128)(2,1)S(1)}, bf16[240,768]{1,0:T(8,128)(2,1)S(1)}, u32[]{:S(2)}, u32[]{:S(2)}) collective-permute-start(bf16[240,768]{1,0:T(8,128)(2,1)S(1)} %collective-permute-done.20.refs_8_), channel_id=1, source_target_pairs={{0,4},{8,0},{16,8},{24,16},{28,24},{20,28},{12,20},{4,12},{1,5},{9... | collective-permute-start | bytes 1105928 | tf_op jit(solution)/shard_map/ppermute | solution.py:323
  97.8 19.0 %collective-permute-start.26 = (bf16[240,768]{1,0:T(8,128)(2,1)S(1)}, bf16[240,768]{1,0:T(8,128)(2,1)}, u32[]{:S(2)}, u32[]{:S(2)}) collective-permute-start(bf16[240,768]{1,0:T(8,128)(2,1)S(1)} %collective-permute-done.22.refs_10_), channel_id=1, source_target_pairs={{0,8},{8,16},{16,24},{24,28},{28,20},{20,12},{12,4},{4,0},{1,9},{9... | collective-permute-start | bytes 1105928 | tf_op jit(solution)/shard_map/ppermute | solution.py:323
  100.6 14.1 %collective-permute-start.36 = (bf16[192,768]{1,0:T(8,128)(2,1)}, bf16[192,768]{1,0:T(8,128)(2,1)}, u32[]{:S(2)}, u32[]{:S(2)}) collective-permute-start(bf16[192,768]{1,0:T(8,128)(2,1)} %copy-done.33), channel_id=1, source_target_pairs={{0,8},{8,16},{16,24},{24,28},{28,20},{20,12},{12,4},{4,0},{1,9},{9... | collective-permute-start | bytes 884744 | tf_op jit(solution)/shard_map/ppermute | solution.py:323
  100.9 13.8 %collective-permute-start.38 = (bf16[192,768]{1,0:T(8,128)(2,1)}, bf16[192,768]{1,0:T(8,128)(2,1)}, u32[]{:S(2)}, u32[]{:S(2)}) collective-permute-start(bf16[192,768]{1,0:T(8,128)(2,1)} %copy-done.36), channel_id=1, source_target_pairs={{0,4},{8,0},{16,8},{24,16},{28,24},{20,28},{12,20},{4,12},{1,5},{9... | collective-permute-start | bytes 884744 | tf_op jit(solution)/shard_map/ppermute | solution.py:323
  114.8 25.3 %collective-permute-start.21 = (bf16[240,768]{1,0:T(8,128)(2,1)S(1)}, bf16[240,768]{1,0:T(8,128)(2,1)S(1)}, u32[]{:S(2)}, u32[]{:S(2)}) collective-permute-start(bf16[240,768]{1,0:T(8,128)(2,1)S(1)} %collective-permute-done.20.refs_8_), channel_id=1, source_target_pairs={{0,1},{1,0},{2,3},{3,2},{4,5},{5,4},{6,7},{7,6},{8,9},{9,8},{10,11... | collective-permute-start | bytes 1105928 | tf_op jit(solution)/shard_map/ppermute | solution.py:327
  114.8 25.4 %collective-permute-start.40 = (bf16[192,768]{1,0:T(8,128)(2,1)}, bf16[192,768]{1,0:T(8,128)(2,1)}, u32[]{:S(2)}, u32[]{:S(2)}) collective-permute-start(bf16[192,768]{1,0:T(8,128)(2,1)} %collective-permute-done.36.refs_9_), channel_id=1, source_target_pairs={{0,8},{8,16},{16,24},{24,28},{28,20},{20,12},{12,4},{4,0},{1,9},{9... | collective-permute-start | bytes 884744 | tf_op jit(solution)/shard_map/ppermute | solution.py:323
  116.2 24.5 %collective-permute-start.23 = (bf16[240,768]{1,0:T(8,128)(2,1)S(1)}, bf16[240,768]{1,0:T(8,128)(2,1)S(1)}, u32[]{:S(2)}, u32[]{:S(2)}) collective-permute-start(bf16[240,768]{1,0:T(8,128)(2,1)S(1)} %collective-permute-done.22.refs_10_), channel_id=1, source_target_pairs={{0,1},{1,0},{2,3},{3,2},{4,5},{5,4},{6,7},{7,6},{8,9},{9,8},{10,11... | collective-permute-start | bytes 1105928 | tf_op jit(solution)/shard_map/ppermute | solution.py:327
  116.4 24.4 %collective-permute-start.25 = (bf16[240,768]{1,0:T(8,128)(2,1)S(1)}, bf16[240,768]{1,0:T(8,128)(2,1)S(1)}, u32[]{:S(2)}, u32[]{:S(2)}) collective-permute-start(bf16[240,768]{1,0:T(8,128)(2,1)S(1)} %collective-permute-done.24.refs_12_), channel_id=1, source_target_pairs={{0,1},{1,0},{2,3},{3,2},{4,5},{5,4},{6,7},{7,6},{8,9},{9,8},{10,11... | collective-permute-start | bytes 1105928 | tf_op jit(solution)/shard_map/ppermute | solution.py:327
  116.7 24.5 %collective-permute-start.27 = (bf16[240,768]{1,0:T(8,128)(2,1)}, bf16[240,768]{1,0:T(8,128)(2,1)S(1)}, u32[]{:S(2)}, u32[]{:S(2)}) collective-permute-start(bf16[240,768]{1,0:T(8,128)(2,1)} %collective-permute-done.26.refs_14_), channel_id=1, source_target_pairs={{0,1},{1,0},{2,3},{3,2},{4,5},{5,4},{6,7},{7,6},{8,9},{9,8},{10,11... | collective-permute-start | bytes 1105928 | tf_op jit(solution)/shard_map/ppermute | solution.py:327
  140.1 27.2 %collective-permute-start.33 = (bf16[192,768]{1,0:T(8,128)(2,1)S(1)}, bf16[192,768]{1,0:T(8,128)(2,1)S(1)}, u32[]{:S(2)}, u32[]{:S(2)}) collective-permute-start(bf16[192,768]{1,0:T(8,128)(2,1)S(1)} %copy-done.34), channel_id=1, source_target_pairs={{0,1},{1,0},{2,3},{3,2},{4,5},{5,4},{6,7},{7,6},{8,9},{9,8},{10,11... | collective-permute-start | bytes 884744 | tf_op jit(solution)/shard_map/ppermute | solution.py:327
  140.2 27.2 %collective-permute-start.35 = (bf16[192,768]{1,0:T(8,128)(2,1)S(1)}, bf16[192,768]{1,0:T(8,128)(2,1)S(1)}, u32[]{:S(2)}, u32[]{:S(2)}) collective-permute-start(bf16[192,768]{1,0:T(8,128)(2,1)S(1)} %copy-done.37), channel_id=1, source_target_pairs={{0,1},{1,0},{2,3},{3,2},{4,5},{5,4},{6,7},{7,6},{8,9},{9,8},{10,11... | collective-permute-start | bytes 884744 | tf_op jit(solution)/shard_map/ppermute | solution.py:327
  140.7 26.7 %collective-permute-start.37 = (bf16[192,768]{1,0:T(8,128)(2,1)}, bf16[192,768]{1,0:T(8,128)(2,1)S(1)}, u32[]{:S(2)}, u32[]{:S(2)}) collective-permute-start(bf16[192,768]{1,0:T(8,128)(2,1)} %collective-permute-done.36.refs_9_), channel_id=1, source_target_pairs={{0,1},{1,0},{2,3},{3,2},{4,5},{5,4},{6,7},{7,6},{8,9},{9,8},{10,11... | collective-permute-start | bytes 884744 | tf_op jit(solution)/shard_map/ppermute | solution.py:327
  140.8 26.6 %collective-permute-start.39 = (bf16[192,768]{1,0:T(8,128)(2,1)}, bf16[192,768]{1,0:T(8,128)(2,1)S(1)}, u32[]{:S(2)}, u32[]{:S(2)}) collective-permute-start(bf16[192,768]{1,0:T(8,128)(2,1)} %collective-permute-done.38.refs_11_), channel_id=1, source_target_pairs={{0,1},{1,0},{2,3},{3,2},{4,5},{5,4},{6,7},{7,6},{8,9},{9,8},{10,11... | collective-permute-start | bytes 884744 | tf_op jit(solution)/shard_map/ppermute | solution.py:327
  141.2 26.2 %collective-permute-start.41 = (bf16[192,768]{1,0:T(8,128)(2,1)}, bf16[192,768]{1,0:T(8,128)(2,1)}, u32[]{:S(2)}, u32[]{:S(2)}) collective-permute-start(bf16[192,768]{1,0:T(8,128)(2,1)} %collective-permute-done.40.refs_13_), channel_id=1, source_target_pairs={{0,1},{1,0},{2,3},{3,2},{4,5},{5,4},{6,7},{7,6},{8,9},{9,8},{10,11... | collective-permute-start | bytes 884744 | tf_op jit(solution)/shard_map/ppermute | solution.py:327
  192.9 173.3 %collective-permute-start.69 = (bf16[3072,384]{1,0:T(8,128)(2,1)}, bf16[3072,384]{1,0:T(8,128)(2,1)S(1)}, u32[]{:S(2)}, u32[]{:S(2)}) collective-permute-start(bf16[3072,384]{1,0:T(8,128)(2,1)} %weight_grad.7), channel_id=1, source_target_pairs={{0,1},{1,0},{2,3},{3,2},{4,5},{5,4},{6,7},{7,6},{8,9},{9,8},{10,11... | collective-permute-start | bytes 7077896 | tf_op jit(solution)/shard_map/ppermute | solution.py:327
  227.1 48.7 %collective-permute-start.51 = (bf16[768,384]{1,0:T(8,128)(2,1)}, bf16[768,384]{1,0:T(8,128)(2,1)S(1)}, u32[]{:S(2)}, u32[]{:S(2)}) collective-permute-start(bf16[768,384]{1,0:T(8,128)(2,1)} %weight_grad.5), channel_id=1, source_target_pairs={{0,1},{1,0},{2,3},{3,2},{4,5},{5,4},{6,7},{7,6},{8,9},{9,8},{10,11... | collective-permute-start | bytes 1769480 | tf_op jit(solution)/shard_map/ppermute | solution.py:327
  254.5 38.1 %collective-permute-start.42 = (bf16[768,1152]{1,0:T(8,128)(2,1)}, bf16[768,1152]{1,0:T(8,128)(2,1)}, u32[]{:S(2)}, u32[]{:S(2)}) collective-permute-start(bf16[768,1152]{1,0:T(8,128)(2,1)} %weight_grad.4), channel_id=1, source_target_pairs={{0,1},{1,0},{2,3},{3,2},{4,5},{5,4},{6,7},{7,6},{8,9},{9,8},{10,11... | collective-permute-start | bytes 5308424 | tf_op jit(solution)/shard_map/ppermute | solution.py:327
  298.9 62.1 %collective-permute-start.43 = (bf16[384,1152]{1,0:T(8,128)(2,1)}, bf16[384,1152]{1,0:T(8,128)(2,1)S(1)}, u32[]{:S(2)}, u32[]{:S(2)}) collective-permute-start(bf16[384,1152]{1,0:T(8,128)(2,1)} %get-tuple-element.67), channel_id=1, source_target_pairs={{0,2},{1,3},{2,0},{3,1},{4,6},{5,7},{6,4},{7,5},{8,10},{9,11},{10,... | collective-permute-start | bytes 2654216 | tf_op jit(solution)/shard_map/ppermute | solution.py:327
  300.3 54.1 %collective-permute-start.54 = (bf16[48,384]{1,0:T(8,128)(2,1)S(1)}, bf16[48,384]{1,0:T(8,128)(2,1)}, u32[]{:S(2)}, u32[]{:S(2)}) collective-permute-start(bf16[48,384]{1,0:T(8,128)(2,1)S(1)} %get-tuple-element.100), channel_id=1, source_target_pairs={{0,8},{4,12},{8,16},{12,20},{16,24},{20,28},{24,0},{28,4},{1,9},{5... | collective-permute-start | bytes 110600 | tf_op jit(solution)/shard_map/ppermute | solution.py:688
  301.6 52.9 %collective-permute-start.55 = (bf16[48,384]{1,0:T(8,128)(2,1)S(1)}, bf16[48,384]{1,0:T(8,128)(2,1)}, u32[]{:S(2)}, u32[]{:S(2)}) collective-permute-start(bf16[48,384]{1,0:T(8,128)(2,1)S(1)} %get-tuple-element.102), channel_id=1, source_target_pairs={{0,16},{4,20},{8,24},{12,28},{16,0},{20,4},{24,8},{28,12},{1,17},{... | collective-permute-start | bytes 110600 | tf_op jit(solution)/shard_map/ppermute | solution.py:688
  303.8 50.6 %collective-permute-start.56 = (bf16[48,384]{1,0:T(8,128)(2,1)S(1)}, bf16[48,384]{1,0:T(8,128)(2,1)}, u32[]{:S(2)}, u32[]{:S(2)}) collective-permute-start(bf16[48,384]{1,0:T(8,128)(2,1)S(1)} %get-tuple-element.101), channel_id=1, source_target_pairs={{0,24},{4,28},{8,0},{12,4},{16,8},{20,12},{24,16},{28,20},{1,25},{... | collective-permute-start | bytes 110600 | tf_op jit(solution)/shard_map/ppermute | solution.py:688
  354.4 29.8 %collective-permute-start.60 = (bf16[768,1536]{1,0:T(8,128)(2,1)}, bf16[768,1536]{1,0:T(8,128)(2,1)}, u32[]{:S(2)}, u32[]{:S(2)}) collective-permute-start(bf16[768,1536]{1,0:T(8,128)(2,1)} %weight_grad.6), channel_id=1, source_target_pairs={{0,1},{1,0},{2,3},{3,2},{4,5},{5,4},{6,7},{7,6},{8,9},{9,8},{10,11... | collective-permute-start | bytes 7077896 | tf_op jit(solution)/shard_map/ppermute | solution.py:327
  364.3 14.5 %collective-permute-start.44 = (bf16[4,48,1152]{2,1,0:T(8,128)(2,1)}, bf16[4,48,1152]{2,1,0:T(8,128)(2,1)}, u32[]{:S(2)}, u32[]{:S(2)}) collective-permute-start(bf16[4,48,1152]{2,1,0:T(8,128)(2,1)} %dynamic-slice_bitcast_fusion.2), channel_id=1, source_target_pairs={{0,4},{4,0},{8,12},{12,8},{16,20},{20,16},{24,28},{28,24},{1,5},{5... | collective-permute-start | bytes 1327112 | tf_op jit(solution)/shard_map/ppermute | solution.py:650
  377.7 42.4 %collective-permute-start.70 = (bf16[1536,384]{1,0:T(8,128)(2,1)}, bf16[1536,384]{1,0:T(8,128)(2,1)S(1)}, u32[]{:S(2)}, u32[]{:S(2)}) collective-permute-start(bf16[1536,384]{1,0:T(8,128)(2,1)} %get-tuple-element.80), channel_id=1, source_target_pairs={{0,2},{1,3},{2,0},{3,1},{4,6},{5,7},{6,4},{7,5},{8,10},{9,11},{10,... | collective-permute-start | bytes 3538952 | tf_op jit(solution)/shard_map/ppermute | solution.py:327
  391.2 27.0 %collective-permute-start.61 = (bf16[384,1536]{1,0:T(8,128)(2,1)}, bf16[384,1536]{1,0:T(8,128)(2,1)S(1)}, u32[]{:S(2)}, u32[]{:S(2)}) collective-permute-start(bf16[384,1536]{1,0:T(8,128)(2,1)} %get-tuple-element.78), channel_id=1, source_target_pairs={{0,4},{4,0},{8,12},{12,8},{16,20},{20,16},{24,28},{28,24},{1,5},{5... | collective-permute-start | bytes 3538952 | tf_op jit(solution)/shard_map/ppermute | solution.py:650
  391.6 17.5 %collective-permute-start.49 = (bf16[48,1152]{1,0:T(8,128)(2,1)S(1)}, bf16[48,1152]{1,0:T(8,128)(2,1)S(1)}, u32[]{:S(2)}, u32[]{:S(2)}) collective-permute-start(bf16[48,1152]{1,0:T(8,128)(2,1)S(1)} %fusion.14), channel_id=1, source_target_pairs={{0,2},{1,3},{2,0},{3,1},{4,6},{5,7},{6,4},{7,5},{8,10},{9,11},{10,... | collective-permute-start | bytes 331784 | tf_op jit(solution)/shard_map/ppermute | solution.py:327
  393.4 16.4 %collective-permute-start.50 = (bf16[48,1152]{1,0:T(8,128)(2,1)S(1)}, bf16[48,1152]{1,0:T(8,128)(2,1)S(1)}, u32[]{:S(2)}, u32[]{:S(2)}) collective-permute-start(bf16[48,1152]{1,0:T(8,128)(2,1)S(1)} %fusion.14), channel_id=1, source_target_pairs={{0,3},{1,2},{2,1},{3,0},{4,7},{5,6},{6,5},{7,4},{8,11},{9,10},{10,... | collective-permute-start | bytes 331784 | tf_op jit(solution)/shard_map/ppermute | solution.py:327
  418.6 13.3 %collective-permute-start.62 = (bf16[4,48,1536]{2,1,0:T(8,128)(2,1)S(1)}, bf16[4,48,1536]{2,1,0:T(8,128)(2,1)S(1)}, u32[]{:S(2)}, u32[]{:S(2)}) collective-permute-start(bf16[4,48,1536]{2,1,0:T(8,128)(2,1)S(1)} %dynamic-slice_bitcast_fusion.1), channel_id=1, source_target_pairs={{0,2},{1,3},{2,0},{3,1},{4,6},{5,7},{6,4},{7,5},{8,10},{9,11},{10,... | collective-permute-start | bytes 1769480 | tf_op jit(solution)/shard_map/ppermute | solution.py:327
  420.6 16.3 %collective-permute-start.71 = (bf16[4,192,384]{2,1,0:T(8,128)(2,1)S(1)}, bf16[4,192,384]{2,1,0:T(8,128)(2,1)S(1)}, u32[]{:S(2)}, u32[]{:S(2)}) collective-permute-start(bf16[4,192,384]{2,1,0:T(8,128)(2,1)S(1)} %dynamic-slice_bitcast_fusion), channel_id=1, source_target_pairs={{0,4},{4,0},{8,12},{12,8},{16,20},{20,16},{24,28},{28,24},{1,5},{5... | collective-permute-start | bytes 1769480 | tf_op jit(solution)/shard_map/ppermute | solution.py:650
  433.0 14.0 %collective-permute-start.64 = (bf16[48,1536]{1,0:T(8,128)(2,1)S(1)}, bf16[48,1536]{1,0:T(8,128)(2,1)S(1)}, u32[]{:S(2)}, u32[]{:S(2)}) collective-permute-start(bf16[48,1536]{1,0:T(8,128)(2,1)S(1)} %get-tuple-element.96), channel_id=1, source_target_pairs={{0,16},{4,20},{8,24},{12,28},{16,0},{20,4},{24,8},{28,12},{1,17},{... | collective-permute-start | bytes 442376 | tf_op jit(solution)/shard_map/ppermute | solution.py:688
  434.2 12.9 %collective-permute-start.65 = (bf16[48,1536]{1,0:T(8,128)(2,1)S(1)}, bf16[48,1536]{1,0:T(8,128)(2,1)S(1)}, u32[]{:S(2)}, u32[]{:S(2)}) collective-permute-start(bf16[48,1536]{1,0:T(8,128)(2,1)S(1)} %get-tuple-element.95), channel_id=1, source_target_pairs={{0,24},{4,28},{8,0},{12,4},{16,8},{20,12},{24,16},{28,20},{1,25},{... | collective-permute-start | bytes 442376 | tf_op jit(solution)/shard_map/ppermute | solution.py:688
  437.1 12.7 %collective-permute-start.72 = (bf16[192,384]{1,0:T(8,128)(2,1)S(1)}, bf16[192,384]{1,0:T(8,128)(2,1)S(1)}, u32[]{:S(2)}, u32[]{:S(2)}) collective-permute-start(bf16[192,384]{1,0:T(8,128)(2,1)S(1)} %get-tuple-element.91), channel_id=1, source_target_pairs={{0,8},{4,12},{8,16},{12,20},{16,24},{20,28},{24,0},{28,4},{1,9},{5... | collective-permute-start | bytes 442376 | tf_op jit(solution)/shard_map/ppermute | solution.py:688
  437.2 19.4 %collective-permute-start.73 = (bf16[192,384]{1,0:T(8,128)(2,1)S(1)}, bf16[192,384]{1,0:T(8,128)(2,1)S(1)}, u32[]{:S(2)}, u32[]{:S(2)}) collective-permute-start(bf16[192,384]{1,0:T(8,128)(2,1)S(1)} %get-tuple-element.93), channel_id=1, source_target_pairs={{0,16},{4,20},{8,24},{12,28},{16,0},{20,4},{24,8},{28,12},{1,17},{... | collective-permute-start | bytes 442376 | tf_op jit(solution)/shard_map/ppermute | solution.py:688
  441.0 15.6 %collective-permute-start.74 = (bf16[192,384]{1,0:T(8,128)(2,1)S(1)}, bf16[192,384]{1,0:T(8,128)(2,1)S(1)}, u32[]{:S(2)}, u32[]{:S(2)}) collective-permute-start(bf16[192,384]{1,0:T(8,128)(2,1)S(1)} %get-tuple-element.92), channel_id=1, source_target_pairs={{0,24},{4,28},{8,0},{12,4},{16,8},{20,12},{24,16},{28,20},{1,25},{... | collective-permute-start | bytes 442376 | tf_op jit(solution)/shard_map/ppermute | solution.py:688
  459.5 12.5 %collective-permute-start.68 = (bf16[48,1536]{1,0:T(8,128)(2,1)S(1)}, bf16[48,1536]{1,0:T(8,128)(2,1)S(1)}, u32[]{:S(2)}, u32[]{:S(2)}) collective-permute-start(bf16[48,1536]{1,0:T(8,128)(2,1)S(1)} %fusion.10), channel_id=1, source_target_pairs={{0,3},{1,2},{2,1},{3,0},{4,7},{5,6},{6,5},{7,4},{8,11},{9,10},{10,... | collective-permute-start | bytes 442376 | tf_op jit(solution)/shard_map/ppermute | solution.py:327
  (80 other events, 1147.1 us)

commit v2 on v1

v2 whole, which is shorter than its diff:
```python
import functools
import math

import jax
import jax.numpy as jnp
from jax import lax
from jax.experimental import pallas as pl
from jax.experimental.pallas import tpu as pltpu
from jax.sharding import PartitionSpec as P

HEADS = 12
DH = 64
BF = jnp.bfloat16
F32 = jnp.float32
NEGATIVE = -1e30
EPSILON = 1e-12
QB = 128
KB = 128
SPAN = 5
ROWS = 1024
VMEM = 60 * 1024 * 1024
COST = 0.05
ANY = pl.BlockSpec(memory_space=pl.ANY)


def dot(left, right):
    return jnp.dot(left, right, preferred_element_type=F32)


def dot_right(left, right):
    return lax.dot_general(left, right, (((1,), (1,)), ((), ())), preferred_element_type=F32)


def params(steps=1):
    return pltpu.CompilerParams(
        dimension_semantics=("arbitrary",) * steps, vmem_limit_bytes=VMEM
    )


def cost(flops, size):
    return pl.CostEstimate(flops=int(flops * COST), bytes_accessed=int(size * COST), transcendentals=0)


def struct(shape, dtype):
    return jax.ShapeDtypeStruct(shape, dtype)


def whole(shape):
    return pl.BlockSpec(shape, lambda i, s: (0,) * len(shape))


def rows_of(width, height=ROWS):
    return pl.BlockSpec((height, width), lambda i, s: (i, 0))


def norm(hidden):
    center = hidden - jnp.mean(hidden, axis=-1, keepdims=True)
    inverse = lax.rsqrt(jnp.mean(center * center, axis=-1, keepdims=True) + EPSILON)
    return center * inverse, inverse


def norm_back(grad, normed, inverse):
    mean = jnp.mean(grad, axis=-1, keepdims=True)
    along = jnp.mean(grad * normed, axis=-1, keepdims=True)
    return inverse * (grad - mean - normed * along)


def gelu_parts(inner):
    phi = 0.5 + 0.5 * lax.erf(inner * 0.7071067811865476)
    density = jnp.exp((-0.5 * inner) * inner) * 0.3989422804014327
    return inner * phi, phi + inner * density


def column_sum(value):
    return jnp.sum(value, axis=0, keepdims=True)


def windows(seq_row):
    tiles = seq_row.reshape(seq_row.shape[0] // QB, QB)
    below = jnp.sum((seq_row[None] < tiles[:, :1]).astype(jnp.int32), axis=1)
    upto = jnp.sum((seq_row[None] <= tiles[:, -1:]).astype(jnp.int32), axis=1)
    low = below // KB
    return jnp.concatenate([low, (upto + KB - 1) // KB - low])


def first_half(shape):
    return lax.broadcasted_iota(jnp.int32, shape, len(shape) - 1) < DH


def stack_pair(pair):
    low = first_half(pair.shape)
    zero = jnp.zeros_like(pair)
    return jnp.concatenate([jnp.where(low, pair, zero), jnp.where(low, zero, pair)], axis=0)


def fold_pair(both):
    half = both.shape[0] // 2
    return jnp.where(first_half((half, both.shape[1])), both[:half], both[half:])


def attend_kernel(win, seq_ref, mask_ref, q_ref, k_ref, v_ref, ctx_ref, p_ref, bias_ref, s_ref):
    i = pl.program_id(0)
    low = win[i]
    count = win[pl.num_programs(0) + i]
    pairs = q_ref.shape[1] // (2 * DH)

    def body(n):
        w = n * KB
        base = pl.multiple_of(low * KB, KB)
        start = pl.multiple_of(i * QB, QB)
        for pair in range(pairs):
            lanes = slice(pair * 2 * DH, (pair + 1) * 2 * DH)
            s_ref[pair, :, :w] = dot_right(stack_pair(q_ref[:, lanes]), k_ref[pl.ds(base, w), lanes])
        own = jnp.broadcast_to(seq_ref[:, pl.ds(start, QB)], (QB, QB)).T
        rows = start + lax.broadcasted_iota(jnp.int32, (QB, KB), 0)
        for b in range(n):
            off = pl.multiple_of(base + b * KB, KB)
            cols = off + lax.broadcasted_iota(jnp.int32, (QB, KB), 1)
            visible = (mask_ref[:, pl.ds(off, KB)] == 1) | (rows == cols)
            allowed = (own == seq_ref[:, pl.ds(off, KB)]) & visible
            bias_ref[:, b * KB : (b + 1) * KB] = jnp.where(allowed, 0.0, NEGATIVE).astype(F32)
        ones = jnp.ones((w, 2 * DH), BF)
        for group in range(0, pairs, GROUP):
            expons = []
            for pair in range(group, group + GROUP):
                lanes = slice(pair * 2 * DH, (pair + 1) * 2 * DH)
                bias = bias_ref[:, :w]
                scores = s_ref[pair, :, :w] + jnp.concatenate([bias, bias], axis=0)
                expons.append(jnp.exp(scores - jnp.max(scores, axis=1, keepdims=True)).astype(BF))
            for pair in range(group, group + GROUP):
                lanes = slice(pair * 2 * DH, (pair + 1) * 2 * DH)
                expon = expons[pair - group]
                mixed = dot(expon, jnp.concatenate([v_ref[pl.ds(base, w), lanes], ones], axis=1))
                scale = 1.0 / mixed[:, 2 * DH :]
                ctx_ref[:, lanes] = fold_pair(mixed[:, : 2 * DH] * scale).astype(BF)
                for b in range(n):
                    p_ref[0, pair, :, b * KB : (b + 1) * KB] = (
                        expon[:, b * KB : (b + 1) * KB].astype(F32) * scale
                    ).astype(BF)

    for n in range(1, SPAN + 1):
        pl.when(count == n)(functools.partial(body, n))


GROUP = 6


def attend(win, seq, mask, q, k, v):
    tok, d = q.shape
    tiles, pairs = tok // QB, d // (2 * DH)
    return pl.pallas_call(
        attend_kernel,
        grid_spec=pltpu.PrefetchScalarGridSpec(
            num_scalar_prefetch=1,
            grid=(tiles,),
            in_specs=[whole(seq.shape), whole(mask.shape), rows_of(d, QB), whole(k.shape), whole(v.shape)],
            out_specs=[
                rows_of(d, QB),
                pl.BlockSpec((1, pairs, 2 * QB, SPAN * KB), lambda i, s: (i, 0, 0, 0)),
            ],
            scratch_shapes=[pltpu.VMEM((QB, SPAN * KB), F32), pltpu.VMEM((pairs, 2 * QB, SPAN * KB), F32)],
        ),
        out_shape=[struct((tok, d), BF), struct((tiles, pairs, 2 * QB, SPAN * KB), BF)],
        compiler_params=params(),
        cost_estimate=cost(1.4e10, 2e7),
        name="attend",
    )(win, seq, mask, q, k, v)


def attend_back(place_win, side, q, k, v, ctx, do, p, tokens, out_grad):
    tok, d = q.shape
    half = d // 2
    tiles, pairs = tok // QB, half // (2 * DH)
    pick = (lambda s: s[0]) if side == 0 else (lambda s: 1 - s[0])
    row = pl.BlockSpec((QB, half), lambda i, s: (i, pick(s)))
    cols = pl.BlockSpec((tok, half), lambda i, s: (0, pick(s)))

    def kernel(s, q_ref, k_ref, v_ref, ctx_ref, do_ref, p_ref, x_ref, out_grad_ref, grad_ref, sum_ref, w_ref, dkt, dvt, s_ref):
        i = pl.program_id(0)
        low, count = s[3 + i], s[3 + tiles + i]
        start = pl.multiple_of(i * QB, QB)

        @pl.when(i == 0)
        def _():
            dkt[...] = jnp.zeros_like(dkt)
            dvt[...] = jnp.zeros_like(dvt)
            sum_ref[...] = jnp.zeros_like(sum_ref)

        def body(n):
            w = n * KB
            base = pl.multiple_of(low * KB, KB)
            lanes = [slice(p * 2 * DH, (p + 1) * 2 * DH) for p in range(pairs)]
            for pair, ln in enumerate(lanes):
                s_ref[pair, :, :w] = dot_right(stack_pair(do_ref[:, ln]), v_ref[pl.ds(base, w), ln])
            for pair, ln in enumerate(lanes):
                dvt[ln, pl.ds(base, w)] += dot(stack_pair(do_ref[:, ln]).T, p_ref[0, pair, :, :w])
            scores = []
            for pair, ln in enumerate(lanes):
                along = do_ref[:, ln].astype(F32) * ctx_ref[:, ln].astype(F32)
                delta = jnp.sum(stack_pair(along), axis=1, keepdims=True)
                scores.append((p_ref[0, pair, :, :w].astype(F32) * (s_ref[pair, :, :w] - delta)).astype(BF))
            for pair, ln in enumerate(lanes):
                dq = fold_pair(dot(scores[pair], k_ref[pl.ds(base, w), ln])) * (1.0 / math.sqrt(DH))
                dq = dq.astype(BF)
                grad_ref[pl.ds(start, QB), ln] = dq
                sum_ref[0:1, ln] += column_sum(dq.astype(F32))
            for pair, ln in enumerate(lanes):
                dkt[ln, pl.ds(base, w)] += dot(stack_pair(q_ref[:, ln]).T, scores[pair])

        for n in range(1, SPAN + 1):
            pl.when(count == n)(functools.partial(body, n))

        @pl.when(i == tiles - 1)
        def _():
            for o in range(0, tok, QB):
                grad_ref[o : o + QB, half : 2 * half] = dkt[:, o : o + QB].T.astype(BF)
                dv = dvt[:, o : o + QB].T.astype(BF)
                grad_ref[o : o + QB, 2 * half :] = dv
                sum_ref[1:2, :] += column_sum(dv.astype(F32))
            turned = x_ref[...].T
            rows = d // OWNERS
            for n in range(3):
                grads = dot(turned, grad_ref[:, n * half : (n + 1) * half])
                w_ref[:, n * rows : (n + 1) * rows, :] = grads.astype(BF).reshape(OWNERS, rows, half)
            w_ref[:, 3 * rows :, :] = out_grad_ref[...]

    return pl.pallas_call(
        kernel,
        grid_spec=pltpu.PrefetchScalarGridSpec(
            num_scalar_prefetch=1,
            grid=(tiles,),
            in_specs=[
                row,
                cols,
                cols,
                row,
                row,
                pl.BlockSpec((1, pairs, 2 * QB, SPAN * KB), lambda i, s: (i, pick(s), 0, 0)),
                whole((tok, d)),
                whole(out_grad.shape),
            ],
            out_specs=[whole((tok, 3 * half)), whole((SUMS, half)), whole((OWNERS, d // 2, half))],
            scratch_shapes=[
                pltpu.VMEM((half, tok), F32),
                pltpu.VMEM((half, tok), F32),
                pltpu.VMEM((pairs, 2 * QB, SPAN * KB), F32),
            ],
        ),
        out_shape=[
            struct((tok, 3 * half), BF),
            struct((SUMS, half), F32),
            struct((OWNERS, d // 2, half), BF),
        ],
        compiler_params=params(),
        cost_estimate=cost(1e10, 1e7),
        name="attend_back",
    )(place_win, q, k, v, ctx, do, p, tokens, out_grad)


class Weight:
    def __init__(self, shard, first):
        self.rows, self.width = shard.shape
        self.shard = shard
        self.first = first


class Group:
    def __init__(self, mesh, shards):
        self.fsdp = mesh.shape["fsdp"]
        self.fast = fast_path(mesh, shards)
        self.pieces = []
        self.weights = []
        first = 0
        for shard in shards:
            self.weights.append(Weight(shard, first))
            first += shard.size // (2 * PIECE)
        self.height = first

    def full(self, k):
        weight = self.weights[k]
        return (weight.rows * (self.fsdp if self.fast else 1), weight.width)

    def operands(self, used):
        if not self.fast:
            return [self.weights[k].shard for k in used]
        return [self.weights[k].shard for k in used] + [array for array, _, _ in self.pieces]

    def load(self, used, table, refs, targets, sems):
        if not self.fast:
            for n, target in enumerate(targets):
                pltpu.make_async_copy(refs[n], target, sems.at[n]).start()
            return
        core = table[self.fsdp]
        for n, k in enumerate(used):
            weight, target, sem = self.weights[k], targets[n], sems.at[n]
            half = weight.rows // 2
            base = pl.multiple_of(table[0] * weight.rows, weight.rows)
            pltpu.make_async_copy(refs[n], target.at[pl.ds(base, weight.rows), :], sem).start()
            for piece, (_, sources, mate) in zip(refs[len(used) :], self.pieces):
                side = (1 - core) if mate else core
                height = piece.shape[0] // len(sources)
                for order, source in enumerate(sources):
                    row = pl.multiple_of(table[source] * weight.rows + side * half, 16)
                    for c in range(weight.width // PIECE):
                        start = order * height + weight.first + c * half
                        pltpu.make_async_copy(
                            piece.at[start : start + half, :],
                            target.at[pl.ds(row, half), c * PIECE : (c + 1) * PIECE],
                            sem,
                        ).start()

    def wait(self, targets, sems):
        for n, target in enumerate(targets):
            pltpu.make_async_copy(target, target, sems.at[n]).wait()

    def wait_one(self, n, targets, sems):
        pltpu.make_async_copy(targets[n], targets[n], sems.at[n]).wait()

    def scratch(self, used):
        return [pltpu.VMEM(self.full(k), BF) for k in used] + [pltpu.SemaphoreType.DMA((len(used),))]


PIECE = 768
OWNERS = 8
SUMS = 16


def fast_path(mesh, shards):
    return (
        mesh.shape["fsdp"] == 8
        and mesh.shape["rep"] == 4
        and all(s.shape[0] % 32 == 0 and s.shape[1] % PIECE == 0 for s in shards)
    )


RING = (0, 2, 4, 6, 7, 5, 3, 1)


def ring_table():
    size = len(RING)
    place = {v: p for p, v in enumerate(RING)}
    steps = list(range(0, -(size // 2) - 1, -1)) + list(range(1, size - size // 2))
    return [[RING[(place[f] + s) % size] for s in steps] for f in range(size)]


def ring_step(value, step):
    size = len(RING)
    return lax.ppermute(value, "fsdp", [(RING[p], RING[(p + step) % size]) for p in range(size)])


def rep_step(value, bits):
    return lax.ppermute(value, "rep", [(r, r ^ bits) for r in range(4)])


def pallas(body, name, table, operands, outs, scratch, flops, limit=60):
    operands, outs = list(operands), list(outs)
    size = sum(o.size * o.dtype.itemsize for o in operands + outs)
    return pl.pallas_call(
        body,
        in_specs=[pl.BlockSpec(memory_space=pltpu.SMEM)] + [ANY] * len(operands),
        out_specs=[ANY] * len(outs),
        out_shape=outs,
        scratch_shapes=list(scratch) + [pltpu.SemaphoreType.DMA((COPIES,))],
        compiler_params=pltpu.CompilerParams(vmem_limit_bytes=limit << 20),
        cost_estimate=cost(flops, size),
        name=name,
    )(table, *operands)


COPIES = 48


class Copies:
    def __init__(self, sems):
        self.sems, self.started = sems, []

    def start(self, source, target):
        copy = pltpu.make_async_copy(source, target, self.sems.at[len(self.started)])
        copy.start()
        self.started.append([copy, False])
        return len(self.started) - 1

    def wait(self, *numbers):
        for n in numbers:
            if not self.started[n][1]:
                self.started[n][0].wait()
                self.started[n][1] = True

    def end(self):
        self.wait(*range(len(self.started)))


def vmem(*shape, dtype=BF):
    return pltpu.VMEM(shape, dtype)


def pack(table, groups, vectors):
    shards = [w.shard for g in groups for w in g.weights]
    core = table.shape[0] - 1
    outs = [struct((g.height + (SMALL if g is groups[0] else 0), PIECE), BF) for g in groups]

    def body(s, *refs):
        vec_refs = refs[: len(vectors)]
        shard_refs = list(refs[len(vectors) : len(vectors) + len(shards)])
        outs, refs = refs[len(vectors) + len(shards) :][: len(groups)], refs[len(vectors) + len(shards) + len(groups) :]
        staged, held, sems = refs[: len(groups)], refs[len(groups) : -1], refs[-1]
        copies = Copies(sems)
        loads = [copies.start(r, h) for r, h in zip(vec_refs, held)]
        ready = []
        for g, group in enumerate(groups):
            ready.append([])
            for weight in group.weights:
                ref, half = shard_refs.pop(0), weight.rows // 2
                rows = pl.ds(pl.multiple_of(s[core] * half, half), half)
                for c in range(weight.width // PIECE):
                    ready[g].append(
                        copies.start(
                            ref.at[rows, c * PIECE : (c + 1) * PIECE],
                            staged[g].at[weight.first + c * half : weight.first + (c + 1) * half, :],
                        )
                    )
        copies.wait(*loads)
        used = [r[...].astype(F32).reshape(1, -1) for r in held]
        row = jnp.concatenate(used[:-1], axis=1)
        last = jnp.concatenate([used[-1], jnp.zeros((1, PIECE - used[-1].shape[1]), F32)], axis=1)
        rest = jnp.zeros((SMALL - 2, PIECE), F32)
        staged[0][groups[0].height :, :] = jnp.concatenate([row, last, rest], axis=0).astype(BF)
        for g in range(len(groups)):
            copies.wait(*ready[g])
            copies.start(staged[g], outs[g])
        copies.end()

    return pallas(
        body,
        "pack",
        table,
        vectors + shards,
        outs,
        [vmem(*o.shape) for o in outs] + [vmem(*v.shape) for v in vectors],
        1,
    )


def project(table, group, tokens, small):
    tok, d = tokens.shape
    used = (0, 1, 2)
    extra = group.operands(used)
    fsdp, part = group.fsdp, d // group.fsdp
    wide = 4 * d // fsdp

    def body(s, x_hbm, small_hbm, *refs):
        pieces, outs, refs = refs[: len(extra)], refs[len(extra) : len(extra) + 8], refs[len(extra) + 8 :]
        x_ref, res_ref, vec_ref, bias_ref, all_small, small_sem, *weights, weight_sems, sems = refs
        copies = Copies(sems)
        tokens_in = copies.start(x_hbm, x_ref)
        group.load(used, s, pieces, weights, weight_sems)
        if group.fast:
            own = small_hbm.at[small_hbm.shape[0] - SMALL :, :]
            pltpu.make_async_copy(own, all_small.at[s[0]], small_sem).start()
            for piece, (_, sources, mate) in zip(pieces[len(used) :], group.pieces):
                if not mate:
                    pltpu.make_async_copy(
                        piece.at[group.height : group.height + SMALL, :], all_small.at[s[sources[0]]], small_sem
                    ).start()
        else:
            pltpu.make_async_copy(small_hbm, all_small, small_sem).start()
        pltpu.make_async_copy(all_small, all_small, small_sem).wait()
        rows = [all_small[f].astype(F32) for f in range(fsdp)]
        for v in range(8):
            vec_ref[v : v + 1, :] = jnp.concatenate([r[0:1, v * part : (v + 1) * part] for r in rows], axis=1)
        bias_ref[...] = jnp.zeros_like(bias_ref)
        bias_ref[0:1, :] = jnp.concatenate([r[1:2, :wide] for r in rows], axis=1)
        copies.start(vec_ref, outs[3])
        copies.start(bias_ref, outs[4])
        copies.wait(tokens_in)
        for n, weight in enumerate(weights):
            group.wait_one(n, weights, weight_sems)
            copies.start(weight, outs[5 + n])
            result = dot(x_ref[...], weight[...])
            if n == 0:
                result = (result + vec_ref[0:1, :]).astype(BF) * jnp.asarray(1.0 / math.sqrt(DH), BF)
            if n == 2:
                result = result + vec_ref[1:2, :]
            res_ref[n] = result.astype(BF)
            copies.start(res_ref.at[n], outs[n])
        copies.end()

    return pallas(
        body,
        "project",
        table,
        [tokens, small] + extra,
        [struct((tok, d), BF)] * 3
        + [struct((8, d), F32), struct((8, 4 * d), F32)]
        + [struct(group.full(k), BF) for k in used],
        [vmem(tok, d), vmem(3, tok, d), vmem(8, d, dtype=F32), vmem(8, 4 * d, dtype=F32)]
        + [vmem(fsdp, SMALL, d), pltpu.SemaphoreType.DMA]
        + group.scratch(used),
        6 * tok * d * d,
    )


SMALL = 16


def forward_block(table, inner, outer, context, tokens, out_grad, vectors, bias_inner):
    tok, d = tokens.shape
    ff = inner.full(1)[1]
    extra_inner, extra_outer = inner.operands((0, 1)), outer.operands((0,))
    count = len(extra_inner)
    extra = extra_inner + extra_outer
    rows, wide = struct((tok, d), BF), struct((tok, ff), BF)
    half, part = d // 2, ff // OWNERS
    outs = [rows, struct((tok, d), F32), rows, wide, struct((tok, d), F32), rows, struct((SUMS, d), F32)]
    outs += [struct((OWNERS, half, part), BF)] * 2
    outs += [struct(inner.full(0), BF), struct(inner.full(1), BF), struct(outer.full(0), BF)]

    def body(s, ctx_hbm, x_hbm, g_hbm, vec_hbm, bias_hbm, *refs):
        pieces, refs = refs[: len(extra)], refs[len(extra) :]
        out_hbm, hid_hbm, low_hbm, slope_hbm, second_hbm, grad_hbm, sum_hbm, mine_hbm, other_hbm = refs[:9]
        w_out_hbm, w_in_hbm, w_outer_hbm = refs[9:12]
        ctx_ref, x_ref, g_ref, vec_ref, bias_ref, hid_ref, low_ref, act_ref, slope_ref = refs[12:21]
        total, sum_ref, both, w_out, w_in, inner_sems, w_outer, outer_sems, sems = refs[21:]
        core = s[table.shape[0] - 1]
        copies = Copies(sems)
        loads = [copies.start(a, b) for a, b in ((ctx_hbm, ctx_ref), (x_hbm, x_ref), (vec_hbm, vec_ref))]
        inner.load((0, 1), s, pieces[:count], (w_out, w_in), inner_sems)
        outer.load((0,), s, pieces[count:], (w_outer,), outer_sems)
        later = [copies.start(bias_hbm, bias_ref), copies.start(g_hbm, g_ref)]
        sum_ref[...] = jnp.zeros_like(sum_ref)
        copies.wait(*loads)
        inner.wait_one(0, (w_out,), inner_sems)
        copies.start(w_out, w_out_hbm)
        hidden = x_ref[...].astype(F32) + dot(ctx_ref[...], w_out[...]) + vec_ref[2:3, :]
        hid_ref[...] = hidden
        hidden_out = copies.start(hid_ref, hid_hbm)
        normed, _ = norm(hidden)
        first = normed * vec_ref[3:4, :] + vec_ref[4:5, :]
        low_ref[...] = first.astype(BF)
        low_out = copies.start(low_ref, low_hbm)
        total[...] = first + vec_ref[5:6, :]
        inner.wait_one(1, (w_out, w_in), inner_sems)
        copies.start(w_in, w_in_hbm)
        outer.wait_one(0, (w_outer,), outer_sems)
        copies.start(w_outer, w_outer_hbm)
        copies.wait(*later)
        for c in range(0, ff, d):
            cols = slice(c, c + d)
            act, slope = gelu_parts(dot(low_ref[...], w_in[:, cols]) + bias_ref[0:1, cols])
            act = act.astype(BF)
            act_ref[:, cols] = act
            slope_ref[:, cols] = slope.astype(BF)
            copies.start(slope_ref.at[:, cols], slope_hbm.at[:, cols])
            total[...] += dot(act, w_outer[cols, :])
        normed, inverse = norm(total[...])
        gain = vec_ref[6:7, :]
        x_ref[...] = (normed * gain + vec_ref[7:8, :]).astype(BF)
        copies.start(x_ref, out_hbm)
        grad = g_ref[...].astype(F32)
        sum_ref[2:3, :] = column_sum(grad * normed)
        sum_ref[3:4, :] = column_sum(grad)
        second = norm_back(grad * gain, normed, inverse)
        low = second.astype(BF)
        ctx_ref[...] = low
        copies.start(ctx_ref, grad_hbm)
        copies.wait(hidden_out)
        hid_ref[...] = second
        copies.start(hid_ref, second_hbm)
        sum_ref[4:5, :] = column_sum(low.astype(F32))
        copies.start(sum_ref, sum_hbm)
        turned = low.T
        for i in range(0, OWNERS, 2):
            grads = dot(turned, act_ref[:, i * part : (i + 2) * part]).astype(BF)
            for k in (0, 1):
                columns = slice(k * part, (k + 1) * part)
                both[0, i + k], both[1, i + k] = grads[:half, columns], grads[half:, columns]
            pair = pl.ds(i, 2)
            copies.start(both.at[1 - core, pair], other_hbm.at[pair])
            copies.start(both.at[core, pair], mine_hbm.at[pair])
        copies.end()

    row = vmem(tok, d)
    return pallas(
        body,
        "forward_block",
        table,
        [context, tokens, out_grad, vectors, bias_inner] + extra,
        outs,
        [row, row, row, vmem(8, d, dtype=F32), vmem(8, ff, dtype=F32), vmem(tok, d, dtype=F32), row]
        + [vmem(tok, ff), vmem(tok, ff), vmem(tok, d, dtype=F32), vmem(SUMS, d, dtype=F32)]
        + [vmem(2, OWNERS, half, part)]
        + inner.scratch((0, 1))
        + outer.scratch((0,)),
        2 * tok * d * (d + 3 * ff),
        62,
    )


def active_back(choice, grad_low, slope, w_outer, first_low):
    tok, d = grad_low.shape
    ff = slope.shape[1]
    blocks = [slice(c, c + d) for c in range(0, ff, d)]
    half, rows, part = len(blocks) // 2, d // OWNERS, d // 2

    def body(s, g_hbm, slope_hbm, w_hbm, low_hbm, out_hbm, sum_hbm, mine_hbm, other_hbm, *refs):
        g_ref, slope_ref, w_ref, low_ref, out_ref, sum_ref, turned, held, sems = refs
        copies = Copies(sems)
        first = copies.start(g_hbm, g_ref)
        loads = [
            (copies.start(w_hbm.at[b, :], w_ref.at[b, :]), copies.start(slope_hbm.at[:, b], slope_ref.at[:, b]))
            for b in blocks
        ]
        left = copies.start(low_hbm, low_ref)
        sum_ref[...] = jnp.zeros_like(sum_ref)
        copies.wait(first)
        for n, b in enumerate(blocks):
            copies.wait(*loads[n])
            low = (dot_right(g_ref[...], w_ref[b, :]) * slope_ref[:, b].astype(F32)).astype(BF)
            out_ref[:, b] = low
            copies.start(out_ref.at[:, b], out_hbm.at[:, b])
            sum_ref[8 + n : 9 + n, :] = column_sum(low.astype(F32))
            if n == 0:
                copies.wait(left)
                turned[...] = low_ref[...].T
            grads = dot(turned[...], low).astype(BF)
            for k in range(0, d, part):
                at = (n % half * d + k) // part * rows
                held[n // half, :, at : at + rows, :] = grads[:, k : k + part].reshape(OWNERS, rows, part)
        copies.start(held.at[1 - s[0]], other_hbm)
        copies.start(held.at[s[0]], mine_hbm)
        copies.start(sum_ref, sum_hbm)
        copies.end()

    grad = struct((OWNERS, rows * ff // (2 * part), part), BF)
    return pallas(
        body,
        "active_back",
        choice,
        [grad_low, slope, w_outer, first_low],
        [struct((tok, ff), BF), struct((SUMS, d), F32), grad, grad],
        [vmem(tok, d), vmem(tok, ff), vmem(ff, d), vmem(tok, d), vmem(tok, ff), vmem(SUMS, d, dtype=F32)]
        + [vmem(d, tok), vmem(2, *grad.shape)],
        4 * tok * d * ff,
    )


def inner_back(choice, grad_inner, grad_second, hidden, vectors, w_out, w_in, context):
    tok, d = hidden.shape
    ff, half = grad_inner.shape[1], d // 2
    blocks = [slice(c, c + d) for c in range(0, ff, d)]

    def body(s, g_hbm, second_hbm, hid_hbm, vec_hbm, w_out_hbm, w_in_hbm, *refs):
        left_hbm, out_hbm, ctx_hbm, sum_hbm, mine_hbm, other_hbm = refs[:6]
        g_ref, second_ref, hid_ref, vec_ref, w_out, w_in, left_ref, ctx_ref, sum_ref, held, sems = refs[6:]
        copies = Copies(sems)
        loads = [
            (copies.start(g_hbm.at[:, b], g_ref.at[:, b]), copies.start(w_in_hbm.at[:, b], w_in.at[:, b]))
            for b in blocks[:1]
        ]
        first = copies.start(second_hbm, second_ref)
        loads += [
            (copies.start(g_hbm.at[:, b], g_ref.at[:, b]), copies.start(w_in_hbm.at[:, b], w_in.at[:, b]))
            for b in blocks[1:]
        ]
        later = [copies.start(a, b) for a, b in ((hid_hbm, hid_ref), (vec_hbm, vec_ref), (w_out_hbm, w_out))]
        later.append(copies.start(left_hbm, left_ref))
        sum_ref[...] = jnp.zeros_like(sum_ref)
        for n, b in enumerate(blocks):
            copies.wait(*loads[n])
            part = dot_right(g_ref[:, b], w_in[:, b])
            if n == 0:
                copies.wait(first)
            second_ref[...] += part
        copies.wait(*later)
        grad = second_ref[...]
        normed, inverse = norm(hid_ref[...])
        sum_ref[5:6, :] = column_sum(grad * normed)
        sum_ref[6:7, :] = column_sum(grad)
        hidden_grad = norm_back(grad * vec_ref[3:4, :], normed, inverse)
        second_ref[...] = hidden_grad
        copies.start(second_ref, out_hbm)
        low = hidden_grad.astype(BF)
        ctx_ref[...] = dot_right(low, w_out[...]).astype(BF)
        copies.start(ctx_ref, ctx_hbm)
        grads = dot(left_ref[...].T, low).astype(BF)
        for k in (0, 1):
            held[k] = grads[:, k * half : (k + 1) * half].reshape(OWNERS, d // OWNERS, half)
        copies.start(held.at[1 - s[0]], other_hbm)
        copies.start(held.at[s[0]], mine_hbm)
        sum_ref[7:8, :] = column_sum(low.astype(F32))
        copies.start(sum_ref, sum_hbm)
        copies.end()

    full, grad = vmem(tok, d, dtype=F32), struct((OWNERS, d // OWNERS, half), BF)
    return pallas(
        body,
        "inner_back",
        choice,
        [grad_inner, grad_second, hidden, vectors, w_out, w_in, context],
        [struct((tok, d), F32), struct((tok, d), BF), struct((SUMS, d), F32), grad, grad],
        [vmem(tok, ff), full, full, vmem(8, d, dtype=F32), vmem(d, d), vmem(d, ff), vmem(tok, d), vmem(tok, d)]
        + [vmem(SUMS, d, dtype=F32), vmem(2, *grad.shape)],
        2 * tok * d * (2 * d + ff),
    )


def tokens_back(choice, grad_hidden, mine, other, weights):
    tok, d = grad_hidden.shape
    half = d // 2

    def body(s, hid_hbm, mine_hbm, other_hbm, *refs):
        weights, out_hbm, hid_ref, grad_ref, w_ref, out_ref, sems = refs[:3], *refs[3:]
        copies = Copies(sems)
        loads = []
        for k, (grad, side) in enumerate(((other_hbm, 1 - s[0]), (mine_hbm, s[0]))):
            cols = pl.ds(pl.multiple_of(side * half, half), half)
            for n, weight in enumerate(weights):
                at = 3 * k + n
                loads.append(
                    (
                        copies.start(grad.at[:, n * half : (n + 1) * half], grad_ref.at[at]),
                        copies.start(weight.at[:, cols], w_ref.at[at]),
                    )
                )
            if k == 0:
                first = copies.start(hid_hbm, hid_ref)
        for at, load in enumerate(loads):
            copies.wait(*load)
            part = dot_right(grad_ref[at], w_ref[at])
            copies.wait(first)
            if at < 5:
                hid_ref[...] += part
            else:
                out_ref[...] = (hid_ref[...] + part).astype(BF)
        copies.start(out_ref, out_hbm)
        copies.end()

    return pallas(
        body,
        "tokens_back",
        choice,
        [grad_hidden, mine, other, *weights],
        [struct((tok, d), BF)],
        [vmem(tok, d, dtype=F32), vmem(6, tok, half), vmem(6, d, half), vmem(tok, d)],
        6 * tok * d * d,
    )[0]


def axis_step(value, axis):
    if axis == "x":
        return rep_step(value, 2)
    return lax.ppermute(value, "fsdp", [(f, f ^ 1) for f in range(8)])


def after(value, *events):
    return lax.optimization_barrier((value,) + events)[0] if events else value


def added(*terms):
    total = terms[0].astype(F32)
    for term in terms[1:]:
        total = total + term.astype(F32)
    return total.astype(BF)


def chosen(parts, bit, axis):
    return lax.dynamic_index_in_dim(parts, bit, axis, keepdims=False)


def halves(value, bit, axis):
    owners, rows, n = value.shape
    if axis == "y":
        return chosen(value.reshape(owners // 2, 2, rows, n), bit, 1)
    return chosen(value.reshape(owners, 2, rows // 2, n), bit, 1)


class Stream:
    def __init__(self, place, terms, order):
        self.place, self.terms, self.order = place, terms, order

    def move(self, axis, *events):
        bit = self.place.x if axis == "x" else self.place.y
        terms = self.terms[:-1] + [after(self.terms[-1], *events)]
        send = added(*(halves(v, 1 - bit, axis) for v in terms))
        self.terms = [halves(v, bit, axis) for v in terms] + [axis_step(send, axis)]
        return [send]

    def first(self, *events):
        return self.move(self.order[0], *events)

    def second(self, *events):
        return self.move(self.order[1], *events)


class Owned:
    def __init__(self, place, mine, received):
        self.place, mid = place, mine.shape[1] // 2
        self.streams = [
            Stream(place, [mine[:, :mid], received[:, :mid]], "xy"),
            Stream(place, [mine[:, mid:], received[:, mid:]], "yx"),
        ]

    def first(self, *events):
        return [s for stream in self.streams for s in stream.first(*events)]

    def second(self, *events):
        return [s for stream in self.streams for s in stream.second(*events)]

    def third(self, *events):
        sums = [added(*s.terms[:-1], after(s.terms[-1], *events)) for s in self.streams]
        parts = jnp.concatenate(sums, 1)
        z = self.place.z
        moved = [
            lax.ppermute(
                chosen(parts, (z + k) % 4, 0), "fsdp", [(f, (f // 2 + k) % 4 * 2 + f % 2) for f in range(8)]
            )
            for k in (1, 3, 2)
        ]
        self.terms = [chosen(parts, z, 0)] + moved
        return [parts]

    def fourth(self, *events):
        self.own = added(*self.terms[:-1], after(self.terms[-1], *events))
        self.other = rep_step(self.own, 2)
        return [self.own]

    def fifth(self, *events):
        other = after(self.other, *events)
        low = jnp.where(self.place.x == 0, self.own, other)
        high = jnp.where(self.place.x == 0, other, self.own)
        mid = low.shape[0] // 2
        half = jnp.concatenate([low[:mid], high[:mid], low[mid:], high[mid:]], 0)
        self.both = (half, rep_step(half, 1))
        return [half]

    def last(self):
        mine, mate = self.both
        first = self.place.core == 0
        return jnp.where(first, mine, mate), jnp.where(first, mate, mine)


class Place:
    def __init__(self, mesh):
        f, r = lax.axis_index("fsdp"), lax.axis_index("rep")
        self.f, self.core, self.x = f, r % 2, r // 2
        self.y, self.z = f % 2, f // 2
        self.choice = jnp.stack([self.core, self.x, self.y]).astype(jnp.int32)
        if mesh.shape["fsdp"] == len(RING):
            row = lax.dynamic_index_in_dim(jnp.array(ring_table(), jnp.int32), f, 0, keepdims=False)
            self.table = jnp.concatenate([row, self.core[None].astype(jnp.int32)])
        else:
            self.table = jnp.zeros((1,), jnp.int32)


class Ring:
    def __init__(self, group, payload, last):
        self.group, self.ways, self.last, self.count = group, {1: [payload], -1: [payload]}, last, 0

    def ways_of(self, count):
        return (1, -1) if count < len(RING) // 2 else (self.last,)

    def source(self, way, count):
        return count if way == 1 or count == len(RING) // 2 else len(RING) // 2 + count

    @property
    def came(self):
        return tuple(self.ways[way][self.count] for way in self.ways_of(self.count))

    def step(self, *events):
        self.count += 1
        for way in self.ways_of(self.count):
            self.ways[way].append(ring_step(after(self.ways[way][-1], *events), way))
            self.group.pieces.append((self.ways[way][-1], (self.source(way, self.count),), False))

    def share(self, count, *events):
        for way in self.ways_of(count):
            piece = rep_step(after(self.ways[way][count], *events), 1)
            self.group.pieces.append((piece, (self.source(way, count),), True))


class Travel:
    def __init__(self, rings):
        self.rings, self.past, self.seen, self.shared = rings, [], (), [0] * len(rings)

    def run(self, order, *events):
        for n in order:
            ring = self.rings[n]
            if len(self.past) > 2:
                last = self.past[-3]
                self.seen = self.came(last)
                self.share(last[0])
            ring.step(*events, *self.seen)
            self.past.append((n, ring.came))

    def came(self, entry):
        return entry[1]

    def share(self, n, *events):
        ring = self.rings[n]
        while self.shared[n] < ring.count:
            self.shared[n] += 1
            ring.share(self.shared[n], *events)

    def settle(self, n):
        self.share(n)


def local(mesh, *args):
    (
        tokens, seq_ids, key_mask, weight_query, bias_query, weight_key, weight_value, bias_value,
        weight_out, bias_out, norm1_gain, norm1_bias, weight_inner, bias_inner, weight_outer, bias_outer,
        norm2_gain, norm2_bias, out_grad,
    ) = args
    place = Place(mesh)
    choice, table = place.choice, place.table
    fsdp = mesh.shape["fsdp"]
    d = tokens.shape[1]
    win = windows(seq_ids[0])
    narrow = [bias_query, bias_value, bias_out, norm1_gain, norm1_bias, bias_outer, norm2_gain, norm2_bias]
    shards = [[weight_query, weight_key, weight_value], [weight_out, weight_inner], [weight_outer]]
    fast = all(fast_path(mesh, s) for s in shards)
    if fast:
        groups = [Group(mesh, s) for s in shards]
        packed = pack(table, groups, narrow + [bias_inner])
        rings = [Ring(g, p, way) for g, p, way in zip(groups, packed, (1, -1, 1))]
        small = packed[0]
        travel = Travel(rings)
        travel.run((0, 1, 2, 0, 1, 0, 2, 0))
        travel.settle(0)
        travel.run((1,))
    else:
        groups = [Group(mesh, [lax.all_gather(w, "fsdp", axis=0, tiled=True) for w in s]) for s in shards]
        rows = [jnp.concatenate(narrow), bias_inner]
        rows = [jnp.concatenate([r, jnp.zeros((d - r.size,), BF)])[None] for r in rows]
        small = jnp.concatenate(rows + [jnp.zeros((SMALL - 2, d), BF)], 0)
        small = lax.all_gather(small, "fsdp", axis=0, tiled=False)
    qkv, inner_group, outer_group = groups

    q, k, v, vectors, full_bias_inner, *weights = project(table, qkv, tokens, small)
    if fast:
        travel.run((2, 1), q)
        q = after(q, *travel.seen)
    context, probs = attend(win, seq_ids, key_mask, q, k, v)
    if fast:
        travel.run((2,), context)
        travel.settle(1)
        travel.settle(2)
    (
        layer_out, hidden, first_low, slope, grad_second, grad_outer, sums2, outer_mine, outer_other,
        w_out, w_in, w_outer,
    ) = forward_block(
        place_table(table, choice), inner_group, outer_group, context, tokens, out_grad, vectors, full_bias_inner
    )
    if not fast:
        choice = jnp.zeros((3,), jnp.int32)
    if fast:
        outer_sum = Owned(place, outer_mine, rep_step(outer_other, 1))
    grad_inner, sums_inner, inner_mine, inner_other = active_back(choice, grad_outer, slope, w_outer, first_low)
    if fast:
        inner_sum = Owned(place, inner_mine, rep_step(inner_other, 1))
        event = outer_sum.first(inner_mine)
        grad_inner = after(grad_inner, *event)
    grad_hidden, grad_context, sums1, out_mine, out_other = inner_back(
        choice, grad_inner, grad_second, hidden, vectors, w_out, w_in, context
    )
    if fast:
        event = outer_sum.second(out_mine)
        event += inner_sum.first(out_mine)
        grad_context = after(grad_context, *event)
    place_win = jnp.concatenate([choice, win])
    grads_other, sums_other, query_other = attend_back(
        place_win, 1, q, k, v, context, grad_context, probs, tokens, out_other
    )
    if fast:
        query_came = rep_step(query_other, 1)
        event = inner_sum.second(grads_other)
        event += outer_sum.third(grads_other)
        grad_context = after(grad_context, *event)
    grads_mine, sums_mine, query_mine = attend_back(
        place_win, 0, q, k, v, context, grad_context, probs, tokens, out_mine
    )
    if fast:
        query_sum = Owned(place, query_mine, query_came)
        event = query_sum.first(query_mine)
        event += inner_sum.third(query_mine)
        event += outer_sum.fourth(query_mine)
        grad_hidden = after(grad_hidden, *event)
    grad_tokens = tokens_back(choice, grad_hidden, grads_mine, grads_other, weights)
    sums_att = by_core(choice[0], sums_mine, sums_other, 1)
    sums = sums1 + sums2 + sums_inner + sums_att
    if fast:
        event = query_sum.second(grad_tokens)
        sums = sums + after(rep_step(sums, 1), *event)
        event += inner_sum.fourth(*event)
        event += outer_sum.fifth(*event)
        sums = sums + after(rep_step(sums, 2), *event)
        event = query_sum.third(*event)
        sums = sums + after(axis_step(sums, "y"), *event)
        event += inner_sum.fifth(sums)
        low, high = outer_sum.last()
        final_outer = jnp.concatenate([low, high], 0).T.astype(F32)
        sums = sums + after(z_step(sums, 1), *event)
        sums = sums + after(z_step(sums, 2), *event)
        low, high = inner_sum.last()
        rows = d // fsdp
        blocks = [v[c : c + rows] for v in (low, high) for c in range(0, v.shape[0], rows)]
        final_inner = jnp.concatenate(blocks, 1).astype(F32)
        event = query_sum.fourth(final_outer, final_inner, sums)
        query_sum.fifth(*event)
        low, high = query_sum.last()
        final_query, final_key, final_value, final_out = (
            jnp.concatenate([low[c : c + rows], high[c : c + rows]], 1).astype(F32)
            for c in range(0, 4 * rows, rows)
        )
    else:

        def plain(*blocks):
            total = jnp.concatenate(blocks, 2)
            total = total.reshape(-1, total.shape[2])
            owned = lax.psum_scatter(total, "fsdp", scatter_dimension=0, tiled=True)
            return lax.psum(owned, "rep").astype(F32)

        sums = lax.psum(sums, ("fsdp", "rep"))
        final_outer = plain(jnp.concatenate([outer_mine, outer_other], 1).transpose(0, 2, 1))
        part = d // OWNERS
        unstack = lambda v: [v[:, c : c + part] for c in range(0, v.shape[1], part)]
        final_inner = plain(*unstack(inner_mine), *unstack(inner_other))
        final_query, final_key, final_value, final_out = (
            plain(a, b) for a, b in zip(unstack(query_mine), unstack(query_other))
        )

    narrow_sums = lax.dynamic_slice_in_dim(sums, place.f * (d // fsdp), d // fsdp, 1)
    inner_sums = lax.dynamic_slice_in_dim(sums[8:12].reshape(-1), place.f * bias_inner.size, bias_inner.size, 0)
    return (
        layer_out,
        grad_tokens,
        final_query,
        narrow_sums[0],
        final_key,
        final_value,
        narrow_sums[1],
        final_out,
        narrow_sums[7],
        narrow_sums[5],
        narrow_sums[6],
        final_inner,
        inner_sums,
        final_outer,
        narrow_sums[4],
        narrow_sums[2],
        narrow_sums[3],
    )


def by_core(core, mine, other, axis):
    return jnp.where(core == 0, jnp.concatenate([mine, other], axis), jnp.concatenate([other, mine], axis))


def z_step(value, bits):
    return lax.ppermute(value, "fsdp", [(f, f ^ (2 * bits)) for f in range(8)])


def place_table(table, choice):
    return jnp.concatenate([table[:-1], choice[:1]]) if table.shape[0] > 1 else jnp.zeros((1,), jnp.int32)


def solution(mesh):
    rows, shard, part = P(("fsdp", "rep"), None), P("fsdp", None), P("fsdp")
    return jax.shard_map(
        functools.partial(local, mesh),
        mesh=mesh,
        in_specs=(
            rows, rows, rows, shard, part, shard, shard, part, shard, part, part, part, shard, part, shard,
            part, part, part, rows,
        ),
        out_specs=(
            rows, rows, shard, part, shard, shard, part, shard, part, part, part, shard, part, shard, part,
            part, part,
        ),
        check_vma=False,
    )
```

time: 482 us -> 354 us (0.73)
  blocking collectives: 83.7 us -> 0 us
  Pallas kernels: 188 us -> 139 us
  other arithmetic: 12.7 us -> 36.2 us
  waiting for transfers between devices: 96.2 us -> 84.9 us
  local copies, waits for them, and re-layouts: 29.2 us -> 21 us
    psum x1 -> x0, blocking collectives: 47.2 us -> none  [local(): sums = lax.psum(sums, ('fsdp', 'rep'))]
    pallas_call x15 -> x8, Pallas kernels: 165 us -> 124 us  [the longest x6 91 us: pallas(): pl.pallas_call(body, in_specs=[pl.BlockSpec(memory_space=pltpu.SMEM)] + [...]
    all_gather x1 -> x0, blocking collectives: 36.5 us -> none  [local(): lax.all_gather(jnp.concatenate(narrow + [bias_inner]), 'fsdp', axis=0, ti...]
    ppermute x41 -> x38, waiting for transfers between devices: 39.1 us -> 13.7 us  [rep_step(): return lax.ppermute(value, 'rep', [(r, r ^ bits) for r in range(4)])]
    convert_element_type x20 -> x27, other arithmetic: 10.1 us -> 30.5 us  [the longest x21 26.3 us: added(): return total.astype(BF)]
    ppermute x21, waiting for transfers between devices: 34.8 us -> 47.2 us  [ring_step(): lax.ppermute(value, 'fsdp', [(RING[p], RING[(p + step) % size]) for p in...]
    unnamed x116 -> x160, local copies, waits for them, and re-layouts: 16.1 us -> 6.42 us
    pallas_call x1, Pallas kernels: 23.1 us -> 15 us  [attend(): pl.pallas_call(attend_kernel, grid_spec=pltpu.PrefetchScalarGridSpec(num_...]
  transfers between devices with their start and end apart: 78 -> 77, of which waited for: 21 -> 23; matrix products, arithmetic and copies ran while one was open for 7% -> 14% of each run, Pallas kernels for 34% -> 31%
where the time goes in v2:
time: 354 us; the launch traced here: 347 us
  Pallas kernels  139 us (39%)
  waiting for transfers between devices  84.9 us (24%)
  starting transfers between devices  63.6 us (18%)
  other arithmetic  36.2 us (10%)
  local copies, waits for them, and re-layouts  21 us (6%)
    pallas_call x6, Pallas kernels, pallas(): pl.pallas_call(body, in_specs=[pl.BlockSpec(memory_space=pltpu.SMEM)] + [...  91 us
    ppermute x21, waiting for transfers between devices, ring_step(): lax.ppermute(value, 'fsdp', [(RING[p], RING[(p + step) % size]) for p in...  47.2 us
    pallas_call x2, Pallas kernels, attend_back(): pl.pallas_call(kernel, grid_spec=pltpu.PrefetchScalarGridSpec(num_scalar_...  32.9 us
    ppermute x21, starting transfers between devices, ring_step(): lax.ppermute(value, 'fsdp', [(RING[p], RING[(p + step) % size]) for p in...  29.6 us
    convert_element_type x21, other arithmetic, added(): return total.astype(BF)  26.3 us
    pallas_call x1, Pallas kernels, attend(): pl.pallas_call(attend_kernel, grid_spec=pltpu.PrefetchScalarGridSpec(num_...  15 us
    ppermute x38, starting transfers between devices, rep_step(): return lax.ppermute(value, 'rep', [(r, r ^ bits) for r in range(4)])  14.3 us
    ppermute x38, waiting for transfers between devices, rep_step(): return lax.ppermute(value, 'rep', [(r, r ^ bits) for r in range(4)])  13.7 us
  transfers between devices with their start and end apart: 77, of which 23 were waited for; matrix products, arithmetic and copies ran while one was open for 14% of the time, Pallas kernels for 31%

profile of v2, /device:TPU:0, one launch (start us, length us, event | category | flops | bytes accessed | tf_op | source)
XLA Modules:
  0.0 346.7 jit_solution(3146278082154048202)
XLA Ops:
  2.0 3.2 pack.1
  5.2 3.1 collective-permute-start
  10.3 2.0 collective-permute-start.6
  12.3 2.9 collective-permute-done.refs_3_
  15.2 2.1 collective-permute-start.7
  20.5 2.6 collective-permute-done.14.refs_2_
  23.1 2.1 collective-permute-start.5
  26.8 2.6 collective-permute-done.6.refs_17_
  29.4 2.1 collective-permute-start.16
  34.7 2.1 collective-permute-start.8
  39.0 8.0 %collective-permute-done.8.refs_9_ = bf16[160,768]{1,0:T(8,128)(2,1)S(1)} collective-permute-done((bf16[160,768]{1,0:T(8,128)(2,1)S(1)}, bf16[160,768]{1,0:T(8,128)(2,1)S(1)}, u32[]{:S(2)}, u32[]{:S(2)}) %collective-permute-start.8) | collective-permute-done | bytes 245792 | tf_op jit(solution)/shard_map/ppermute | solution.py:348
  47.0 1.7 collective-permute-start.9
  49.6 1.8 collective-permute-start.32
  51.4 2.7 collective-permute-done.9.refs_10_
  56.1 2.0 collective-permute-done.18.refs_15_
  58.1 5.4 %collective-permute-done.32.refs_21_ = bf16[192,768]{1,0:T(8,128)(2,1)S(1)} collective-permute-done((bf16[192,768]{1,0:T(8,128)(2,1)S(1)}, bf16[192,768]{1,0:T(8,128)(2,1)S(1)}, u32[]{:S(2)}, u32[]{:S(2)}) %collective-permute-start.32) | collective-permute-done | bytes 294944 | tf_op jit(solution)/shard_map/ppermute | solution.py:348
  66.8 10.0 %project.1 = (bf16[1024,768]{1,0:T(8,128)(2,1)}, bf16[1024,768]{1,0:T(8,128)(2,1)}, bf16[1024,768]{1,0:T(8,128)(2,1)}, f32[8,768]{1,0:T(8,128)}, f32[8,3072]{1,0...) custom-call(s32[9]{0:T(128)} %pad_add_fusion.s, bf16[1024,768]{1,0:T(8,128)(2,1)} %x_ref.3, ...), custom_call_target="tpu_custom_call" | custom-call | flops 181193936 | bytes 704102 | tf_op jit(solution)/shard_map/project/pallas_call | solution.py:358
  79.4 7.0 %collective-permute-done.36.refs_25_ = bf16[192,768]{1,0:T(8,128)(2,1)S(1)} collective-permute-done((bf16[192,768]{1,0:T(8,128)(2,1)S(1)}, bf16[192,768]{1,0:T(8,128)(2,1)S(1)}, u32[]{:S(2)}, u32[]{:S(2)}) %collective-permute-start.36) | collective-permute-done | bytes 294944 | tf_op jit(solution)/shard_map/ppermute | solution.py:348
  87.0 1.8 collective-permute-start.26
  89.4 15.0 %attend.1 = (bf16[1024,768]{1,0:T(8,128)(2,1)}, bf16[8,6,256,640]{3,2,1,0:T(8,128)(2,1)}) custom-call(s32[16]{0:T(128)} %pad_add_fusion.1.win, s32[1,1024]{1,0:T(1,128)} %seq_ref.1, s32[1,1024]{1,0:T(1,128)} %mask_ref.1, bf16[1024,768]{1,0:T(8,128)(2,1)} %get-tuple-element.117.q_ref, bf16[1024,768]{1,0:T(8,128)(2,1)} %get-tuple-element.118.k_ref, ...), custom_call_target="tpu_custom_call" | custom-call | flops 700000000 | bytes 1000000 | tf_op jit(solution)/shard_map/attend/pallas_call | solution.py:151
  107.5 4.6 %collective-permute-done.37.refs_26_ = bf16[192,768]{1,0:T(8,128)(2,1)S(1)} collective-permute-done((bf16[192,768]{1,0:T(8,128)(2,1)}, bf16[192,768]{1,0:T(8,128)(2,1)S(1)}, u32[]{:S(2)}, u32[]{:S(2)}) %collective-permute-start.37) | collective-permute-done | bytes 294944 | tf_op jit(solution)/shard_map/ppermute | solution.py:348
  112.1 1.8 collective-permute-done.38.refs_27_
  116.2 29.4 %forward_block.1 = (bf16[1024,768]{1,0:T(8,128)(2,1)}, f32[1024,768]{1,0:T(8,128)}, bf16[1024,768]{1,0:T(8,128)(2,1)}, bf16[1024,3072]{1,0:T(8,128)(2,1)}, f32[1...) custom-call(s32[9]{0:T(128)} %pad_add_fusion.s, ...), custom_call_target="tpu_custom_call" | custom-call | flops 785173696 | bytes 2407219 | tf_op jit(solution)/shard_map/forward_block/pallas_call | solution.py:358
  146.4 18.6 %active_back.1 = (bf16[1024,3072]{1,0:T(8,128)(2,1)}, f32[16,768]{1,0:T(8,128)}, bf16[8,384,384]{2,1,0:T(8,128)(2,1)}, bf16[8,384,384]{2,1,0:T(8,128)(2,1)}) custom-call(s32[3]{0:T(128)} %pad_add_fusion.2.s, bf16[1024,768]{1,0:T(8,128)(2,1)} %get-tuple-element.132.g_hbm, bf16[1024,3072]{1,0:T(8,128)(2,1)} %get-tuple-element.133.slope_hbm, ...), custom_call_target="tpu_custom_call" | custom-call | flops 483183808 | bytes 1260748 | tf_op jit(solution)/shard_map/active_back/pallas_call | solution.py:358
  169.4 1.9 fusion.60
  176.3 1.9 fusion.58
  178.2 17.6 %inner_back.1 = (f32[1024,768]{1,0:T(8,128)}, bf16[1024,768]{1,0:T(8,128)(2,1)}, f32[16,768]{1,0:T(8,128)}, bf16[8,96,384]{2,1,0:T(8,128)(2,1)}, bf16[8,96,384]{2,1,0:T(8,128)(2,1)}) custom-call(s32[3]{0:T(128)} %pad_add_fusion.2.s, bf16[1024,3072]{1,0:T(8,128)(2,1)} %get-tuple-element.142.g_hbm, f32[1024,768]{1,0:T(8,128)} %get-tuple-element.143.second_hbm, ...), custom_call_target="tpu_custom_call" | custom-call | flops 362387872 | bytes 1301299 | tf_op jit(solution)/shard_map/inner_back/pallas_call | solution.py:358
  195.8 2.0 fusion.3
  200.3 2.1 fusion.13
  202.4 1.8 fusion.12
  204.2 16.4 %attend_back.2 = (bf16[1024,1152]{1,0:T(8,128)(2,1)}, f32[16,384]{1,0:T(8,128)}, bf16[8,384,384]{2,1,0:T(8,128)(2,1)}) custom-call(s32[19]{0:T(128)} %concatenate.55.s, bf16[1024,768]{1,0:T(8,128)(2,1)} %get-tuple-element.117.q_ref, bf16[1024,768]{1,0:T(8,128)(2,1)} %get-tuple-element.118.k_ref, bf16[1024,768]{1,0:T(8,128)(2,1)} %get-tuple-element.119.v_ref, ...), custom_call_target="tpu_custom_call" | custom-call | flops 500000000 | bytes 500000 | tf_op jit(solution)/shard_map/attend_back/pallas_call | solution.py:227
  220.9 2.2 fusion.15
  224.0 1.8 fusion.14
  225.8 1.7 collective-permute-start.51
  229.0 16.5 %attend_back.3 = (bf16[1024,1152]{1,0:T(8,128)(2,1)}, f32[16,384]{1,0:T(8,128)}, bf16[8,384,384]{2,1,0:T(8,128)(2,1)}) custom-call(s32[19]{0:T(128)} %concatenate.55.s, bf16[1024,768]{1,0:T(8,128)(2,1)} %get-tuple-element.117.q_ref, bf16[1024,768]{1,0:T(8,128)(2,1)} %get-tuple-element.118.k_ref, bf16[1024,768]{1,0:T(8,128)(2,1)} %get-tuple-element.119.v_ref, ...), custom_call_target="tpu_custom_call" | custom-call | flops 500000000 | bytes 500000 | tf_op jit(solution)/shard_map/attend_back/pallas_call | solution.py:227
  247.0 2.0 fusion.55
  255.2 2.8 collective-permute-start.61
  258.0 8.9 %collective-permute-done.55 = bf16[192,384]{1,0:T(8,128)(2,1)S(1)} collective-permute-done((bf16[192,384]{1,0:T(8,128)(2,1)S(1)}, bf16[192,384]{1,0:T(8,128)(2,1)S(1)}, u32[]{:S(2)}, u32[]{:S(2)}) %collective-permute-start.55) | collective-permute-done | bytes 147488 | tf_op jit(solution)/shard_map/ppermute | solution.py:814
  266.9 1.9 fusion.56
  269.9 2.4 collective-permute-start.58
  273.3 2.2 collective-permute-start.59
  277.8 12.3 %tokens_back.1 = bf16[1024,768]{1,0:T(8,128)(2,1)} custom-call(s32[3]{0:T(128)} %pad_add_fusion.2.s, f32[1024,768]{1,0:T(8,128)} %get-tuple-element.171.hid_hbm, bf16[1024,1152]{1,0:T(8,128)(2,1)} %get-tuple-element.172.mine_hbm, bf16[1024,1152]{1,0:T(8,128)(2,1)} %get-tuple-element.158.other_hbm, bf16[768,768]{1,0:T(8,128)(2,1)} %get-tuple-element.173.refs_0_, ...), custom_call_target="tpu_custom_call" | custom-call | flops 181193936 | bytes 648806 | tf_op jit(solution)/shard_map/tokens_back/pallas_call | solution.py:358
  292.2 1.8 collective-permute-start.60
  300.2 1.7 collective-permute-done.62
  303.4 6.7 %collective-permute-done.70 = f32[16,768]{1,0:T(8,128)S(1)} collective-permute-done((f32[16,768]{1,0:T(8,128)S(1)}, f32[16,768]{1,0:T(8,128)S(1)}, u32[]{:S(2)}, u32[]{:S(2)}) %collective-permute-start.70) | collective-permute-done | bytes 49184 | tf_op jit(solution)/shard_map/ppermute | solution.py:352
  316.8 2.6 collective-permute-start.65
  320.0 13.5 %collective-permute-done.74 = f32[16,768]{1,0:T(8,128)S(1)} collective-permute-done((f32[16,768]{1,0:T(8,128)S(1)}, f32[16,768]{1,0:T(8,128)S(1)}, u32[]{:S(2)}, u32[]{:S(2)}) %collective-permute-start.74) | collective-permute-done | bytes 49184 | tf_op jit(solution)/shard_map/ppermute | solution.py:1060
  336.2 4.2 %collective-permute-done.75 = bf16[192,384]{1,0:T(8,128)(2,1)S(1)} collective-permute-done((bf16[192,384]{1,0:T(8,128)(2,1)S(1)}, bf16[192,384]{1,0:T(8,128)(2,1)S(1)}, u32[]{:S(2)}, u32[]{:S(2)}) %collective-permute-start.75) | collective-permute-done | bytes 147488 | tf_op jit(solution)/shard_map/ppermute | solution.py:352
  (357 shorter events, 81.4 us)
Async XLA Ops:
  8.2 14.8 %collective-permute-start.14 = (bf16[240,768]{1,0:T(8,128)(2,1)}, bf16[240,768]{1,0:T(8,128)(2,1)S(1)}, u32[]{:S(2)}, u32[]{:S(2)}) collective-permute-start(bf16[240,768]{1,0:T(8,128)(2,1)} %get-tuple-element.112), channel_id=1, source_target_pairs={{0,8},{8,16},{16,24},{24,28},{28,20},{20,12},{12,4},{4,0},{1,9},{9... | collective-permute-start | bytes 1105928 | tf_op jit(solution)/shard_map/ppermute | solution.py:348
  10.3 16.6 %collective-permute-start.15 = (bf16[240,768]{1,0:T(8,128)(2,1)}, bf16[240,768]{1,0:T(8,128)(2,1)S(1)}, u32[]{:S(2)}, u32[]{:S(2)}) collective-permute-start(bf16[240,768]{1,0:T(8,128)(2,1)} %get-tuple-element.112), channel_id=1, source_target_pairs={{0,4},{8,0},{16,8},{24,16},{28,24},{20,28},{12,20},{4,12},{1,5},{9... | collective-permute-start | bytes 1105928 | tf_op jit(solution)/shard_map/ppermute | solution.py:348
  10.3 19.1 %collective-permute-start.6 = (bf16[192,768]{1,0:T(8,128)(2,1)}, bf16[192,768]{1,0:T(8,128)(2,1)S(1)}, u32[]{:S(2)}, u32[]{:S(2)}) collective-permute-start(bf16[192,768]{1,0:T(8,128)(2,1)} %get-tuple-element.109), channel_id=1, source_target_pairs={{0,8},{8,16},{16,24},{24,28},{28,20},{20,12},{12,4},{4,0},{1,9},{9... | collective-permute-start | bytes 884744 | tf_op jit(solution)/shard_map/ppermute | solution.py:348
  15.2 18.0 %collective-permute-start.7 = (bf16[192,768]{1,0:T(8,128)(2,1)}, bf16[192,768]{1,0:T(8,128)(2,1)S(1)}, u32[]{:S(2)}, u32[]{:S(2)}) collective-permute-start(bf16[192,768]{1,0:T(8,128)(2,1)} %get-tuple-element.109), channel_id=1, source_target_pairs={{0,4},{8,0},{16,8},{24,16},{28,24},{20,28},{12,20},{4,12},{1,5},{9... | collective-permute-start | bytes 884744 | tf_op jit(solution)/shard_map/ppermute | solution.py:348
  18.9 15.7 %collective-permute-start.4 = (bf16[160,768]{1,0:T(8,128)(2,1)S(1)}, bf16[160,768]{1,0:T(8,128)(2,1)S(1)}, u32[]{:S(2)}, u32[]{:S(2)}) collective-permute-start(bf16[160,768]{1,0:T(8,128)(2,1)S(1)} %collective-permute-done.refs_3_), channel_id=1, source_target_pairs={{0,8},{8,16},{16,24},{24,28},{28,20},{20,12},{12,4},{4,0},{1,9},{9... | collective-permute-start | bytes 737288 | tf_op jit(solution)/shard_map/ppermute | solution.py:348
  23.1 15.3 %collective-permute-start.5 = (bf16[160,768]{1,0:T(8,128)(2,1)S(1)}, bf16[160,768]{1,0:T(8,128)(2,1)S(1)}, u32[]{:S(2)}, u32[]{:S(2)}) collective-permute-start(bf16[160,768]{1,0:T(8,128)(2,1)S(1)} %collective-permute-done.1.refs_4_), channel_id=1, source_target_pairs={{0,4},{8,0},{16,8},{24,16},{28,24},{20,28},{12,20},{4,12},{1,5},{9... | collective-permute-start | bytes 737288 | tf_op jit(solution)/shard_map/ppermute | solution.py:348
  26.8 11.6 %collective-permute-start.2 = (bf16[160,768]{1,0:T(8,128)(2,1)S(1)}, bf16[160,768]{1,0:T(8,128)(2,1)S(1)}, u32[]{:S(2)}, u32[]{:S(2)}) collective-permute-start(bf16[160,768]{1,0:T(8,128)(2,1)S(1)} %collective-permute-done.refs_3_), channel_id=1, source_target_pairs={{0,1},{1,0},{2,3},{3,2},{4,5},{5,4},{6,7},{7,6},{8,9},{9,8},{10,11... | collective-permute-start | bytes 737288 | tf_op jit(solution)/shard_map/ppermute | solution.py:352
  29.4 19.3 %collective-permute-start.16 = (bf16[240,768]{1,0:T(8,128)(2,1)S(1)}, bf16[240,768]{1,0:T(8,128)(2,1)S(1)}, u32[]{:S(2)}, u32[]{:S(2)}) collective-permute-start(bf16[240,768]{1,0:T(8,128)(2,1)S(1)} %collective-permute-done.14.refs_2_), channel_id=1, source_target_pairs={{0,8},{8,16},{16,24},{24,28},{28,20},{20,12},{12,4},{4,0},{1,9},{9... | collective-permute-start | bytes 1105928 | tf_op jit(solution)/shard_map/ppermute | solution.py:348
  33.1 15.6 %collective-permute-start.17 = (bf16[240,768]{1,0:T(8,128)(2,1)S(1)}, bf16[240,768]{1,0:T(8,128)(2,1)S(1)}, u32[]{:S(2)}, u32[]{:S(2)}) collective-permute-start(bf16[240,768]{1,0:T(8,128)(2,1)S(1)} %collective-permute-done.15.refs_3_), channel_id=1, source_target_pairs={{0,4},{8,0},{16,8},{24,16},{28,24},{20,28},{12,20},{4,12},{1,5},{9... | collective-permute-start | bytes 1105928 | tf_op jit(solution)/shard_map/ppermute | solution.py:348
  34.7 12.3 %collective-permute-start.8 = (bf16[160,768]{1,0:T(8,128)(2,1)S(1)}, bf16[160,768]{1,0:T(8,128)(2,1)S(1)}, u32[]{:S(2)}, u32[]{:S(2)}) collective-permute-start(bf16[160,768]{1,0:T(8,128)(2,1)S(1)} %collective-permute-done.4.refs_7_), channel_id=1, source_target_pairs={{0,8},{8,16},{16,24},{24,28},{28,20},{20,12},{12,4},{4,0},{1,9},{9... | collective-permute-start | bytes 737288 | tf_op jit(solution)/shard_map/ppermute | solution.py:348
  49.6 14.0 %collective-permute-start.32 = (bf16[192,768]{1,0:T(8,128)(2,1)S(1)}, bf16[192,768]{1,0:T(8,128)(2,1)S(1)}, u32[]{:S(2)}, u32[]{:S(2)}) collective-permute-start(bf16[192,768]{1,0:T(8,128)(2,1)S(1)} %collective-permute-done.6.refs_17_), channel_id=1, source_target_pairs={{0,8},{8,16},{16,24},{24,28},{28,20},{20,12},{12,4},{4,0},{1,9},{9... | collective-permute-start | bytes 884744 | tf_op jit(solution)/shard_map/ppermute | solution.py:348
  63.5 13.5 %collective-permute-start.20 = (bf16[240,768]{1,0:T(8,128)(2,1)S(1)}, bf16[240,768]{1,0:T(8,128)(2,1)S(1)}, u32[]{:S(2)}, u32[]{:S(2)}) collective-permute-start(bf16[240,768]{1,0:T(8,128)(2,1)S(1)} %collective-permute-done.14.refs_2_), channel_id=1, source_target_pairs={{0,1},{1,0},{2,3},{3,2},{4,5},{5,4},{6,7},{7,6},{8,9},{9,8},{10,11... | collective-permute-start | bytes 1105928 | tf_op jit(solution)/shard_map/ppermute | solution.py:352
  63.5 13.3 %collective-permute-start.31 = (bf16[192,768]{1,0:T(8,128)(2,1)S(1)}, bf16[192,768]{1,0:T(8,128)(2,1)}, u32[]{:S(2)}, u32[]{:S(2)}) collective-permute-start(bf16[192,768]{1,0:T(8,128)(2,1)S(1)} %collective-permute-done.7.refs_18_), channel_id=1, source_target_pairs={{0,1},{1,0},{2,3},{3,2},{4,5},{5,4},{6,7},{7,6},{8,9},{9,8},{10,11... | collective-permute-start | bytes 884744 | tf_op jit(solution)/shard_map/ppermute | solution.py:352
  64.1 13.7 %collective-permute-start.21 = (bf16[240,768]{1,0:T(8,128)(2,1)S(1)}, bf16[240,768]{1,0:T(8,128)(2,1)S(1)}, u32[]{:S(2)}, u32[]{:S(2)}) collective-permute-start(bf16[240,768]{1,0:T(8,128)(2,1)S(1)} %collective-permute-done.15.refs_3_), channel_id=1, source_target_pairs={{0,1},{1,0},{2,3},{3,2},{4,5},{5,4},{6,7},{7,6},{8,9},{9,8},{10,11... | collective-permute-start | bytes 1105928 | tf_op jit(solution)/shard_map/ppermute | solution.py:352
  64.2 13.7 %collective-permute-start.25 = (bf16[240,768]{1,0:T(8,128)(2,1)S(1)}, bf16[240,768]{1,0:T(8,128)(2,1)S(1)}, u32[]{:S(2)}, u32[]{:S(2)}) collective-permute-start(bf16[240,768]{1,0:T(8,128)(2,1)S(1)} %collective-permute-done.17.refs_7_), channel_id=1, source_target_pairs={{0,4},{8,0},{16,8},{24,16},{28,24},{20,28},{12,20},{4,12},{1,5},{9... | collective-permute-start | bytes 1105928 | tf_op jit(solution)/shard_map/ppermute | solution.py:348
  65.8 13.4 %collective-permute-start.24 = (bf16[240,768]{1,0:T(8,128)(2,1)S(1)}, bf16[240,768]{1,0:T(8,128)(2,1)S(1)}, u32[]{:S(2)}, u32[]{:S(2)}) collective-permute-start(bf16[240,768]{1,0:T(8,128)(2,1)S(1)} %collective-permute-done.16.refs_6_), channel_id=1, source_target_pairs={{0,8},{8,16},{16,24},{24,28},{28,20},{20,12},{12,4},{4,0},{1,9},{9... | collective-permute-start | bytes 1105928 | tf_op jit(solution)/shard_map/ppermute | solution.py:348
  77.8 27.5 %collective-permute-start.22 = (bf16[240,768]{1,0:T(8,128)(2,1)S(1)}, bf16[240,768]{1,0:T(8,128)(2,1)S(1)}, u32[]{:S(2)}, u32[]{:S(2)}) collective-permute-start(bf16[240,768]{1,0:T(8,128)(2,1)S(1)} %collective-permute-done.16.refs_6_), channel_id=1, source_target_pairs={{0,1},{1,0},{2,3},{3,2},{4,5},{5,4},{6,7},{7,6},{8,9},{9,8},{10,11... | collective-permute-start | bytes 1105928 | tf_op jit(solution)/shard_map/ppermute | solution.py:352
  77.9 26.5 %collective-permute-start.35 = (bf16[192,768]{1,0:T(8,128)(2,1)}, bf16[192,768]{1,0:T(8,128)(2,1)}, u32[]{:S(2)}, u32[]{:S(2)}) collective-permute-start(bf16[192,768]{1,0:T(8,128)(2,1)} %collective-permute-done.33.refs_22_), channel_id=1, source_target_pairs={{0,1},{1,0},{2,3},{3,2},{4,5},{5,4},{6,7},{7,6},{8,9},{9,8},{10,11... | collective-permute-start | bytes 884744 | tf_op jit(solution)/shard_map/ppermute | solution.py:352
  78.5 28.4 %collective-permute-start.23 = (bf16[240,768]{1,0:T(8,128)(2,1)S(1)}, bf16[240,768]{1,0:T(8,128)(2,1)S(1)}, u32[]{:S(2)}, u32[]{:S(2)}) collective-permute-start(bf16[240,768]{1,0:T(8,128)(2,1)S(1)} %collective-permute-done.17.refs_7_), channel_id=1, source_target_pairs={{0,1},{1,0},{2,3},{3,2},{4,5},{5,4},{6,7},{7,6},{8,9},{9,8},{10,11... | collective-permute-start | bytes 1105928 | tf_op jit(solution)/shard_map/ppermute | solution.py:352
  79.2 28.2 %collective-permute-start.27 = (bf16[240,768]{1,0:T(8,128)(2,1)S(1)}, bf16[240,768]{1,0:T(8,128)(2,1)S(1)}, u32[]{:S(2)}, u32[]{:S(2)}) collective-permute-start(bf16[240,768]{1,0:T(8,128)(2,1)S(1)} %collective-permute-done.24.refs_10_), channel_id=1, source_target_pairs={{0,1},{1,0},{2,3},{3,2},{4,5},{5,4},{6,7},{7,6},{8,9},{9,8},{10,11... | collective-permute-start | bytes 1105928 | tf_op jit(solution)/shard_map/ppermute | solution.py:352
  87.0 19.9 %collective-permute-start.26 = (bf16[240,768]{1,0:T(8,128)(2,1)S(1)}, bf16[240,768]{1,0:T(8,128)(2,1)S(1)}, u32[]{:S(2)}, u32[]{:S(2)}) collective-permute-start(bf16[240,768]{1,0:T(8,128)(2,1)S(1)} %collective-permute-done.25.refs_11_), channel_id=1, source_target_pairs={{0,4},{8,0},{16,8},{24,16},{28,24},{20,28},{12,20},{4,12},{1,5},{9... | collective-permute-start | bytes 1105928 | tf_op jit(solution)/shard_map/ppermute | solution.py:348
  145.6 23.8 %collective-permute-start.42 = (bf16[8,384,384]{2,1,0:T(8,128)(2,1)}, bf16[8,384,384]{2,1,0:T(8,128)(2,1)}, u32[]{:S(2)}, u32[]{:S(2)}) collective-permute-start(bf16[8,384,384]{2,1,0:T(8,128)(2,1)} %get-tuple-element.138), channel_id=1, source_target_pairs={{0,1},{1,0},{2,3},{3,2},{4,5},{5,4},{6,7},{7,6},{8,9},{9,8},{10,11... | collective-permute-start | bytes 7077896 | tf_op jit(solution)/shard_map/ppermute | solution.py:352
  165.0 11.4 %collective-permute-start.45 = (bf16[8,384,384]{2,1,0:T(8,128)(2,1)}, bf16[8,384,384]{2,1,0:T(8,128)(2,1)}, u32[]{:S(2)}, u32[]{:S(2)}) collective-permute-start(bf16[8,384,384]{2,1,0:T(8,128)(2,1)} %get-tuple-element.152), channel_id=1, source_target_pairs={{0,1},{1,0},{2,3},{3,2},{4,5},{5,4},{6,7},{7,6},{8,9},{9,8},{10,11... | collective-permute-start | bytes 7077896 | tf_op jit(solution)/shard_map/ppermute | solution.py:352
  172.4 27.7 %collective-permute-start.44 = (bf16[4,192,384]{2,1,0:T(8,128)(2,1)}, bf16[4,192,384]{2,1,0:T(8,128)(2,1)}, u32[]{:S(2)}, u32[]{:S(2)}) collective-permute-start(bf16[4,192,384]{2,1,0:T(8,128)(2,1)} %fusion.1), channel_id=1, source_target_pairs={{0,4},{4,0},{8,12},{12,8},{16,20},{20,16},{24,28},{28,24},{1,5},{5... | collective-permute-start | bytes 1769480 | tf_op jit(solution)/shard_map/ppermute | solution.py:752
  174.8 27.6 %collective-permute-start.43 = (bf16[8,96,384]{2,1,0:T(8,128)(2,1)}, bf16[8,96,384]{2,1,0:T(8,128)(2,1)}, u32[]{:S(2)}, u32[]{:S(2)}) collective-permute-start(bf16[8,96,384]{2,1,0:T(8,128)(2,1)} %fusion), channel_id=1, source_target_pairs={{0,2},{1,3},{2,0},{3,1},{4,6},{5,7},{6,4},{7,5},{8,10},{9,11},{10,... | collective-permute-start | bytes 1769480 | tf_op jit(solution)/shard_map/ppermute | solution.py:352
  197.9 23.0 %collective-permute-start.47 = (bf16[4,192,384]{2,1,0:T(8,128)(2,1)}, bf16[4,192,384]{2,1,0:T(8,128)(2,1)}, u32[]{:S(2)}, u32[]{:S(2)}) collective-permute-start(bf16[4,192,384]{2,1,0:T(8,128)(2,1)} %fusion.3), channel_id=1, source_target_pairs={{0,4},{4,0},{8,12},{12,8},{16,20},{20,16},{24,28},{28,24},{1,5},{5... | collective-permute-start | bytes 1769480 | tf_op jit(solution)/shard_map/ppermute | solution.py:752
  199.1 21.7 %collective-permute-start.46 = (bf16[8,96,384]{2,1,0:T(8,128)(2,1)}, bf16[8,96,384]{2,1,0:T(8,128)(2,1)}, u32[]{:S(2)}, u32[]{:S(2)}) collective-permute-start(bf16[8,96,384]{2,1,0:T(8,128)(2,1)} %fusion.2), channel_id=1, source_target_pairs={{0,2},{1,3},{2,0},{3,1},{4,6},{5,7},{6,4},{7,5},{8,10},{9,11},{10,... | collective-permute-start | bytes 1769480 | tf_op jit(solution)/shard_map/ppermute | solution.py:352
  220.6 46.3 %collective-permute-start.50 = (bf16[8,384,384]{2,1,0:T(8,128)(2,1)}, bf16[8,384,384]{2,1,0:T(8,128)(2,1)}, u32[]{:S(2)}, u32[]{:S(2)}) collective-permute-start(bf16[8,384,384]{2,1,0:T(8,128)(2,1)} %get-tuple-element.165), channel_id=1, source_target_pairs={{0,1},{1,0},{2,3},{3,2},{4,5},{5,4},{6,7},{7,6},{8,9},{9,8},{10,11... | collective-permute-start | bytes 7077896 | tf_op jit(solution)/shard_map/ppermute | solution.py:352
  223.1 25.9 %collective-permute-start.52 = (bf16[4,96,384]{2,1,0:T(8,128)(2,1)}, bf16[4,96,384]{2,1,0:T(8,128)(2,1)S(1)}, u32[]{:S(2)}, u32[]{:S(2)}) collective-permute-start(bf16[4,96,384]{2,1,0:T(8,128)(2,1)} %fusion.15), channel_id=1, source_target_pairs={{0,2},{1,3},{2,0},{3,1},{4,6},{5,7},{6,4},{7,5},{8,10},{9,11},{10,... | collective-permute-start | bytes 884744 | tf_op jit(solution)/shard_map/ppermute | solution.py:352
  225.8 23.3 %collective-permute-start.51 = (bf16[4,96,384]{2,1,0:T(8,128)(2,1)}, bf16[4,96,384]{2,1,0:T(8,128)(2,1)S(1)}, u32[]{:S(2)}, u32[]{:S(2)}) collective-permute-start(bf16[4,96,384]{2,1,0:T(8,128)(2,1)} %fusion.14), channel_id=1, source_target_pairs={{0,4},{4,0},{8,12},{12,8},{16,20},{20,16},{24,28},{28,24},{1,5},{5... | collective-permute-start | bytes 884744 | tf_op jit(solution)/shard_map/ppermute | solution.py:752
  227.5 21.6 %collective-permute-start.49 = (bf16[4,96,384]{2,1,0:T(8,128)(2,1)S(1)}, bf16[4,96,384]{2,1,0:T(8,128)(2,1)S(1)}, u32[]{:S(2)}, u32[]{:S(2)}) collective-permute-start(bf16[4,96,384]{2,1,0:T(8,128)(2,1)S(1)} %copy-done.39), channel_id=1, source_target_pairs={{0,2},{1,3},{2,0},{3,1},{4,6},{5,7},{6,4},{7,5},{8,10},{9,11},{10,... | collective-permute-start | bytes 884744 | tf_op jit(solution)/shard_map/ppermute | solution.py:352
  228.2 21.0 %collective-permute-start.48 = (bf16[4,96,384]{2,1,0:T(8,128)(2,1)S(1)}, bf16[4,96,384]{2,1,0:T(8,128)(2,1)}, u32[]{:S(2)}, u32[]{:S(2)}) collective-permute-start(bf16[4,96,384]{2,1,0:T(8,128)(2,1)S(1)} %copy-done.40), channel_id=1, source_target_pairs={{0,4},{4,0},{8,12},{12,8},{16,20},{20,16},{24,28},{28,24},{1,5},{5... | collective-permute-start | bytes 884744 | tf_op jit(solution)/shard_map/ppermute | solution.py:752
  249.0 52.9 %collective-permute-start.69 = (f32[16,768]{1,0:T(8,128)}, f32[16,768]{1,0:T(8,128)}, u32[]{:S(2)}, u32[]{:S(2)}) collective-permute-start(f32[16,768]{1,0:T(8,128)} %fusion.51), channel_id=1, source_target_pairs={{0,1},{1,0},{2,3},{3,2},{4,5},{5,4},{6,7},{7,6},{8,9},{9,8},{10,11... | collective-permute-start | bytes 147464 | tf_op jit(solution)/shard_map/ppermute | solution.py:352
  252.0 14.9 %collective-permute-start.55 = (bf16[192,384]{1,0:T(8,128)(2,1)S(1)}, bf16[192,384]{1,0:T(8,128)(2,1)S(1)}, u32[]{:S(2)}, u32[]{:S(2)}) collective-permute-start(bf16[192,384]{1,0:T(8,128)(2,1)S(1)} %get-tuple-element.276), channel_id=1, source_target_pairs={{0,16},{4,20},{8,24},{12,28},{16,0},{20,4},{24,8},{28,12},{1,17},{... | collective-permute-start | bytes 442376 | tf_op jit(solution)/shard_map/ppermute | solution.py:814
  255.2 41.5 %collective-permute-start.61 = (bf16[192,384]{1,0:T(8,128)(2,1)}, bf16[192,384]{1,0:T(8,128)(2,1)}, u32[]{:S(2)}, u32[]{:S(2)}) collective-permute-start(bf16[192,384]{1,0:T(8,128)(2,1)} %get-tuple-element.273), channel_id=1, source_target_pairs={{0,16},{4,20},{8,24},{12,28},{16,0},{20,4},{24,8},{28,12},{1,17},{... | collective-permute-start | bytes 442376 | tf_op jit(solution)/shard_map/ppermute | solution.py:814
  258.0 15.3 %collective-permute-start.53 = (bf16[192,384]{1,0:T(8,128)(2,1)S(1)}, bf16[192,384]{1,0:T(8,128)(2,1)S(1)}, u32[]{:S(2)}, u32[]{:S(2)}) collective-permute-start(bf16[192,384]{1,0:T(8,128)(2,1)S(1)} %get-tuple-element.274), channel_id=1, source_target_pairs={{0,8},{4,12},{8,16},{12,20},{16,24},{20,28},{24,0},{28,4},{1,9},{5... | collective-permute-start | bytes 442376 | tf_op jit(solution)/shard_map/ppermute | solution.py:814
  269.9 21.6 %collective-permute-start.58 = (bf16[4,192,384]{2,1,0:T(8,128)(2,1)}, bf16[4,192,384]{2,1,0:T(8,128)(2,1)}, u32[]{:S(2)}, u32[]{:S(2)}) collective-permute-start(bf16[4,192,384]{2,1,0:T(8,128)(2,1)} %fusion.5), channel_id=1, source_target_pairs={{0,4},{4,0},{8,12},{12,8},{16,20},{20,16},{24,28},{28,24},{1,5},{5... | collective-permute-start | bytes 1769480 | tf_op jit(solution)/shard_map/ppermute | solution.py:752
  273.3 25.1 %collective-permute-start.59 = (bf16[192,384]{1,0:T(8,128)(2,1)}, bf16[192,384]{1,0:T(8,128)(2,1)}, u32[]{:S(2)}, u32[]{:S(2)}) collective-permute-start(bf16[192,384]{1,0:T(8,128)(2,1)} %get-tuple-element.271), channel_id=1, source_target_pairs={{0,8},{4,12},{8,16},{12,20},{16,24},{20,28},{24,0},{28,4},{1,9},{5... | collective-permute-start | bytes 442376 | tf_op jit(solution)/shard_map/ppermute | solution.py:814
  275.5 19.6 %collective-permute-start.56 = (bf16[8,96,384]{2,1,0:T(8,128)(2,1)}, bf16[8,96,384]{2,1,0:T(8,128)(2,1)}, u32[]{:S(2)}, u32[]{:S(2)}) collective-permute-start(bf16[8,96,384]{2,1,0:T(8,128)(2,1)} %fusion.4), channel_id=1, source_target_pairs={{0,2},{1,3},{2,0},{3,1},{4,6},{5,7},{6,4},{7,5},{8,10},{9,11},{10,... | collective-permute-start | bytes 1769480 | tf_op jit(solution)/shard_map/ppermute | solution.py:352
  296.7 13.7 %collective-permute-start.63 = (bf16[4,96,384]{2,1,0:T(8,128)(2,1)S(1)}, bf16[4,96,384]{2,1,0:T(8,128)(2,1)S(1)}, u32[]{:S(2)}, u32[]{:S(2)}) collective-permute-start(bf16[4,96,384]{2,1,0:T(8,128)(2,1)S(1)} %fusion.17), channel_id=1, source_target_pairs={{0,2},{1,3},{2,0},{3,1},{4,6},{5,7},{6,4},{7,5},{8,10},{9,11},{10,... | collective-permute-start | bytes 884744 | tf_op jit(solution)/shard_map/ppermute | solution.py:352
  298.4 13.2 %collective-permute-start.57 = (bf16[4,96,384]{2,1,0:T(8,128)(2,1)S(1)}, bf16[4,96,384]{2,1,0:T(8,128)(2,1)S(1)}, u32[]{:S(2)}, u32[]{:S(2)}) collective-permute-start(bf16[4,96,384]{2,1,0:T(8,128)(2,1)S(1)} %fusion.16), channel_id=1, source_target_pairs={{0,4},{4,0},{8,12},{12,8},{16,20},{20,16},{24,28},{28,24},{1,5},{5... | collective-permute-start | bytes 884744 | tf_op jit(solution)/shard_map/ppermute | solution.py:752
  300.1 14.3 %collective-permute-start.68 = (bf16[192,384]{1,0:T(8,128)(2,1)S(1)}, bf16[192,384]{1,0:T(8,128)(2,1)S(1)}, u32[]{:S(2)}, u32[]{:S(2)}) collective-permute-start(bf16[192,384]{1,0:T(8,128)(2,1)S(1)} %fusion.23), channel_id=1, source_target_pairs={{0,2},{1,3},{2,0},{3,1},{4,6},{5,7},{6,4},{7,5},{8,10},{9,11},{10,... | collective-permute-start | bytes 442376 | tf_op jit(solution)/shard_map/ppermute | solution.py:352
  303.3 13.5 %collective-permute-start.67 = (bf16[384,384]{1,0:T(8,128)(2,1)S(1)}, bf16[384,384]{1,0:T(8,128)(2,1)S(1)}, u32[]{:S(2)}, u32[]{:S(2)}) collective-permute-start(bf16[384,384]{1,0:T(8,128)(2,1)S(1)} %pad_maximum_fusion.3), channel_id=1, source_target_pairs={{0,1},{1,0},{2,3},{3,2},{4,5},{5,4},{6,7},{7,6},{8,9},{9,8},{10,11... | collective-permute-start | bytes 884744 | tf_op jit(solution)/shard_map/ppermute | solution.py:352
  314.5 18.9 %collective-permute-start.72 = (bf16[384,384]{1,0:T(8,128)(2,1)S(1)}, bf16[384,384]{1,0:T(8,128)(2,1)S(1)}, u32[]{:S(2)}, u32[]{:S(2)}) collective-permute-start(bf16[384,384]{1,0:T(8,128)(2,1)S(1)} %pad_maximum_fusion.4), channel_id=1, source_target_pairs={{0,1},{1,0},{2,3},{3,2},{4,5},{5,4},{6,7},{7,6},{8,9},{9,8},{10,11... | collective-permute-start | bytes 884744 | tf_op jit(solution)/shard_map/ppermute | solution.py:352
  314.6 20.2 %collective-permute-start.66 = (bf16[192,384]{1,0:T(8,128)(2,1)S(1)}, bf16[192,384]{1,0:T(8,128)(2,1)S(1)}, u32[]{:S(2)}, u32[]{:S(2)}) collective-permute-start(bf16[192,384]{1,0:T(8,128)(2,1)S(1)} %get-tuple-element.266), channel_id=1, source_target_pairs={{0,16},{4,20},{8,24},{12,28},{16,0},{20,4},{24,8},{28,12},{1,17},{... | collective-permute-start | bytes 442376 | tf_op jit(solution)/shard_map/ppermute | solution.py:814
  315.5 19.3 %collective-permute-start.64 = (bf16[192,384]{1,0:T(8,128)(2,1)S(1)}, bf16[192,384]{1,0:T(8,128)(2,1)S(1)}, u32[]{:S(2)}, u32[]{:S(2)}) collective-permute-start(bf16[192,384]{1,0:T(8,128)(2,1)S(1)} %get-tuple-element.264), channel_id=1, source_target_pairs={{0,8},{4,12},{8,16},{12,20},{16,24},{20,28},{24,0},{28,4},{1,9},{5... | collective-permute-start | bytes 442376 | tf_op jit(solution)/shard_map/ppermute | solution.py:814
  316.8 18.1 %collective-permute-start.65 = (bf16[192,384]{1,0:T(8,128)(2,1)S(1)}, bf16[192,384]{1,0:T(8,128)(2,1)S(1)}, u32[]{:S(2)}, u32[]{:S(2)}) collective-permute-start(bf16[192,384]{1,0:T(8,128)(2,1)S(1)} %get-tuple-element.265), channel_id=1, source_target_pairs={{0,24},{4,28},{8,0},{12,4},{16,8},{20,12},{24,16},{28,20},{1,25},{... | collective-permute-start | bytes 442376 | tf_op jit(solution)/shard_map/ppermute | solution.py:814
  319.5 13.9 %collective-permute-start.74 = (f32[16,768]{1,0:T(8,128)S(1)}, f32[16,768]{1,0:T(8,128)S(1)}, u32[]{:S(2)}, u32[]{:S(2)}) collective-permute-start(f32[16,768]{1,0:T(8,128)S(1)} %add.423), channel_id=1, source_target_pairs={{0,16},{4,20},{8,24},{12,28},{16,0},{20,4},{24,8},{28,12},{1,17},{... | collective-permute-start | bytes 147464 | tf_op jit(solution)/shard_map/ppermute | solution.py:1060
  (104 other events, 1142.7 us)
